TPU v7x, 128 devices: a whole 4x4x4 slice. The times are simulated.
128 devices in a mesh: dp: 8 (over y, core), vocab: 16 (over x, z).
Axes of the slice: x: 4, y: 4, z: 4, core: 2. Of those that a mesh axis runs over, the one named last changes fastest.
Arguments:
- student_hidden: bfloat16 [896, 4096], P(('dp', 'vocab')), may hold values from -9 to 9
- teacher_hidden: bfloat16 [896, 8192], P(('dp', 'vocab')), may hold values from -9 to 9
- student_head: bfloat16 [98304, 4096], P(('dp', 'vocab'))
- teacher_head: bfloat16 [98304, 8192], P(('dp', 'vocab'))
- token_weight: int32 [896], P(('dp', 'vocab')), may hold values from 0 to 4
- block_count: int32 [8], replicated, may hold values from 2 to 7, as said below
Outputs:
- kl_mean: float32 [], replicated
- hidden_grad: bfloat16 [896, 4096], P(('dp', 'vocab'))
- head_grad: bfloat16 [98304, 4096], P(('dp', 'vocab'))
Inputs may be any that keep to these rules, and one draw needn't show every extreme that they name: `block_count`: the counts sum to 24; one data shard holds 7 blocks.
All inputs are finite; a program needn't handle non-finite values.
Results may differ from a plain program's by a relative error of at most 0.005.
Values may be sent and summed in bfloat16 or wider, within the bound.
No kernel may reach another device: no remote copies, remote signals or barrier semaphores. Data moves between devices by JAX's collectives and lax.ppermute only.
A program may use at most 192 MiB of HBM per device.

v0:
```python
import jax
import jax.numpy as jnp
from jax import lax
from jax.sharding import PartitionSpec as P

BLOCK = 16
MEAN_BLOCKS = 3


def project(hidden, head):
    return lax.dot_general(
        hidden, head, (((1,), (1,)), ((), ())), preferred_element_type=jnp.float32
    )


def pick_counts(owner_shard, shard_ids, table):
    return jnp.sum(jnp.where(shard_ids[None, :] == owner_shard[:, None], table[None, :], 0), axis=1)


def local(student_hidden, teacher_hidden, student_head, teacher_head, token_weight, block_count):
    shards = block_count.shape[0]
    all_student, all_teacher, all_weight = (
        lax.all_gather(student_hidden, ("dp", "vocab"), axis=0, tiled=True),
        lax.all_gather(teacher_hidden, ("dp", "vocab"), axis=0, tiled=True),
        lax.all_gather(token_weight.astype(jnp.bfloat16), ("dp", "vocab"), axis=0, tiled=True),
    )
    total_rows = all_student.shape[0]
    shard_rows = total_rows // shards
    live_total = MEAN_BLOCKS * shards * BLOCK
    shard_ids = jnp.arange(shards, dtype=jnp.int32)
    row_ids = jnp.arange(total_rows, dtype=jnp.int32)
    owner_shard = row_ids // shard_rows
    local_row = row_ids % shard_rows
    live_row = local_row < pick_counts(owner_shard, shard_ids, block_count) * BLOCK
    row_weight = jnp.where(live_row, all_weight.astype(jnp.float32), 0.0)
    teacher_logits = project(all_teacher, teacher_head)
    student_logits = project(all_student, student_head)
    top_t = jnp.max(teacher_logits, axis=1)
    top_s = jnp.max(student_logits, axis=1)
    exp_t = jnp.exp(teacher_logits - top_t[:, None])
    sum_t = jnp.sum(exp_t, axis=1)
    cross_sum = jnp.sum(exp_t * (teacher_logits - student_logits), axis=1)
    sum_s = jnp.sum(jnp.exp(student_logits - top_s[:, None]), axis=1)
    whole_t, whole_s = lax.pmax((top_t, top_s), ("dp", "vocab"))
    factor_t = jnp.exp(top_t - whole_t)
    factor_s = jnp.exp(top_s - whole_s)
    sum_t, cross_sum, sum_s = lax.psum(
        (sum_t * factor_t, cross_sum * factor_t, sum_s * factor_s), ("dp", "vocab")
    )
    top_t = whole_t
    top_s = whole_s
    log_zt = top_t + jnp.log(sum_t)
    log_zs = top_s + jnp.log(sum_s)
    divergence = cross_sum / sum_t - log_zt + log_zs
    kl_mean = jnp.sum(row_weight * divergence) / live_total
    teacher_prob = jnp.exp(teacher_logits - log_zt[:, None])
    student_prob = jnp.exp(student_logits - log_zs[:, None])
    logit_grad = (row_weight[:, None] * (student_prob - teacher_prob)).astype(jnp.bfloat16)
    head_grad = lax.dot_general(
        logit_grad, all_student, (((0,), (0,)), ((), ())), preferred_element_type=jnp.float32
    ).astype(jnp.bfloat16)
    hidden_grad = lax.psum_scatter(
        jnp.dot(logit_grad, student_head, preferred_element_type=jnp.float32),
        ("dp", "vocab"),
        scatter_dimension=0,
        tiled=True,
    ).astype(jnp.bfloat16)
    return (kl_mean, hidden_grad, head_grad)


def solution(mesh):
    placed = (
        P(("dp", "vocab"), None),
        P(("dp", "vocab"), None),
        P(("dp", "vocab"), None),
        P(("dp", "vocab"), None),
        P(("dp", "vocab")),
        P(),
    )
    return jax.shard_map(
        local,
        mesh=mesh,
        in_specs=placed,
        out_specs=(P(), P(("dp", "vocab"), None), P(("dp", "vocab"), None)),
        check_vma=False,
    )
```

profile of v0, /device:TPU:1, one launch (start us, length us, event | category | flops | bytes accessed | tf_op | source)
XLA Modules:
  0.0 813.5 jit_solution(13259043194147103760)
XLA Ops:
  9.5 69.3 %all-reduce = bf16[896]{0:T(1024)(128)(2,1)S(1)} all-reduce(bf16[896]{0:T(1024)(128)(2,1)S(1)} %dynamic-update-slice), channel_id=1, replica_groups=mesh['dp'=8,'vocab'=16] {'dp','vocab'}, use_global_device_ids=true, to_apply=%add | all-reduce | flops 896 | bytes 3584
  79.6 5.7 all-gather.7.cloned.1.call-done
  85.3 9.5 %reshape.30 = bf16[896,4096]{1,0:T(8,128)(2,1)} reshape(bf16[128,7,4096]{2,1,0:T(8,128)(2,1)} %all-gather.7.cloned.1.call-done) | data formatting | bytes 14680064
  94.8 11.1 %fusion.12 = (f32[896]{0:T(1024)S(1)}, f32[896,768]{0,1:T(8,128)S(1)}) fusion(bf16[896,4096]{1,0:T(8,128)(2,1)} %reshape.30, bf16[768,4096]{1,0:T(8,128)(2,1)} %param.8), kind=kOutput, calls=%fused_computation.30 | convolution fusion | flops 5637831680 | bytes 16387584 | tf_op jit(solution)/shard_map/dot_general | solution.py:11
  105.9 60.3 %all-gather.5.cloned.1.call-done = bf16[128,7,8192]{2,1,0:T(8,128)(2,1)} async-done(((bf16[1,7,8192]{2,1,0:T(8,128)(2,1)}), bf16[128,7,8192]{2,1,0:T(8,128)(2,1)}) %all-gather.5.cloned.1.call-update) | async-done | bytes 14680080 | tf_op jit(solution)/shard_map/all_gather | solution.py:24
  166.2 18.6 %reshape.28 = bf16[896,8192]{1,0:T(8,128)(2,1)} reshape(bf16[128,7,8192]{2,1,0:T(8,128)(2,1)} %all-gather.5.cloned.1.call-done) | data formatting | bytes 29360128
  184.8 19.5 %fusion.11 = (f32[896]{0:T(1024)S(1)}, f32[896,768]{0,1:T(8,128)}) fusion(bf16[896,8192]{1,0:T(8,128)(2,1)} %reshape.28, bf16[768,8192]{1,0:T(8,128)(2,1)} %param.9), kind=kOutput, calls=%fused_computation.29 | convolution fusion | flops 11274976256 | bytes 30019072 | tf_op jit(solution)/shard_map/dot_general | solution.py:11
  204.3 64.5 %all-reduce.4 = (f32[896]{0:T(1024)S(1)}, f32[896]{0:T(1024)S(1)}) all-reduce(f32[896]{0:T(1024)S(1)} %get-tuple-element.34, f32[896]{0:T(1024)S(1)} %get-tuple-element.32), channel_id=1, replica_groups=mesh['dp'=8,'vocab'=16] {'dp','vocab'}, use_global_device_ids=true, to_apply=%region_8.9 | all-reduce | flops 1792 | bytes 14336 | tf_op jit(solution)/shard_map/pmax | solution.py:44
  268.8 2.8 multiply_reduce_fusion
  271.6 64.4 %all-reduce.3 = (f32[896]{0:T(1024)S(1)}, f32[896]{0:T(1024)S(1)}, f32[896]{0:T(1024)S(1)}) all-reduce(f32[896]{0:T(1024)S(1)} %get-tuple-element.36, f32[896]{0:T(1024)S(1)} %get-tuple-element.31, f32[896]{0:T(1024)S(1)} %get-tuple-element.30), channel_id=1, replica_groups=mesh['dp'=8,'vocab'=16] {'dp','vocab'}, use_global_device_ids=true, to_apply=%region_10.11 | all-reduce | flops 2688 | bytes 21504 | tf_op jit(solution)/shard_map/psum | solution.py:47
  336.6 3.4 multiply_convert_fusion
  340.0 11.0 %fusion.13 = f32[896,4096]{1,0:T(8,128)} fusion(bf16[896,768]{0,1:T(8,128)(2,1)S(1)} %multiply_convert_fusion, bf16[768,4096]{1,0:T(8,128)(2,1)} %param.8), kind=kOutput, calls=%fused_computation.31 | convolution fusion | flops 5637144576 | bytes 22347776 | tf_op jit(solution)/shard_map/dot_general | solution.py:63
  351.0 356.7 %fusion = f32[8,4096]{1,0:T(8,128)S(1)} fusion(f32[896,4096]{1,0:T(8,128)} %fusion.13), kind=kCustom, calls=%all-reduce-scatter | all-reduce-scatter fusion | flops 4194305 | bytes 14811136
  707.7 1.9 collective-permute-start.15
  709.7 1.9 collective-permute-start.14
  711.6 1.9 collective-permute-start.13
  713.5 1.9 collective-permute-start.12
  715.4 1.9 collective-permute-start.11
  717.4 23.7 %collective-permute-done.15 = bf16[7,4096]{1,0:T(8,128)(2,1)S(1)} collective-permute-done((bf16[7,4096]{1,0:T(8,128)(2,1)S(1)}, bf16[7,4096]{1,0:T(8,128)(2,1)S(1)}, u32[]{:S(2)}, u32[]{:S(2)}) %collective-permute-start.15) | collective-permute-done | bytes 57376
  741.1 1.9 collective-permute-start.10
  743.0 1.9 collective-permute-start.9
  745.0 1.9 collective-permute-start.8
  746.9 10.6 %collective-permute-start.7 = (bf16[8,4096]{1,0:T(8,128)(2,1)S(1)}, bf16[8,4096]{1,0:T(8,128)(2,1)S(1)}, u32[]{:S(2)}, u32[]{:S(2)}) collective-permute-start(bf16[8,4096]{1,0:T(8,128)(2,1)S(1)} %convert.30), channel_id=1, source_target_pairs={{0,8},{1,9},{2,10},{3,11},{4,12},{5,13},{6,14},{7,15},{8,16},{9,17... | collective-permute-start | bytes 196616
  757.5 1.9 collective-permute-start.6
  759.5 13.1 %collective-permute-start.5 = (bf16[8,4096]{1,0:T(8,128)(2,1)S(1)}, bf16[8,4096]{1,0:T(8,128)(2,1)S(1)}, u32[]{:S(2)}, u32[]{:S(2)}) collective-permute-start(bf16[8,4096]{1,0:T(8,128)(2,1)S(1)} %convert.30), channel_id=1, source_target_pairs={{0,6},{1,7},{2,8},{3,9},{4,10},{5,11},{6,12},{7,13},{8,14},{9,15},... | collective-permute-start | bytes 196616
  772.6 4.0 collective-permute-start.4
  776.6 3.4 collective-permute-start.3
  780.0 4.9 collective-permute-start.2
  785.0 1.9 collective-permute-start.1
  786.9 2.5 collective-permute-start
  789.4 11.6 %convolution_convert_fusion = bf16[768,4096]{1,0:T(8,128)(2,1)} fusion(bf16[896,768]{0,1:T(8,128)(2,1)S(1)} %multiply_convert_fusion, bf16[896,4096]{1,0:T(8,128)(2,1)} %reshape.30), kind=kOutput, calls=%fused_computation | convolution fusion | flops 5640290304 | bytes 15007744 | tf_op jit(solution)/shard_map/dot_general | solution.py:59
  801.7 3.1 concatenate
  (31 shorter events, 4.4 us)
Async XLA Ops:
  7.2 78.1 %all-gather.7.cloned.1.call-start = ((), (), s32[]{:S(2)}) async-start(), calls=%async_computation.1 | async-start | bytes 8454144 | tf_op jit(solution)/shard_map/all_gather | solution.py:23
  7.9 158.3 %all-gather.5.cloned.1.call-start = ((), (), s32[]{:S(2)}) async-start(), calls=%async_computation | async-start | bytes 16908288 | tf_op jit(solution)/shard_map/all_gather | solution.py:24
  105.9 162.9 %copy-start = (f32[896,768]{0,1:T(8,128)}, f32[896,768]{0,1:T(8,128)S(1)}, u32[]{:S(2)}) copy-start(f32[896,768]{0,1:T(8,128)S(1)} %get-tuple-element.35) | copy-start | bytes 8257540
  707.7 33.4 %collective-permute-start.15 = (bf16[7,4096]{1,0:T(8,128)(2,1)S(1)}, bf16[7,4096]{1,0:T(8,128)(2,1)S(1)}, u32[]{:S(2)}, u32[]{:S(2)}) collective-permute-start(bf16[7,4096]{1,0:T(8,128)(2,1)S(1)} %slice), channel_id=1, source_target_pairs={{0,16},{1,17},{2,18},{3,19},{4,20},{5,21},{6,22},{7,23},{8,24},{9,... | collective-permute-start | bytes 172040
  709.7 33.4 %collective-permute-start.14 = (bf16[8,4096]{1,0:T(8,128)(2,1)S(1)}, bf16[8,4096]{1,0:T(8,128)(2,1)S(1)}, u32[]{:S(2)}, u32[]{:S(2)}) collective-permute-start(bf16[8,4096]{1,0:T(8,128)(2,1)S(1)} %convert.30), channel_id=1, source_target_pairs={{0,15},{1,16},{2,17},{3,18},{4,19},{5,20},{6,21},{7,22},{8,23},{9,... | collective-permute-start | bytes 196616
  711.6 33.4 %collective-permute-start.13 = (bf16[8,4096]{1,0:T(8,128)(2,1)S(1)}, bf16[8,4096]{1,0:T(8,128)(2,1)S(1)}, u32[]{:S(2)}, u32[]{:S(2)}) collective-permute-start(bf16[8,4096]{1,0:T(8,128)(2,1)S(1)} %convert.30), channel_id=1, source_target_pairs={{0,14},{1,15},{2,16},{3,17},{4,18},{5,19},{6,20},{7,21},{8,22},{9,... | collective-permute-start | bytes 196616
  713.5 33.4 %collective-permute-start.12 = (bf16[8,4096]{1,0:T(8,128)(2,1)S(1)}, bf16[8,4096]{1,0:T(8,128)(2,1)S(1)}, u32[]{:S(2)}, u32[]{:S(2)}) collective-permute-start(bf16[8,4096]{1,0:T(8,128)(2,1)S(1)} %convert.30), channel_id=1, source_target_pairs={{0,13},{1,14},{2,15},{3,16},{4,17},{5,18},{6,19},{7,20},{8,21},{9,... | collective-permute-start | bytes 196616
  715.4 42.1 %collective-permute-start.11 = (bf16[8,4096]{1,0:T(8,128)(2,1)S(1)}, bf16[8,4096]{1,0:T(8,128)(2,1)S(1)}, u32[]{:S(2)}, u32[]{:S(2)}) collective-permute-start(bf16[8,4096]{1,0:T(8,128)(2,1)S(1)} %convert.30), channel_id=1, source_target_pairs={{0,12},{1,13},{2,14},{3,15},{4,16},{5,17},{6,18},{7,19},{8,20},{9,... | collective-permute-start | bytes 196616
  741.1 18.4 %collective-permute-start.10 = (bf16[8,4096]{1,0:T(8,128)(2,1)S(1)}, bf16[8,4096]{1,0:T(8,128)(2,1)S(1)}, u32[]{:S(2)}, u32[]{:S(2)}) collective-permute-start(bf16[8,4096]{1,0:T(8,128)(2,1)S(1)} %convert.30), channel_id=1, source_target_pairs={{0,11},{1,12},{2,13},{3,14},{4,15},{5,16},{6,17},{7,18},{8,19},{9,... | collective-permute-start | bytes 196616
  743.0 29.5 %collective-permute-start.9 = (bf16[8,4096]{1,0:T(8,128)(2,1)S(1)}, bf16[8,4096]{1,0:T(8,128)(2,1)S(1)}, u32[]{:S(2)}, u32[]{:S(2)}) collective-permute-start(bf16[8,4096]{1,0:T(8,128)(2,1)S(1)} %convert.30), channel_id=1, source_target_pairs={{0,10},{1,11},{2,12},{3,13},{4,14},{5,15},{6,16},{7,17},{8,18},{9,... | collective-permute-start | bytes 196616
  745.0 31.6 %collective-permute-start.8 = (bf16[8,4096]{1,0:T(8,128)(2,1)S(1)}, bf16[8,4096]{1,0:T(8,128)(2,1)S(1)}, u32[]{:S(2)}, u32[]{:S(2)}) collective-permute-start(bf16[8,4096]{1,0:T(8,128)(2,1)S(1)} %convert.30), channel_id=1, source_target_pairs={{0,9},{1,10},{2,11},{3,12},{4,13},{5,14},{6,15},{7,16},{8,17},{9,1... | collective-permute-start | bytes 196616
  746.9 33.1 %collective-permute-start.7 = (bf16[8,4096]{1,0:T(8,128)(2,1)S(1)}, bf16[8,4096]{1,0:T(8,128)(2,1)S(1)}, u32[]{:S(2)}, u32[]{:S(2)}) collective-permute-start(bf16[8,4096]{1,0:T(8,128)(2,1)S(1)} %convert.30), channel_id=1, source_target_pairs={{0,8},{1,9},{2,10},{3,11},{4,12},{5,13},{6,14},{7,15},{8,16},{9,17... | collective-permute-start | bytes 196616
  757.5 27.4 %collective-permute-start.6 = (bf16[8,4096]{1,0:T(8,128)(2,1)S(1)}, bf16[8,4096]{1,0:T(8,128)(2,1)S(1)}, u32[]{:S(2)}, u32[]{:S(2)}) collective-permute-start(bf16[8,4096]{1,0:T(8,128)(2,1)S(1)} %convert.30), channel_id=1, source_target_pairs={{0,7},{1,8},{2,9},{3,10},{4,11},{5,12},{6,13},{7,14},{8,15},{9,16}... | collective-permute-start | bytes 196616
  759.5 27.4 %collective-permute-start.5 = (bf16[8,4096]{1,0:T(8,128)(2,1)S(1)}, bf16[8,4096]{1,0:T(8,128)(2,1)S(1)}, u32[]{:S(2)}, u32[]{:S(2)}) collective-permute-start(bf16[8,4096]{1,0:T(8,128)(2,1)S(1)} %convert.30), channel_id=1, source_target_pairs={{0,6},{1,7},{2,8},{3,9},{4,10},{5,11},{6,12},{7,13},{8,14},{9,15},... | collective-permute-start | bytes 196616
  772.6 29.1 %collective-permute-start.4 = (bf16[8,4096]{1,0:T(8,128)(2,1)S(1)}, bf16[8,4096]{1,0:T(8,128)(2,1)S(1)}, u32[]{:S(2)}, u32[]{:S(2)}) collective-permute-start(bf16[8,4096]{1,0:T(8,128)(2,1)S(1)} %convert.30), channel_id=1, source_target_pairs={{0,5},{1,6},{2,7},{3,8},{4,9},{5,10},{6,11},{7,12},{8,13},{9,14},{... | collective-permute-start | bytes 196616
  776.6 25.1 %collective-permute-start.3 = (bf16[8,4096]{1,0:T(8,128)(2,1)S(1)}, bf16[8,4096]{1,0:T(8,128)(2,1)S(1)}, u32[]{:S(2)}, u32[]{:S(2)}) collective-permute-start(bf16[8,4096]{1,0:T(8,128)(2,1)S(1)} %convert.30), channel_id=1, source_target_pairs={{0,4},{1,5},{2,6},{3,7},{4,8},{5,9},{6,10},{7,11},{8,12},{9,13},{1... | collective-permute-start | bytes 196616
  780.0 21.6 %collective-permute-start.2 = (bf16[8,4096]{1,0:T(8,128)(2,1)S(1)}, bf16[8,4096]{1,0:T(8,128)(2,1)S(1)}, u32[]{:S(2)}, u32[]{:S(2)}) collective-permute-start(bf16[8,4096]{1,0:T(8,128)(2,1)S(1)} %convert.30), channel_id=1, source_target_pairs={{0,3},{1,4},{2,5},{3,6},{4,7},{5,8},{6,9},{7,10},{8,11},{9,12},{10... | collective-permute-start | bytes 196616
  785.0 16.7 %collective-permute-start.1 = (bf16[8,4096]{1,0:T(8,128)(2,1)S(1)}, bf16[8,4096]{1,0:T(8,128)(2,1)S(1)}, u32[]{:S(2)}, u32[]{:S(2)}) collective-permute-start(bf16[8,4096]{1,0:T(8,128)(2,1)S(1)} %convert.30), channel_id=1, source_target_pairs={{0,2},{1,3},{2,4},{3,5},{4,6},{5,7},{6,8},{7,9},{8,10},{9,11},{10,... | collective-permute-start | bytes 196616
  786.9 14.8 %collective-permute-start = (bf16[8,4096]{1,0:T(8,128)(2,1)S(1)}, bf16[8,4096]{1,0:T(8,128)(2,1)S(1)}, u32[]{:S(2)}, u32[]{:S(2)}) collective-permute-start(bf16[8,4096]{1,0:T(8,128)(2,1)S(1)} %convert.30), channel_id=1, source_target_pairs={{0,1},{1,2},{2,3},{3,4},{4,5},{5,6},{6,7},{7,8},{8,9},{9,10},{10,1... | collective-permute-start | bytes 196616
Sparse Core Ops, SparseCore 0:
  11.1 74.1 all-gather.6
  88.5 77.6 all-gather.4
where the time goes:
time: 817 us; the launch traced here: 813 us
  blocking collectives  555 us (68%)
  waiting for transfers between devices  91.1 us (11%)
  starting transfers between devices  57.8 us (7%)
  matrix products  53.2 us (7%)
  local copies, waits for them, and re-layouts  32.1 us (4%)
  between operations  16.1 us (2%)
  other arithmetic  8.21 us (1%)
    unnamed x2, blocking collectives  426 us
    pmax x1, blocking collectives, local(): whole_t, whole_s = lax.pmax((top_t, top_s), ('dp', 'vocab'))  64.5 us
    psum x1, blocking collectives, local(): lax.psum((sum_t * factor_t, cross_sum * factor_t, sum_s * factor_s), ('dp...  64.4 us
    all_gather x1, waiting for transfers between devices, local(): lax.all_gather(teacher_hidden, ('dp', 'vocab'), axis=0, tiled=True)  60.3 us
    unnamed x16, starting transfers between devices  57.7 us
    unnamed x8, local copies, waits for them, and re-layouts  31.4 us
    dot_general x2, matrix products, project(): lax.dot_general(hidden, head, (((1,), (1,)), ((), ())), preferred_element...  30.6 us
    unnamed x18, waiting for transfers between devices  25.1 us
  transfers between devices with their start and end apart: 18, of which 3 were waited for; matrix products, arithmetic and copies ran while one was open for 4% of the time, Pallas kernels for 0%

commit v1 on v0

v1 whole, which is shorter than its diff:
```python
import jax
import jax.numpy as jnp
from jax import lax
from jax.experimental import pallas as pl
from jax.experimental.pallas import tpu as pltpu
from jax.sharding import PartitionSpec as P

BLOCK = 16
LIVE = 384
OWN = 7
VOC = 768
DT = 8192
DS = 4096
AXES = ("dp", "vocab")
F32 = jnp.float32
BF16 = jnp.bfloat16
NT = (((1,), (1,)), ((), ()))
NN = (((1,), (0,)), ((), ()))


def flat(y, c, x, z):
    return ((y * 2 + c) * 4 + x) * 4 + z


def perm_of(move):
    return [
        (flat(y, c, x, z), flat(*move(y, c, x, z)))
        for y in range(4)
        for c in range(2)
        for x in range(4)
        for z in range(4)
    ]


def minor(shift):
    return perm_of(
        lambda y, c, x, z: (y, c, (x + shift) % 4, z) if c == 0 else ((y + shift) % 4, c, x, z)
    )


def major(shift):
    return perm_of(
        lambda y, c, x, z: ((y + shift) % 4, c, x, z) if c == 0 else (y, c, (x + shift) % 4, z)
    )


SWAP = perm_of(lambda y, c, x, z: (y, 1 - c, x, z))


def permute(value, pairs):
    return lax.ppermute(value, AXES, pairs)


def unit_table(y, x, core, sign):
    k = jnp.arange(4, dtype=jnp.int32)[:, None]
    l = jnp.arange(4, dtype=jnp.int32)[None, :]
    step_y = jnp.where(core == 0, k, l)
    step_x = jnp.where(core == 0, l, k)
    yy = (y + sign * step_y + 4) % 4
    xx = (x + sign * step_x + 4) % 4
    return (yy * 2 + core) * 4 + xx


def params(limit_mib):
    return pltpu.CompilerParams(
        dimension_semantics=("arbitrary",), vmem_limit_bytes=limit_mib * 1024 * 1024
    )


def logits_call(table, stacks, teacher_head, student_head, prior, last):
    n = len(stacks)
    steps = 4 * n

    def kernel(table_ref, *refs):
        stack_refs = refs[:n]
        ht_ref, hs_ref = refs[n], refs[n + 1]
        pos = n + 2
        if prior is not None:
            pt_ref, ps_ref = refs[pos], refs[pos + 1]
            pos += 2
        t_ref, s_ref = refs[pos], refs[pos + 1]
        pos += 2
        if last:
            stat_ref = refs[pos]
            pos += 1
        rows_ref = refs[pos]
        i = pl.program_id(0)
        for k in range(n):
            @pl.when(i // 4 == k)
            def _(k=k):
                rows_ref[...] = stack_refs[k][0]

        add_t = lax.dot_general(ht_ref[...], rows_ref[:, :256], NT, preferred_element_type=F32)
        add_s = lax.dot_general(hs_ref[...], rows_ref[:, 256:], NT, preferred_element_type=F32)

        @pl.when(i == 0)
        def _():
            if prior is None:
                t_ref[...] = add_t
                s_ref[...] = add_s
            else:
                t_ref[...] = pt_ref[...] + add_t
                s_ref[...] = ps_ref[...] + add_s

        @pl.when(i > 0)
        def _():
            t_ref[...] += add_t
            s_ref[...] += add_s

        if last:
            @pl.when(i == steps - 1)
            def _():
                t = t_ref[...]
                s = s_ref[...]
                top_t = jnp.max(t, axis=0, keepdims=True)
                top_s = jnp.max(s, axis=0, keepdims=True)
                exp_t = jnp.exp(t - top_t)
                sum_t = jnp.sum(exp_t, axis=0, keepdims=True)
                cross = jnp.sum(exp_t * (t - s), axis=0, keepdims=True)
                sum_s = jnp.sum(jnp.exp(s - top_s), axis=0, keepdims=True)
                lse_t = top_t + jnp.log(sum_t)
                lse_s = top_s + jnp.log(sum_s)
                mean = cross / sum_t
                for j in range(3):
                    cols = slice(128 * j, 128 * (j + 1))
                    stat_ref[j : j + 1, :] = lse_t[:, cols]
                    stat_ref[3 + j : 4 + j, :] = lse_s[:, cols]
                    stat_ref[8 + j : 9 + j, :] = mean[:, cols]

    whole = pl.BlockSpec((VOC, LIVE), lambda i, tab: (0, 0))
    in_specs = [
        pl.BlockSpec((1, LIVE, LIVE), lambda i, tab, k=k: (jnp.clip(i - 4 * k, 0, 3), 0, 0))
        for k in range(n)
    ] + [
        pl.BlockSpec((VOC, 256), lambda i, tab: (0, tab[i])),
        pl.BlockSpec((VOC, 128), lambda i, tab: (0, tab[i])),
    ]
    args = [*stacks, teacher_head, student_head]
    if prior is not None:
        in_specs += [whole, whole]
        args += list(prior)
    out_specs = [whole, whole]
    out_shape = [jax.ShapeDtypeStruct((VOC, LIVE), F32)] * 2
    if last:
        out_specs.append(pl.BlockSpec((16, 128), lambda i, tab: (0, 0)))
        out_shape.append(jax.ShapeDtypeStruct((16, 128), F32))
    return pl.pallas_call(
        kernel,
        grid_spec=pltpu.PrefetchScalarGridSpec(
            num_scalar_prefetch=1,
            grid=(steps,),
            in_specs=in_specs,
            out_specs=out_specs,
            scratch_shapes=[pltpu.VMEM((LIVE, LIVE), BF16)],
        ),
        out_shape=out_shape,
        compiler_params=params(40),
        cost_estimate=pl.CostEstimate(
            flops=2 * steps * LIVE * LIVE * VOC,
            bytes_accessed=steps * (LIVE + VOC) * LIVE * 2,
            transcendentals=0,
        ),
    )(table, *args)


def logit_grad_call(table, logits_t, logits_s, stat, all_stats, weight, student_head):
    def kernel(tab, t_ref, s_ref, stat_ref, all_ref, w_ref, h0_ref, h1_ref, out_ref, gt_ref, g_ref, kl_ref):
        i = pl.program_id(0)

        @pl.when(i == 0)
        def _():
            every = all_ref[...]
            top = jnp.max(every, axis=0)
            total = top + jnp.log(jnp.sum(jnp.exp(every - top[None]), axis=0))
            log_zt = jnp.concatenate([total[j : j + 1] for j in range(3)], axis=1)
            log_zs = jnp.concatenate([total[3 + j : 4 + j] for j in range(3)], axis=1)
            own_t = jnp.concatenate([stat_ref[j : j + 1, :] for j in range(3)], axis=1)
            mean = jnp.concatenate([stat_ref[8 + j : 9 + j, :] for j in range(3)], axis=1)
            w = w_ref[...]
            grad = (w * (jnp.exp(s_ref[...] - log_zs) - jnp.exp(t_ref[...] - log_zt))).astype(BF16)
            gt_ref[...] = grad
            g_ref[...] = grad.T
            share = jnp.sum(w * mean * jnp.exp(own_t - log_zt), axis=1, keepdims=True)
            common = jnp.sum(w * (log_zs - log_zt), axis=1, keepdims=True)
            kl_ref[0:1, :] = jnp.broadcast_to(share, (1, 128))
            kl_ref[1:2, :] = jnp.broadcast_to(common, (1, 128))

        pair = jnp.concatenate([h0_ref[...], h1_ref[...]], axis=1)
        part = jnp.dot(g_ref[...], pair, preferred_element_type=F32).astype(BF16)
        out_ref[0] = part[:, :128]
        out_ref[1] = part[:, 128:]

    const = lambda *shape: pl.BlockSpec(shape, lambda i, tab: (0,) * len(shape))
    return pl.pallas_call(
        kernel,
        grid_spec=pltpu.PrefetchScalarGridSpec(
            num_scalar_prefetch=1,
            grid=(8,),
            in_specs=[
                const(VOC, LIVE),
                const(VOC, LIVE),
                const(16, 128),
                const(128, 8, 128),
                const(1, LIVE),
                pl.BlockSpec((VOC, 128), lambda i, tab: (0, tab[2 * i])),
                pl.BlockSpec((VOC, 128), lambda i, tab: (0, tab[2 * i + 1])),
            ],
            out_specs=[
                pl.BlockSpec((2, LIVE, 128), lambda i, tab: (i, 0, 0)),
                const(VOC, LIVE),
                const(LIVE, VOC),
                const(8, 128),
            ],
        ),
        out_shape=[
            jax.ShapeDtypeStruct((16, LIVE, 128), BF16),
            jax.ShapeDtypeStruct((VOC, LIVE), BF16),
            jax.ShapeDtypeStruct((LIVE, VOC), BF16),
            jax.ShapeDtypeStruct((8, 128), F32),
        ],
        compiler_params=params(32),
        cost_estimate=pl.CostEstimate(
            flops=2 * LIVE * VOC * 2048, bytes_accessed=8 * 1024 * 1024, transcendentals=VOC * LIVE * 2
        ),
    )(table, logits_t, logits_s, stat, all_stats, weight, student_head, student_head)


def hidden_half_call(table, grad, student_head):
    def kernel(tab, g_ref, h0_ref, h1_ref, out_ref):
        pair = jnp.concatenate([h0_ref[...], h1_ref[...]], axis=1)
        part = jnp.dot(g_ref[...], pair, preferred_element_type=F32)
        out_ref[0] = part[:, :128]
        out_ref[1] = part[:, 128:]

    return pl.pallas_call(
        kernel,
        grid_spec=pltpu.PrefetchScalarGridSpec(
            num_scalar_prefetch=1,
            grid=(8,),
            in_specs=[
                pl.BlockSpec((LIVE, VOC), lambda i, tab: (0, 0)),
                pl.BlockSpec((VOC, 128), lambda i, tab: (0, tab[2 * i])),
                pl.BlockSpec((VOC, 128), lambda i, tab: (0, tab[2 * i + 1])),
            ],
            out_specs=pl.BlockSpec((2, LIVE, 128), lambda i, tab: (i, 0, 0)),
        ),
        out_shape=jax.ShapeDtypeStruct((16, LIVE, 128), F32),
        compiler_params=params(32),
        cost_estimate=pl.CostEstimate(
            flops=2 * LIVE * VOC * 2048, bytes_accessed=7 * 1024 * 1024, transcendentals=0
        ),
    )(table, grad, student_head, student_head)


def head_grad_call(table, stacks, grad_t):
    n = len(stacks)

    def kernel(tab, *refs):
        g_ref, out_ref, rows_ref = refs[n], refs[n + 1], refs[n + 2]
        i = pl.program_id(0)
        for k in range(n):
            @pl.when(i // 4 == k)
            def _(k=k):
                rows_ref[...] = refs[k][0]

        out_ref[...] = jnp.dot(g_ref[...], rows_ref[...], preferred_element_type=F32).astype(BF16)

    return pl.pallas_call(
        kernel,
        grid_spec=pltpu.PrefetchScalarGridSpec(
            num_scalar_prefetch=1,
            grid=(4 * n,),
            in_specs=[
                pl.BlockSpec((1, LIVE, 128), lambda i, tab, k=k: (jnp.clip(i - 4 * k, 0, 3), 0, 2))
                for k in range(n)
            ]
            + [pl.BlockSpec((VOC, LIVE), lambda i, tab: (0, 0))],
            out_specs=pl.BlockSpec((VOC, 128), lambda i, tab: (0, tab[i])),
            scratch_shapes=[pltpu.VMEM((LIVE, 128), BF16)],
        ),
        out_shape=jax.ShapeDtypeStruct((VOC, DS), BF16),
        compiler_params=params(32),
        cost_estimate=pl.CostEstimate(
            flops=4 * LIVE * VOC * DS, bytes_accessed=10 * 1024 * 1024, transcendentals=0
        ),
    )(table, *stacks, grad_t)


def local(student_hidden, teacher_hidden, student_head, teacher_head, token_weight, block_count):
    me = lax.axis_index("dp") * 16 + lax.axis_index("vocab")
    y, core, x = me // 32, (me // 16) % 2, (me // 4) % 4

    units = jnp.concatenate(
        [teacher_hidden.reshape(OWN, 32, 256), student_hidden.reshape(OWN, 32, 128)], axis=2
    ).transpose(1, 0, 2)
    weights = jnp.pad(token_weight.astype(BF16), (0, LIVE - OWN))
    units = jnp.concatenate([units, jnp.broadcast_to(weights, (32, 1, LIVE))], axis=1)
    units = jnp.broadcast_to(units[:, None], (32, 4, 8, LIVE)).reshape(128, 8, LIVE)
    arrived = lax.all_to_all(units, AXES, split_axis=0, concat_axis=0, tiled=True)

    ends = jnp.cumsum(block_count)
    block = jnp.arange(LIVE, dtype=jnp.int32) // BLOCK
    shard = jnp.sum((block[:, None] >= ends[None, :]).astype(jnp.int32), axis=1)
    begin = jnp.sum(jnp.where(jnp.arange(8)[None, :] < shard[:, None], block_count[None, :], 0), axis=1)
    place = (block - begin) * BLOCK + jnp.arange(LIVE, dtype=jnp.int32) % BLOCK
    slot = (shard * 16 + place // OWN) * 8 + place % OWN
    slots = jnp.arange(1024, dtype=jnp.int32)
    pick = (slot[:, None] == slots[None, :]).astype(BF16)
    own = jnp.dot(pick, arrived.reshape(1024, LIVE), preferred_element_type=F32).astype(BF16)
    weight = lax.dot_general(arrived[:, 7, :8].reshape(1, 1024), pick, NT, preferred_element_type=F32)

    stack = jnp.stack([own] + [permute(own, minor(l)) for l in (1, 2, 3)])
    stacks = [stack] + [permute(stack, major(k)) for k in (1, 2, 3)]
    others = [permute(s, SWAP) for s in stacks]
    tab_own = unit_table(y, x, core, -1)
    tab_sib = unit_table(y, x, 1 - core, -1)

    def logits(ks, prior, last):
        table = jnp.concatenate([t[k] for k in ks for t in (tab_own, tab_sib)])
        held = [s[k] for k in ks for s in (stacks, others)]
        return logits_call(table, held, teacher_head, student_head, prior, last)

    logits_t, logits_s = logits((0,), None, False)
    logits_t, logits_s, stat = logits((1, 3, 2), (logits_t, logits_s), True)

    sent = jnp.broadcast_to(stat[None, :8], (128, 8, 128))
    all_stats = lax.all_to_all(sent, AXES, split_axis=0, concat_axis=0, tiled=True)

    dest_own = unit_table(y, x, core, 1).reshape(16)
    dest_sib = unit_table(y, x, 1 - core, 1).reshape(16)
    half, grad_t, grad, kl = logit_grad_call(
        dest_sib, logits_t, logits_s, stat, all_stats, weight, student_head
    )
    half = permute(half, SWAP)
    mine = hidden_half_call(dest_own, grad, student_head)
    head_grad = head_grad_call(
        jnp.concatenate([tab_own.reshape(16), tab_sib.reshape(16)]), [*stacks, *others], grad_t
    )

    total = (mine + half.astype(F32)).reshape(4, 4, LIVE, 128)
    out = total.astype(BF16)
    total = total[0] + sum(permute(out[k], major(k)).astype(F32) for k in (1, 2, 3))
    total = total[0] + sum(permute(total[l], minor(l)) for l in (1, 2, 3))

    share = kl[0, 0]
    hi = share.astype(BF16)
    mid = (share - hi.astype(F32)).astype(BF16)
    low = (share - hi.astype(F32) - mid.astype(F32)).astype(BF16)
    lane = jnp.arange(128)
    extra = jnp.where(lane == 0, hi, jnp.where(lane == 1, mid, jnp.where(lane == 2, low, jnp.zeros((), BF16))))
    back = lax.dot_general(
        pick, total.astype(BF16), (((0,), (0,)), ((), ())), preferred_element_type=F32
    ).astype(BF16)
    back = jnp.where((slots % 8 == 7)[:, None], extra[None, :], back).reshape(128, 8, 128)
    back = lax.all_to_all(back, AXES, split_axis=0, concat_axis=0, tiled=True).astype(F32)
    hidden_grad = jnp.sum(back.reshape(32, 4, 8, 128), axis=1)
    hidden_grad = hidden_grad.transpose(1, 0, 2).reshape(8, DS)[:OWN].astype(BF16)
    kl_mean = (jnp.sum(back[:, 7, :3]) + kl[1, 0]) / LIVE
    return kl_mean, hidden_grad, head_grad


def solution(mesh):
    rows = P(AXES, None)
    return jax.shard_map(
        local,
        mesh=mesh,
        in_specs=(rows, rows, rows, rows, P(AXES), P()),
        out_specs=(P(), rows, rows),
        check_vma=False,
    )
```

time: 817 us -> 221 us (0.27)
  blocking collectives: 555 us -> 0 us
  Pallas kernels: 0 us -> 68.1 us
  matrix products: 53.2 us -> 3.74 us
  starting transfers between devices: 57.8 us -> 40.5 us
  waiting for transfers between devices: 91.1 us -> 76.5 us
  between operations: 16.1 us -> 4.74 us
  local copies, waits for them, and re-layouts: 32.1 us -> 20.8 us
    unnamed x2 -> x0, blocking collectives: 426 us -> none
    pallas_call x0 -> x5, Pallas kernels: none -> 68.1 us  [the longest x2 35.2 us: logits_call(): pl.pallas_call(kernel, grid_spec=pltpu.PrefetchScalarGridSpec(num_scalar_...]
    all_gather x2 -> x0, waiting for transfers between devices: 66 us -> none  [the longest x1 60.3 us: local(): lax.all_gather(teacher_hidden, ('dp', 'vocab'), axis=0, tiled=True)]
    pmax x1 -> x0, blocking collectives: 64.5 us -> none  [local(): whole_t, whole_s = lax.pmax((top_t, top_s), ('dp', 'vocab'))]
    psum x1 -> x0, blocking collectives: 64.4 us -> none  [local(): lax.psum((sum_t * factor_t, cross_sum * factor_t, sum_s * factor_s), ('dp...]
    unnamed x16 -> x0, starting transfers between devices: 57.7 us -> none
    dot_general x4 -> x3, matrix products: 53.2 us -> 3.74 us  [the longest x1 2.7 us: local(): lax.dot_general(pick, total.astype(BF16), (((0,), (0,)), ((), ())), prefe...]
    ppermute x0 -> x17, waiting for transfers between devices: none -> 49.2 us  [permute(): return lax.ppermute(value, AXES, pairs)]
  transfers between devices with their start and end apart: 18 -> 20, of which waited for: 3 -> 11; matrix products, arithmetic and copies ran while one was open for 4% -> 2% of each run, Pallas kernels for 0% -> 16%
where the time goes in v1:
time: 221 us; the launch traced here: 219 us
  waiting for transfers between devices  76.5 us (35%)
  Pallas kernels  68.1 us (31%)
  starting transfers between devices  40.5 us (18%)
  local copies, waits for them, and re-layouts  20.8 us (9%)
  between operations  4.74 us (2%)
  other arithmetic  4.57 us (2%)
  matrix products  3.74 us (2%)
    ppermute x17, waiting for transfers between devices, permute(): return lax.ppermute(value, AXES, pairs)  49.2 us
    pallas_call x2, Pallas kernels, logits_call(): pl.pallas_call(kernel, grid_spec=pltpu.PrefetchScalarGridSpec(num_scalar_...  35.2 us
    pallas_call x1, Pallas kernels, head_grad_call(): pl.pallas_call(kernel, grid_spec=pltpu.PrefetchScalarGridSpec(num_scalar_...  22.5 us
    ppermute x17, starting transfers between devices, permute(): return lax.ppermute(value, AXES, pairs)  16.4 us
    unnamed x26, local copies, waits for them, and re-layouts  15.7 us
    all_to_all x1, waiting for transfers between devices, local(): lax.all_to_all(units, AXES, split_axis=0, concat_axis=0, tiled=True)  15.6 us
    all_to_all x1, waiting for transfers between devices, local(): lax.all_to_all(sent, AXES, split_axis=0, concat_axis=0, tiled=True)  11.7 us
    all_to_all x1, starting transfers between devices, local(): lax.all_to_all(units, AXES, split_axis=0, concat_axis=0, tiled=True)  11.5 us
  transfers between devices with their start and end apart: 20, of which 11 were waited for; matrix products, arithmetic and copies ran while one was open for 2% of the time, Pallas kernels for 16%

profile of v1, /device:TPU:1, one launch (start us, length us, event | category | flops | bytes accessed | tf_op | source)
XLA Modules:
  0.0 219.0 jit_solution(10983141566773513764)
XLA Ops:
  4.2 11.5 %all-to-all-start = ((bf16[128,8,384]{2,1,0:T(8,128)(2,1)}), bf16[128,8,384]{2,1,0:T(8,128)(2,1)S(1)}, u32[]{:S(2)}, u32[]{:S(2)}) async-start(bf16[128,8,384]{2,1,0:T(8,128)(2,1)} %bitcast.9), calls=%async_computation | async-start | bytes 1572864 | tf_op jit(solution)/shard_map/all_to_all | solution.py:299
  16.1 15.6 %all-to-all-done = bf16[128,8,384]{2,1,0:T(8,128)(2,1)S(1)} async-done(((bf16[128,8,384]{2,1,0:T(8,128)(2,1)}), bf16[128,8,384]{2,1,0:T(8,128)(2,1)S(1)}, u32[]{:S(2)}, u32[]{:S(2)}) %all-to-all-start) | async-done | bytes 786464 | tf_op jit(solution)/shard_map/all_to_all | solution.py:299
  33.2 1.3 collective-permute-start.1
  34.5 3.7 %collective-permute-done.2 = bf16[384,384]{1,0:T(8,128)(2,1)S(1)} collective-permute-done((bf16[384,384]{1,0:T(8,128)(2,1)S(1)}, bf16[384,384]{1,0:T(8,128)(2,1)S(1)}, u32[]{:S(2)}, u32[]{:S(2)}) %collective-permute-start.2) | collective-permute-done | bytes 294944 | tf_op jit(solution)/shard_map/ppermute | solution.py:51
  38.2 2.4 %collective-permute-done.1 = bf16[384,384]{1,0:T(8,128)(2,1)S(1)} collective-permute-done((bf16[384,384]{1,0:T(8,128)(2,1)S(1)}, bf16[384,384]{1,0:T(8,128)(2,1)S(1)}, u32[]{:S(2)}, u32[]{:S(2)}) %collective-permute-start.1) | collective-permute-done | bytes 294944 | tf_op jit(solution)/shard_map/ppermute | solution.py:51
  40.6 3.1 %collective-permute-done = bf16[384,384]{1,0:T(8,128)(2,1)S(1)} collective-permute-done((bf16[384,384]{1,0:T(8,128)(2,1)S(1)}, bf16[384,384]{1,0:T(8,128)(2,1)S(1)}, u32[]{:S(2)}, u32[]{:S(2)}) %collective-permute-start) | collective-permute-done | bytes 294944 | tf_op jit(solution)/shard_map/ppermute | solution.py:51
  44.0 2.7 %collective-permute-start.5 = (bf16[4,384,384]{2,1,0:T(8,128)(2,1)S(1)}, bf16[4,384,384]{2,1,0:T(8,128)(2,1)}, u32[]{:S(2)}, u32[]{:S(2)}) collective-permute-start(bf16[4,384,384]{2,1,0:T(8,128)(2,1)S(1)} %pad_maximum_fusion.refs_0_), channel_id=1, source_target_pairs={{0,96},{1,97},{2,98},{3,99},{4,100},{5,101},{6,102},{7,103},{8,104... | collective-permute-start | bytes 3538952 | tf_op jit(solution)/shard_map/ppermute | solution.py:51
  46.8 2.3 %collective-permute-start.9 = (bf16[4,384,384]{2,1,0:T(8,128)(2,1)S(1)}, bf16[4,384,384]{2,1,0:T(8,128)(2,1)S(1)}, u32[]{:S(2)}, u32[]{:S(2)}) collective-permute-start(bf16[4,384,384]{2,1,0:T(8,128)(2,1)S(1)} %pad_maximum_fusion.refs_0_), channel_id=1, source_target_pairs={{0,16},{1,17},{2,18},{3,19},{4,20},{5,21},{6,22},{7,23},{8,24},{9,... | collective-permute-start | bytes 3538952 | tf_op jit(solution)/shard_map/ppermute | solution.py:51
  49.1 24.2 %collective-permute-done.3.refs_0_.refs_1_ = bf16[4,384,384]{2,1,0:T(8,128)(2,1)} collective-permute-done((bf16[4,384,384]{2,1,0:T(8,128)(2,1)S(1)}, bf16[4,384,384]{2,1,0:T(8,128)(2,1)}, u32[]{:S(2)}, u32[]{:S(2)}) %collective-permute-start.3) | collective-permute-done | bytes 1179680 | tf_op jit(solution)/shard_map/ppermute | solution.py:51
  73.3 2.7 %collective-permute-start.4 = (bf16[4,384,384]{2,1,0:T(8,128)(2,1)}, bf16[4,384,384]{2,1,0:T(8,128)(2,1)}, u32[]{:S(2)}, u32[]{:S(2)}) collective-permute-start(bf16[4,384,384]{2,1,0:T(8,128)(2,1)} %collective-permute-done.3.refs_0_.refs_1_), channel_id=1, source_target_pairs={{0,16},{1,17},{2,18},{3,19},{4,20},{5,21},{6,22},{7,23},{8,24},{9,... | collective-permute-start | bytes 3538952 | tf_op jit(solution)/shard_map/ppermute | solution.py:51
  76.9 2.8 %copy-done = bf16[768,4096]{1,0:T(8,128)(2,1)S(1)} copy-done((bf16[768,4096]{1,0:T(8,128)(2,1)S(1)}, bf16[768,4096]{1,0:T(8,128)(2,1)}, u32[]{:S(2)}) %copy-start) | copy-done | bytes 6291480
  79.7 8.6 %shard_map.85 = (f32[768,384]{1,0:T(8,128)S(1)}, f32[768,384]{1,0:T(8,128)S(1)}) custom-call(s32[8]{0:T(128)S(1)} %pad_add_fusion.table_ref, bf16[4,384,384]{2,1,0:T(8,128)(2,1)S(1)} %pad_maximum_fusion.refs_0_, bf16[4,384,384]{2,1,0:T(8,128)(2,1)S(1)} %collective-permute-done.9.refs_1_.refs_4_, bf16[768,8192]{1,0:T(8,128)(2,1)} %refs_6_.1, ...), custom_call_target="tpu_custom_call" | custom-call | flops 1811939328 | bytes 7077888 | tf_op jit(solution)/shard_map/pallas_call | solution.py:147
  88.3 26.6 %shard_map.86 = (f32[768,384]{1,0:T(8,128)S(1)}, f32[768,384]{1,0:T(8,128)S(1)}, f32[16,128]{1,0:T(8,128)S(1)}) custom-call(s32[24]{0:T(128)S(1)} %concatenate.15.table_ref, bf16[4,384,384]{2,1,0:T(8,128)(2,1)} %collective-permute-done.3.refs_0_.refs_1_, bf16[4,384,384]{2,1,0:T(8,128)(2,1)} %collective-permute-done.4.refs_1_.refs_5_, ...), custom_call_target="tpu_custom_call" | custom-call | flops 5435817984 | bytes 21233664 | tf_op jit(solution)/shard_map/pallas_call | solution.py:147
  117.9 6.0 %all-to-all-start.1 = ((f32[128,8,128]{2,1,0:T(8,128)}), f32[128,8,128]{2,1,0:T(8,128)S(1)}, u32[]{:S(2)}, u32[]{:S(2)}) async-start(f32[128,8,128]{2,1,0:T(8,128)} %broadcast_in_dim.164), calls=%async_computation.1 | async-start | bytes 1048576 | tf_op jit(solution)/shard_map/all_to_all | solution.py:327
  123.9 1.2 slice_reduce_fusion.1
  125.6 11.7 %all-to-all-done.1.all_ref = f32[128,8,128]{2,1,0:T(8,128)S(1)} async-done(((f32[128,8,128]{2,1,0:T(8,128)}), f32[128,8,128]{2,1,0:T(8,128)S(1)}, u32[]{:S(2)}, u32[]{:S(2)}) %all-to-all-start.1) | async-done | bytes 524320 | tf_op jit(solution)/shard_map/all_to_all | solution.py:327
  137.3 2.8 %copy-done.1 = bf16[768,4096]{1,0:T(8,128)(2,1)S(1)} copy-done((bf16[768,4096]{1,0:T(8,128)(2,1)S(1)}, bf16[768,4096]{1,0:T(8,128)(2,1)}, u32[]{:S(2)}) %copy-start.1) | copy-done | bytes 6291480
  140.1 1.3 copy-done.4
  141.3 1.3 copy-done.6
  142.6 6.2 %shard_map.87 = (bf16[16,384,128]{2,1,0:T(8,128)(2,1)}, bf16[768,384]{1,0:T(8,128)(2,1)S(1)}, bf16[384,768]{1,0:T(8,128)(2,1)S(1)}, f32[8,128]{1,0:T(8,128)S(1)}) custom-call(s32[16]{0:T(128)S(1)} %fusion.41.tab, f32[768,384]{1,0:T(8,128)S(1)} %copy-done.4, f32[768,384]{1,0:T(8,128)S(1)} %copy-done.6, f32[16,128]{1,0:T(8,128)S(1)} %get-tuple-element.16.stat_ref, ...), custom_call_target="tpu_custom_call" | custom-call | flops 1207959552 | bytes 8388608 | tf_op jit(solution)/shard_map/pallas_call | solution.py:194
  149.7 1.3 collective-permute-start.10
  151.6 2.8 %copy-done.2 = bf16[768,4096]{1,0:T(8,128)(2,1)S(1)} copy-done((bf16[768,4096]{1,0:T(8,128)(2,1)S(1)}, bf16[768,4096]{1,0:T(8,128)(2,1)}, u32[]{:S(2)}) %copy-start.2) | copy-done | bytes 6291480
  154.4 4.2 %shard_map.88 = f32[16,384,128]{2,1,0:T(8,128)S(1)} custom-call(s32[16]{0:T(128)S(1)} %fusion.42.tab, bf16[384,768]{1,0:T(8,128)(2,1)S(1)} %get-tuple-element.18.g_ref, bf16[768,4096]{1,0:T(8,128)(2,1)S(1)} %copy-done.2, bf16[768,4096]{1,0:T(8,128)(2,1)S(1)} %copy-done.2), custom_call_target="tpu_custom_call" | custom-call | flops 1207959552 | bytes 7340032 | tf_op jit(solution)/shard_map/pallas_call | solution.py:235
  158.5 2.0 fusion.65
  161.1 1.8 collective-permute-start.12
  163.0 4.8 %collective-permute-done.13 = bf16[4,384,128]{2,1,0:T(8,128)(2,1)S(1)} collective-permute-done((bf16[4,384,128]{2,1,0:T(8,128)(2,1)S(1)}, bf16[4,384,128]{2,1,0:T(8,128)(2,1)S(1)}, u32[]{:S(2)}, u32[]{:S(2)}) %collective-permute-start.13) | collective-permute-done | bytes 393248 | tf_op jit(solution)/shard_map/ppermute | solution.py:51
  167.8 1.8 collective-permute-done.12
  169.5 4.2 %collective-permute-done.11 = bf16[4,384,128]{2,1,0:T(8,128)(2,1)S(1)} collective-permute-done((bf16[4,384,128]{2,1,0:T(8,128)(2,1)S(1)}, bf16[4,384,128]{2,1,0:T(8,128)(2,1)S(1)}, u32[]{:S(2)}, u32[]{:S(2)}) %collective-permute-start.11) | collective-permute-done | bytes 393248 | tf_op jit(solution)/shard_map/ppermute | solution.py:51
  178.6 4.4 %collective-permute-done.14 = f32[384,128]{1,0:T(8,128)} collective-permute-done((f32[384,128]{1,0:T(8,128)S(1)}, f32[384,128]{1,0:T(8,128)}, u32[]{:S(2)}, u32[]{:S(2)}) %collective-permute-start.14) | collective-permute-done | bytes 196640 | tf_op jit(solution)/shard_map/ppermute | solution.py:51
  183.1 2.7 %fusion.6 = bf16[128,8,128]{2,1,0:T(8,128)(2,1)} fusion(s32[384]{0:T(512)S(1)} %fusion.35, pred[1024]{0:T(1024)(128)(4,1)S(1)} %fusion.14, bf16[128]{0:T(256)(128)(2,1)S(1)} %compare_select_fusion.18, f32[4,384,128]{2,1,0:T(8,128)} %copy-done.9, f32[384,128]{1,0:T(8,128)} %collective-permute-done.16, f32[384,128]{1,0:T(8,128)} %collective-permute-done.14, ...), kind=kOutput, calls=%fused_computation.9 | convolution fusion | flops 101515264 | bytes 1051392 | tf_op jit(solution)/shard_map/dot_general | solution.py:351
  185.8 6.6 %all-to-all-start.2 = ((bf16[128,8,128]{2,1,0:T(8,128)(2,1)}), bf16[128,8,128]{2,1,0:T(8,128)(2,1)S(1)}, u32[]{:S(2)}, u32[]{:S(2)}) async-start(bf16[128,8,128]{2,1,0:T(8,128)(2,1)} %fusion.6), calls=%async_computation.2 | async-start | bytes 524288 | tf_op jit(solution)/shard_map/all_to_all | solution.py:355
  192.4 22.5 %shard_map.89 = bf16[768,4096]{1,0:T(8,128)(2,1)} custom-call(s32[32]{0:T(128)S(1)} %pad_add_fusion.1.tab, bf16[4,384,384]{2,1,0:T(8,128)(2,1)S(1)} %pad_maximum_fusion.refs_0_, bf16[4,384,384]{2,1,0:T(8,128)(2,1)} %collective-permute-done.3.refs_0_.refs_1_, bf16[4,384,384]{2,1,0:T(8,128)(2,1)} %collective-permute-done.7.refs_4_.refs_2_, ...), custom_call_target="tpu_custom_call" | custom-call | flops 4831838208 | bytes 10485760 | tf_op jit(solution)/shard_map/pallas_call | solution.py:268
  (92 shorter events, 17.4 us)
Async XLA Ops:
  3.2 12.5 %copy-start.11 = (s32[8]{0:T(128)S(1)}, s32[8]{0:T(128)}, u32[]{:S(2)}) copy-start(s32[8]{0:T(128)} %param.11) | copy-start | bytes 100
  4.2 27.5 %all-to-all-start = ((bf16[128,8,384]{2,1,0:T(8,128)(2,1)}), bf16[128,8,384]{2,1,0:T(8,128)(2,1)S(1)}, u32[]{:S(2)}, u32[]{:S(2)}) async-start(bf16[128,8,384]{2,1,0:T(8,128)(2,1)} %bitcast.9), calls=%async_computation | async-start | bytes 1572864 | tf_op jit(solution)/shard_map/all_to_all | solution.py:299
  31.7 12.1 %copy-start.10 = (bf16[128,8,384]{2,1,0:T(8,128)(2,1)}, bf16[128,8,384]{2,1,0:T(8,128)(2,1)S(1)}, u32[]{:S(2)}) copy-start(bf16[128,8,384]{2,1,0:T(8,128)(2,1)S(1)} %all-to-all-done) | copy-start | bytes 2359300
  32.3 5.9 %collective-permute-start.2 = (bf16[384,384]{1,0:T(8,128)(2,1)S(1)}, bf16[384,384]{1,0:T(8,128)(2,1)S(1)}, u32[]{:S(2)}, u32[]{:S(2)}) collective-permute-start(bf16[384,384]{1,0:T(8,128)(2,1)S(1)} %fusion.3), channel_id=1, source_target_pairs={{0,12},{1,13},{2,14},{3,15},{4,0},{5,1},{6,2},{7,3},{8,4},{9,5},{1... | collective-permute-start | bytes 884744 | tf_op jit(solution)/shard_map/ppermute | solution.py:51
  33.2 7.4 %collective-permute-start.1 = (bf16[384,384]{1,0:T(8,128)(2,1)S(1)}, bf16[384,384]{1,0:T(8,128)(2,1)S(1)}, u32[]{:S(2)}, u32[]{:S(2)}) collective-permute-start(bf16[384,384]{1,0:T(8,128)(2,1)S(1)} %fusion.3), channel_id=1, source_target_pairs={{0,8},{1,9},{2,10},{3,11},{4,12},{5,13},{6,14},{7,15},{8,0},{9,1},... | collective-permute-start | bytes 884744 | tf_op jit(solution)/shard_map/ppermute | solution.py:51
  34.5 9.2 %collective-permute-start = (bf16[384,384]{1,0:T(8,128)(2,1)S(1)}, bf16[384,384]{1,0:T(8,128)(2,1)S(1)}, u32[]{:S(2)}, u32[]{:S(2)}) collective-permute-start(bf16[384,384]{1,0:T(8,128)(2,1)S(1)} %fusion.3), channel_id=1, source_target_pairs={{0,4},{1,5},{2,6},{3,7},{4,8},{5,9},{6,10},{7,11},{8,12},{9,13},{1... | collective-permute-start | bytes 884744 | tf_op jit(solution)/shard_map/ppermute | solution.py:51
  43.9 29.4 %collective-permute-start.3 = (bf16[4,384,384]{2,1,0:T(8,128)(2,1)S(1)}, bf16[4,384,384]{2,1,0:T(8,128)(2,1)}, u32[]{:S(2)}, u32[]{:S(2)}) collective-permute-start(bf16[4,384,384]{2,1,0:T(8,128)(2,1)S(1)} %pad_maximum_fusion.refs_0_), channel_id=1, source_target_pairs={{0,32},{1,33},{2,34},{3,35},{4,36},{5,37},{6,38},{7,39},{8,40},{9,... | collective-permute-start | bytes 3538952 | tf_op jit(solution)/shard_map/ppermute | solution.py:51
  44.0 32.0 %collective-permute-start.5 = (bf16[4,384,384]{2,1,0:T(8,128)(2,1)S(1)}, bf16[4,384,384]{2,1,0:T(8,128)(2,1)}, u32[]{:S(2)}, u32[]{:S(2)}) collective-permute-start(bf16[4,384,384]{2,1,0:T(8,128)(2,1)S(1)} %pad_maximum_fusion.refs_0_), channel_id=1, source_target_pairs={{0,96},{1,97},{2,98},{3,99},{4,100},{5,101},{6,102},{7,103},{8,104... | collective-permute-start | bytes 3538952 | tf_op jit(solution)/shard_map/ppermute | solution.py:51
  46.7 29.3 %collective-permute-start.7 = (bf16[4,384,384]{2,1,0:T(8,128)(2,1)S(1)}, bf16[4,384,384]{2,1,0:T(8,128)(2,1)}, u32[]{:S(2)}, u32[]{:S(2)}) collective-permute-start(bf16[4,384,384]{2,1,0:T(8,128)(2,1)S(1)} %pad_maximum_fusion.refs_0_), channel_id=1, source_target_pairs={{0,64},{1,65},{2,66},{3,67},{4,68},{5,69},{6,70},{7,71},{8,72},{9,... | collective-permute-start | bytes 3538952 | tf_op jit(solution)/shard_map/ppermute | solution.py:51
  46.8 30.1 %collective-permute-start.9 = (bf16[4,384,384]{2,1,0:T(8,128)(2,1)S(1)}, bf16[4,384,384]{2,1,0:T(8,128)(2,1)S(1)}, u32[]{:S(2)}, u32[]{:S(2)}) collective-permute-start(bf16[4,384,384]{2,1,0:T(8,128)(2,1)S(1)} %pad_maximum_fusion.refs_0_), channel_id=1, source_target_pairs={{0,16},{1,17},{2,18},{3,19},{4,20},{5,21},{6,22},{7,23},{8,24},{9,... | collective-permute-start | bytes 3538952 | tf_op jit(solution)/shard_map/ppermute | solution.py:51
  73.3 15.0 %collective-permute-start.4 = (bf16[4,384,384]{2,1,0:T(8,128)(2,1)}, bf16[4,384,384]{2,1,0:T(8,128)(2,1)}, u32[]{:S(2)}, u32[]{:S(2)}) collective-permute-start(bf16[4,384,384]{2,1,0:T(8,128)(2,1)} %collective-permute-done.3.refs_0_.refs_1_), channel_id=1, source_target_pairs={{0,16},{1,17},{2,18},{3,19},{4,20},{5,21},{6,22},{7,23},{8,24},{9,... | collective-permute-start | bytes 3538952 | tf_op jit(solution)/shard_map/ppermute | solution.py:51
  76.0 12.3 %collective-permute-start.6 = (bf16[4,384,384]{2,1,0:T(8,128)(2,1)}, bf16[4,384,384]{2,1,0:T(8,128)(2,1)}, u32[]{:S(2)}, u32[]{:S(2)}) collective-permute-start(bf16[4,384,384]{2,1,0:T(8,128)(2,1)} %collective-permute-done.5.refs_2_.refs_3_), channel_id=1, source_target_pairs={{0,16},{1,17},{2,18},{3,19},{4,20},{5,21},{6,22},{7,23},{8,24},{9,... | collective-permute-start | bytes 3538952 | tf_op jit(solution)/shard_map/ppermute | solution.py:51
  76.0 12.3 %collective-permute-start.8 = (bf16[4,384,384]{2,1,0:T(8,128)(2,1)}, bf16[4,384,384]{2,1,0:T(8,128)(2,1)}, u32[]{:S(2)}, u32[]{:S(2)}) collective-permute-start(bf16[4,384,384]{2,1,0:T(8,128)(2,1)} %collective-permute-done.7.refs_4_.refs_2_), channel_id=1, source_target_pairs={{0,16},{1,17},{2,18},{3,19},{4,20},{5,21},{6,22},{7,23},{8,24},{9,... | collective-permute-start | bytes 3538952 | tf_op jit(solution)/shard_map/ppermute | solution.py:51
  76.9 2.8 %copy-start = (bf16[768,4096]{1,0:T(8,128)(2,1)S(1)}, bf16[768,4096]{1,0:T(8,128)(2,1)}, u32[]{:S(2)}) copy-start(bf16[768,4096]{1,0:T(8,128)(2,1)} %h1_ref.3) | copy-start | bytes 18874372
  114.9 1.0 copy-start.3
  116.0 1.1 copy-start.5
  117.9 19.4 %all-to-all-start.1 = ((f32[128,8,128]{2,1,0:T(8,128)}), f32[128,8,128]{2,1,0:T(8,128)S(1)}, u32[]{:S(2)}, u32[]{:S(2)}) async-start(f32[128,8,128]{2,1,0:T(8,128)} %broadcast_in_dim.164), calls=%async_computation.1 | async-start | bytes 1048576 | tf_op jit(solution)/shard_map/all_to_all | solution.py:327
  137.3 2.8 %copy-start.1 = (bf16[768,4096]{1,0:T(8,128)(2,1)S(1)}, bf16[768,4096]{1,0:T(8,128)(2,1)}, u32[]{:S(2)}) copy-start(bf16[768,4096]{1,0:T(8,128)(2,1)} %h1_ref.3) | copy-start | bytes 18874372
  140.1 1.3 copy-start.4
  141.3 1.3 copy-start.6
  148.8 0.9 copy-start.7
  149.7 8.9 %collective-permute-start.10 = (bf16[16,384,128]{2,1,0:T(8,128)(2,1)}, bf16[16,384,128]{2,1,0:T(8,128)(2,1)}, u32[]{:S(2)}, u32[]{:S(2)}) collective-permute-start(bf16[16,384,128]{2,1,0:T(8,128)(2,1)} %get-tuple-element.19), channel_id=1, source_target_pairs={{0,16},{1,17},{2,18},{3,19},{4,20},{5,21},{6,22},{7,23},{8,24},{9,... | collective-permute-start | bytes 4718600 | tf_op jit(solution)/shard_map/ppermute | solution.py:51
  151.6 2.8 %copy-start.2 = (bf16[768,4096]{1,0:T(8,128)(2,1)S(1)}, bf16[768,4096]{1,0:T(8,128)(2,1)}, u32[]{:S(2)}) copy-start(bf16[768,4096]{1,0:T(8,128)(2,1)} %h1_ref.3) | copy-start | bytes 18874372
  160.6 7.2 %collective-permute-start.13 = (bf16[4,384,128]{2,1,0:T(8,128)(2,1)S(1)}, bf16[4,384,128]{2,1,0:T(8,128)(2,1)S(1)}, u32[]{:S(2)}, u32[]{:S(2)}) collective-permute-start(bf16[4,384,128]{2,1,0:T(8,128)(2,1)S(1)} %get-tuple-element.24), channel_id=1, source_target_pairs={{0,96},{1,97},{2,98},{3,99},{4,100},{5,101},{6,102},{7,103},{8,104... | collective-permute-start | bytes 1179656 | tf_op jit(solution)/shard_map/ppermute | solution.py:51
  161.1 8.5 %collective-permute-start.12 = (bf16[4,384,128]{2,1,0:T(8,128)(2,1)S(1)}, bf16[4,384,128]{2,1,0:T(8,128)(2,1)S(1)}, u32[]{:S(2)}, u32[]{:S(2)}) collective-permute-start(bf16[4,384,128]{2,1,0:T(8,128)(2,1)S(1)} %get-tuple-element.25), channel_id=1, source_target_pairs={{0,64},{1,65},{2,66},{3,67},{4,68},{5,69},{6,70},{7,71},{8,72},{9,... | collective-permute-start | bytes 1179656 | tf_op jit(solution)/shard_map/ppermute | solution.py:51
  162.9 10.8 %collective-permute-start.11 = (bf16[4,384,128]{2,1,0:T(8,128)(2,1)S(1)}, bf16[4,384,128]{2,1,0:T(8,128)(2,1)S(1)}, u32[]{:S(2)}, u32[]{:S(2)}) collective-permute-start(bf16[4,384,128]{2,1,0:T(8,128)(2,1)S(1)} %get-tuple-element.23), channel_id=1, source_target_pairs={{0,32},{1,33},{2,34},{3,35},{4,36},{5,37},{6,38},{7,39},{8,40},{9,... | collective-permute-start | bytes 1179656 | tf_op jit(solution)/shard_map/ppermute | solution.py:51
  173.9 2.8 %copy-start.9 = (f32[4,384,128]{2,1,0:T(8,128)}, f32[4,384,128]{2,1,0:T(8,128)S(1)}, u32[]{:S(2)}) copy-start(f32[4,384,128]{2,1,0:T(8,128)S(1)} %slice_add_fusion) | copy-start | bytes 2359300
  173.9 18.5 %copy-start.8 = (bf16[768,384]{1,0:T(8,128)(2,1)S(1)}, bf16[768,384]{1,0:T(8,128)(2,1)}, u32[]{:S(2)}) copy-start(bf16[768,384]{1,0:T(8,128)(2,1)} %copy-done.7) | copy-start | bytes 1769476
  173.9 4.7 %collective-permute-start.16 = (f32[384,128]{1,0:T(8,128)S(1)}, f32[384,128]{1,0:T(8,128)}, u32[]{:S(2)}, u32[]{:S(2)}) collective-permute-start(f32[384,128]{1,0:T(8,128)S(1)} %get-tuple-element.27), channel_id=1, source_target_pairs={{0,12},{1,13},{2,14},{3,15},{4,0},{5,1},{6,2},{7,3},{8,4},{9,5},{1... | collective-permute-start | bytes 589832 | tf_op jit(solution)/shard_map/ppermute | solution.py:51
  174.8 8.2 %collective-permute-start.14 = (f32[384,128]{1,0:T(8,128)S(1)}, f32[384,128]{1,0:T(8,128)}, u32[]{:S(2)}, u32[]{:S(2)}) collective-permute-start(f32[384,128]{1,0:T(8,128)S(1)} %get-tuple-element.28), channel_id=1, source_target_pairs={{0,4},{1,5},{2,6},{3,7},{4,8},{5,9},{6,10},{7,11},{8,12},{9,13},{1... | collective-permute-start | bytes 589832 | tf_op jit(solution)/shard_map/ppermute | solution.py:51
  175.5 7.6 %collective-permute-start.15 = (f32[384,128]{1,0:T(8,128)S(1)}, f32[384,128]{1,0:T(8,128)}, u32[]{:S(2)}, u32[]{:S(2)}) collective-permute-start(f32[384,128]{1,0:T(8,128)S(1)} %get-tuple-element.26), channel_id=1, source_target_pairs={{0,8},{1,9},{2,10},{3,11},{4,12},{5,13},{6,14},{7,15},{8,0},{9,1},... | collective-permute-start | bytes 589832 | tf_op jit(solution)/shard_map/ppermute | solution.py:51
  185.8 29.2 %all-to-all-start.2 = ((bf16[128,8,128]{2,1,0:T(8,128)(2,1)}), bf16[128,8,128]{2,1,0:T(8,128)(2,1)S(1)}, u32[]{:S(2)}, u32[]{:S(2)}) async-start(bf16[128,8,128]{2,1,0:T(8,128)(2,1)} %fusion.6), calls=%async_computation.2 | async-start | bytes 524288 | tf_op jit(solution)/shard_map/all_to_all | solution.py:355

commit v2 on v0

v2 whole, which is shorter than its diff:
```python
import jax
import jax.numpy as jnp
from jax import lax
from jax.experimental import pallas as pl
from jax.experimental.pallas import tpu as pltpu
from jax.sharding import PartitionSpec as P

BLOCK = 16
LIVE = 384
OWN = 7
VOC = 768
DT = 8192
DS = 4096
AXES = ("dp", "vocab")
F32 = jnp.float32
BF16 = jnp.bfloat16
NT = (((1,), (1,)), ((), ()))
TN = (((0,), (0,)), ((), ()))


def flat(y, c, x, z):
    return ((y * 2 + c) * 4 + x) * 4 + z


def perm_of(move):
    return [
        (flat(y, c, x, z), flat(*move(y, c, x, z)))
        for y in range(4)
        for c in range(2)
        for x in range(4)
        for z in range(4)
    ]


def minor(shift):
    return perm_of(
        lambda y, c, x, z: (y, c, (x + shift) % 4, z) if c == 0 else ((y + shift) % 4, c, x, z)
    )


def major(shift):
    return perm_of(
        lambda y, c, x, z: ((y + shift) % 4, c, x, z) if c == 0 else (y, c, (x + shift) % 4, z)
    )


def along_z(shift):
    return perm_of(lambda y, c, x, z: (y, c, x, (z + shift) % 4))


def across():
    return perm_of(
        lambda y, c, x, z: ((y + 2) % 4, c, (x - z) % 4, z) if c == 0 else ((y - z) % 4, c, (x + 2) % 4, z)
    )


SWAP = perm_of(lambda y, c, x, z: (y, 1 - c, x, z))


def permute(value, pairs):
    return lax.ppermute(value, AXES, pairs)


def unit_of(y, c, x):
    return y * 4 + x if c == 0 else 16 + x * 4 + y


BIG = 56
SMEM = pl.BlockSpec(memory_space=pltpu.SMEM)
VMEM = pl.BlockSpec(memory_space=pltpu.VMEM)
HBM = pl.BlockSpec(memory_space=pltpu.HBM)
ANY = pl.BlockSpec(memory_space=pl.ANY)


def params(limit_mib):
    return pltpu.CompilerParams(vmem_limit_bytes=limit_mib * 1024 * 1024)


def cost(flops, nbytes, transcendentals=0):
    return pl.CostEstimate(flops=flops, bytes_accessed=nbytes, transcendentals=transcendentals)


def spread_call(teacher_hidden, student_hidden, token_weight):
    def kernel(t_ref, s_ref, w_ref, out_ref):
        w = jnp.pad(w_ref[...].astype(F32), ((0, 0), (0, 256 - OWN)))
        none = jnp.zeros((1, 128), F32)
        for y in range(4):
            for c in range(2):
                for x in range(4):
                    u = unit_of(y, c, x)
                    t = t_ref[:, 256 * u : 256 * (u + 1)].astype(F32)
                    s = s_ref[:, 128 * u : 128 * (u + 1)].astype(F32)
                    t = jnp.concatenate([t, w], axis=0).astype(BF16)
                    s = jnp.concatenate([s, none], axis=0).astype(BF16)
                    for z in range(4):
                        out_ref[flat(y, c, x, z), :, :256] = t
                        out_ref[flat(y, c, x, z), :, 256:] = s

    return pl.pallas_call(
        kernel,
        grid=(1,),
        in_specs=[
            pl.BlockSpec((OWN, DT), lambda i: (0, 0)),
            pl.BlockSpec((OWN, DS), lambda i: (0, 0)),
            pl.BlockSpec((1, OWN), lambda i: (0, 0)),
        ],
        out_specs=pl.BlockSpec((128, 8, LIVE), lambda i: (0, 0, 0)),
        out_shape=jax.ShapeDtypeStruct((128, 8, LIVE), BF16),
        compiler_params=params(BIG),
        cost_estimate=cost(0, 1 << 20),
    )(teacher_hidden, student_hidden, token_weight.reshape(1, OWN))


def assemble_call(places, parts, after):
    def kernel(at_ref, *refs):
        out_ref = refs[-1]
        for k in range(4):
            out_ref[pl.ds(pl.multiple_of(256 * at_ref[k], 256), 256), :] = refs[k][:256, :]
            out_ref[pl.ds(pl.multiple_of(1024 + 128 * at_ref[k], 128), 128), :] = refs[k][256:, :]

    return pl.pallas_call(
        kernel,
        in_specs=[SMEM] + [VMEM] * 4 + [ANY] * len(after),
        out_specs=VMEM,
        out_shape=jax.ShapeDtypeStruct((1536, LIVE), BF16),
        compiler_params=params(8),
        cost_estimate=cost(0, 2 << 20),
    )(places, *parts, *after)


def logits_call(groups, stacks, teacher_head, student_head, prior, last):
    n = len(stacks)

    def kernel(at_ref, ht_ref, hs_ref, *refs):
        refs, (ht_buf, hs_buf, x_buf, acc_t, acc_s, old_t, old_s, sem, sum_sem) = refs[:-9], refs[-9:]
        x_refs, refs = refs[:n], refs[n:]
        old = []
        if prior is not None:
            old = [
                pltpu.make_async_copy(refs[0], old_t, sum_sem.at[0]),
                pltpu.make_async_copy(refs[1], old_s, sum_sem.at[1]),
            ]
            refs = refs[2:]
        new = [
            pltpu.make_async_copy(acc_t, refs[0], sum_sem.at[2]),
            pltpu.make_async_copy(acc_s, refs[1], sum_sem.at[3]),
        ]
        fetch_t, fetch_s = [], []
        for k in range(n):
            g = at_ref[k]
            cols_t = pl.ds(pl.multiple_of(1024 * g, 1024), 1024)
            cols_s = pl.ds(pl.multiple_of(512 * g, 512), 512)
            x = x_refs[k]
            fetch_t.append(
                [
                    pltpu.make_async_copy(x.at[pl.ds(0, 1024), :], x_buf.at[k, pl.ds(0, 1024), :], sem.at[k, 0]),
                    pltpu.make_async_copy(
                        ht_ref.at[pl.ds(0, 384), cols_t], ht_buf.at[k, pl.ds(0, 384), :], sem.at[k, 1]
                    ),
                    pltpu.make_async_copy(
                        ht_ref.at[pl.ds(384, 384), cols_t], ht_buf.at[k, pl.ds(384, 384), :], sem.at[k, 2]
                    ),
                ]
            )
            fetch_s.append(
                [
                    pltpu.make_async_copy(x.at[pl.ds(1024, 512), :], x_buf.at[k, pl.ds(1024, 512), :], sem.at[k, 3]),
                    pltpu.make_async_copy(hs_ref.at[:, cols_s], hs_buf.at[k], sem.at[k, 4]),
                ]
            )
            for c in fetch_t[k] + fetch_s[k]:
                c.start()
        for c in old:
            c.start()
        for k in range(n):
            end = k == n - 1
            for c in fetch_t[k]:
                c.wait()
            add_t = jnp.dot(ht_buf[k], x_buf[k, :1024, :], preferred_element_type=F32)
            if end and old:
                old[0].wait()
                add_t += old_t[...]
            if k > 0:
                acc_t[...] += add_t
            else:
                acc_t[...] = add_t
            if end:
                new[0].start()
            for c in fetch_s[k]:
                c.wait()
            add_s = jnp.dot(hs_buf[k], x_buf[k, 1024:, :], preferred_element_type=F32)
            if end and old:
                old[1].wait()
                add_s += old_s[...]
            if k > 0:
                acc_s[...] += add_s
            else:
                acc_s[...] = add_s
        new[1].start()
        if not last:
            refs[2][...] = jnp.zeros((8, 128), F32)
        if last:
            stat_ref, sent_ref = refs[2:]
            t = acc_t[...]
            top_t = jnp.max(t, axis=0, keepdims=True)
            exp_t = jnp.exp(t - top_t)
            sum_t = jnp.sum(exp_t, axis=0, keepdims=True)
            s = acc_s[...]
            cross = jnp.sum(exp_t * (t - s), axis=0, keepdims=True)
            top_s = jnp.max(s, axis=0, keepdims=True)
            sum_s = jnp.sum(jnp.exp(s - top_s), axis=0, keepdims=True)
            lse_t = top_t + jnp.log(sum_t)
            lse_s = top_s + jnp.log(sum_s)
            mean = cross / sum_t
            for j in range(3):
                cols = slice(128 * j, 128 * (j + 1))
                stat_ref[j : j + 1, :] = lse_t[:, cols]
                stat_ref[3 + j : 4 + j, :] = lse_s[:, cols]
                stat_ref[8 + j : 9 + j, :] = mean[:, cols]
            sent_ref[...] = jnp.broadcast_to(stat_ref[:8, :][None], (128, 8, 128))
        for c in new:
            c.wait()

    args = [groups, teacher_head, student_head, *stacks]
    if prior is not None:
        args += list(prior)
    out_shape = [jax.ShapeDtypeStruct((VOC, LIVE), F32)] * 2
    if last:
        out_shape.append(jax.ShapeDtypeStruct((16, 128), F32))
        out_shape.append(jax.ShapeDtypeStruct((128, 8, 128), F32))
    else:
        out_shape.append(jax.ShapeDtypeStruct((8, 128), F32))
    return pl.pallas_call(
        kernel,
        in_specs=[SMEM] + [ANY] * (len(args) - 1),
        out_specs=[ANY, ANY] + [VMEM] * (len(out_shape) - 2),
        out_shape=out_shape,
        scratch_shapes=[
            pltpu.VMEM((n, VOC, 1024), BF16),
            pltpu.VMEM((n, VOC, 512), BF16),
            pltpu.VMEM((n, 1536, LIVE), BF16),
            pltpu.VMEM((VOC, LIVE), F32),
            pltpu.VMEM((VOC, LIVE), F32),
            pltpu.VMEM((VOC, LIVE), F32),
            pltpu.VMEM((VOC, LIVE), F32),
            pltpu.SemaphoreType.DMA((n, 5)),
            pltpu.SemaphoreType.DMA((4,)),
        ],
        compiler_params=params(BIG),
        cost_estimate=cost(n * 2 * 1536 * LIVE * VOC, n * 8 << 20),
    )(*args)


def head_copies(at_ref, h_ref, h_buf, sem):
    return [
        pltpu.make_async_copy(
            h_ref.at[:, pl.ds(pl.multiple_of(512 * at_ref[k], 512), 512)], h_buf.at[k], sem.at[k]
        )
        for k in range(4)
    ]


def logit_grad_call(groups, logits_t, logits_s, stat, all_stats, weight, student_head):
    def kernel(at_ref, t_ref, s_ref, stat_ref, all_ref, w_ref, h_ref, out_ref, g_ref, kl_ref, t_buf, s_buf, h_buf, o_buf, sem, sum_sem, out_sem):
        sums = [
            pltpu.make_async_copy(s_ref, s_buf, sum_sem.at[0]),
            pltpu.make_async_copy(t_ref, t_buf, sum_sem.at[1]),
        ]
        copies = head_copies(at_ref, h_ref, h_buf, sem)
        for c in sums + copies:
            c.start()
        every = all_ref[...]
        top = jnp.max(every, axis=0)
        total = top + jnp.log(jnp.sum(jnp.exp(every - top[None]), axis=0))
        log_zt = jnp.concatenate([total[j : j + 1] for j in range(3)], axis=1)
        log_zs = jnp.concatenate([total[3 + j : 4 + j] for j in range(3)], axis=1)
        own_t = jnp.concatenate([stat_ref[j : j + 1, :] for j in range(3)], axis=1)
        mean = jnp.concatenate([stat_ref[8 + j : 9 + j, :] for j in range(3)], axis=1)
        w = w_ref[...]
        for c in sums:
            c.wait()
        g_ref[...] = (w * (jnp.exp(s_buf[...] - log_zs) - jnp.exp(t_buf[...] - log_zt))).astype(BF16)
        share = jnp.sum(w * mean * jnp.exp(own_t - log_zt), axis=1, keepdims=True)
        common = jnp.sum(w * (log_zs - log_zt), axis=1, keepdims=True)
        kl_ref[0:1, :] = jnp.broadcast_to(share, (1, 128))
        kl_ref[1:2, :] = jnp.broadcast_to(common, (1, 128))
        leave = []
        for k in range(4):
            copies[k].wait()
            o_buf[k] = lax.dot_general(h_buf[k], g_ref[...], TN, preferred_element_type=F32).astype(BF16)
            leave.append(pltpu.make_async_copy(o_buf.at[k], out_ref.at[k], out_sem.at[k]))
            leave[k].start()
        for c in leave:
            c.wait()

    return pl.pallas_call(
        kernel,
        in_specs=[SMEM, ANY, ANY, VMEM, VMEM, VMEM, ANY],
        out_specs=[ANY, VMEM, VMEM],
        scratch_shapes=[
            pltpu.VMEM((VOC, LIVE), F32),
            pltpu.VMEM((VOC, LIVE), F32),
            pltpu.VMEM((4, VOC, 512), BF16),
            pltpu.VMEM((4, 512, LIVE), BF16),
            pltpu.SemaphoreType.DMA((4,)),
            pltpu.SemaphoreType.DMA((2,)),
            pltpu.SemaphoreType.DMA((4,)),
        ],
        out_shape=[
            jax.ShapeDtypeStruct((4, 512, LIVE), BF16),
            jax.ShapeDtypeStruct((VOC, LIVE), BF16),
            jax.ShapeDtypeStruct((8, 128), F32),
        ],
        compiler_params=params(BIG - 4),
        cost_estimate=cost(2 * LIVE * VOC * 2048, 8 << 20, VOC * LIVE * 2),
    )(groups, logits_t, logits_s, stat, all_stats, weight, student_head)


def hidden_half_call(groups, grad, student_head):
    def kernel(at_ref, g_ref, h_ref, out_ref, h_buf, o_buf, sem, out_sem):
        copies = head_copies(at_ref, h_ref, h_buf, sem)
        for c in copies:
            c.start()
        leave = []
        for k in range(4):
            copies[k].wait()
            o_buf[k] = lax.dot_general(h_buf[k], g_ref[...], TN, preferred_element_type=F32)
            leave.append(pltpu.make_async_copy(o_buf.at[k], out_ref.at[k], out_sem.at[k]))
            leave[k].start()
        for c in leave:
            c.wait()

    return pl.pallas_call(
        kernel,
        in_specs=[SMEM, VMEM, ANY],
        out_specs=ANY,
        scratch_shapes=[
            pltpu.VMEM((4, VOC, 512), BF16),
            pltpu.VMEM((4, 512, LIVE), F32),
            pltpu.SemaphoreType.DMA((4,)),
            pltpu.SemaphoreType.DMA((4,)),
        ],
        out_shape=jax.ShapeDtypeStruct((4, 512, LIVE), F32),
        compiler_params=params(BIG - 4),
        cost_estimate=cost(2 * LIVE * VOC * 2048, 7 << 20),
    )(groups, grad, student_head)


def head_grad_call(groups, stacks, grad):
    n = len(stacks)

    def kernel(at_ref, g_ref, *refs):
        out_ref, done_ref, x_buf, held_ref, in_sem, out_sem = refs[n:]
        fetch = [
            pltpu.make_async_copy(refs[k].at[pl.ds(1024, 512), :], x_buf.at[k % 2], in_sem.at[k % 2])
            for k in range(n)
        ]
        store = [
            pltpu.make_async_copy(
                held_ref.at[k % 2],
                out_ref.at[:, pl.ds(pl.multiple_of(512 * at_ref[k], 512), 512)],
                out_sem.at[k % 2],
            )
            for k in range(n)
        ]
        fetch[0].start()
        for k in range(n):
            if k + 1 < n:
                fetch[k + 1].start()
            fetch[k].wait()
            if k >= 2:
                store[k - 2].wait()
            held_ref[k % 2] = lax.dot_general(
                g_ref[...], x_buf[k % 2], NT, preferred_element_type=F32
            ).astype(BF16)
            store[k].start()
        done_ref[...] = jnp.zeros((8, 128), F32)
        store[n - 2].wait()
        store[n - 1].wait()

    return pl.pallas_call(
        kernel,
        in_specs=[SMEM, VMEM] + [ANY] * n,
        out_specs=[ANY, VMEM],
        out_shape=[jax.ShapeDtypeStruct((VOC, DS), BF16), jax.ShapeDtypeStruct((8, 128), F32)],
        scratch_shapes=[
            pltpu.VMEM((2, 512, LIVE), BF16),
            pltpu.VMEM((2, VOC, 512), BF16),
            pltpu.SemaphoreType.DMA((2,)),
            pltpu.SemaphoreType.DMA((2,)),
        ],
        compiler_params=params(BIG - 4),
        cost_estimate=cost(2 * LIVE * VOC * DS, 10 << 20),
    )(groups, grad, *stacks)


def join_call(full, half):
    def kernel(f_ref, h_ref, o1_ref, o2_ref, o3_ref, own_ref, f_buf, buf, f_sem, sem):
        full = [pltpu.make_async_copy(f_ref.at[k], f_buf.at[k], f_sem.at[k]) for k in range(4)]
        copies = [pltpu.make_async_copy(h_ref.at[k], buf.at[k], sem.at[k]) for k in range(4)]
        for k in (1, 2, 3, 0):
            full[k].start()
            copies[k].start()
        for k, o_ref in ((1, o1_ref), (2, o2_ref), (3, o3_ref), (0, own_ref)):
            full[k].wait()
            copies[k].wait()
            o_ref[...] = (f_buf[k] + buf[k].astype(F32)).astype(o_ref.dtype)

    return pl.pallas_call(
        kernel,
        in_specs=[ANY, ANY],
        out_specs=[VMEM] * 4,
        out_shape=[jax.ShapeDtypeStruct((512, LIVE), BF16)] * 3 + [jax.ShapeDtypeStruct((512, LIVE), F32)],
        scratch_shapes=[
            pltpu.VMEM((4, 512, LIVE), F32),
            pltpu.VMEM((4, 512, LIVE), BF16),
            pltpu.SemaphoreType.DMA((4,)),
            pltpu.SemaphoreType.DMA((4,)),
        ],
        compiler_params=params(16),
        cost_estimate=cost(0, 8 << 20),
    )(full, half)


def sum_major_call(at, own, came, after):
    def kernel(at_ref, own_ref, c0, c1, c2, after_ref, *refs):
        outs, (buf, sem) = refs[:4], refs[4:]
        copies = [pltpu.make_async_copy(c, buf.at[k], sem.at[k]) for k, c in enumerate((c0, c1, c2))]
        for c in copies:
            c.start()
        for c in copies:
            c.wait()
        for l in (1, 2, 3, 0):
            rows = pl.ds(pl.multiple_of(128 * at_ref[l], 128), 128)
            total = own_ref[rows, :]
            for k in range(3):
                total += buf[k, rows, :].astype(F32)
            outs[l][...] = total

    return pl.pallas_call(
        kernel,
        in_specs=[SMEM, VMEM, ANY, ANY, ANY, ANY],
        out_specs=[VMEM] * 4,
        out_shape=[jax.ShapeDtypeStruct((128, LIVE), F32)] * 4,
        scratch_shapes=[pltpu.VMEM((3, 512, LIVE), BF16), pltpu.SemaphoreType.DMA((3,))],
        compiler_params=params(16),
        cost_estimate=cost(0, 4 << 20),
    )(at, own, *came, after)


def return_call(slot, own, came, kl):
    def kernel(slot_ref, own_ref, c0, c1, c2, kl_ref, out_ref, buf, sem):
        copies = [pltpu.make_async_copy(c, buf.at[k], sem.at[k]) for k, c in enumerate((c0, c1, c2))]
        for c in copies:
            c.start()
        share = kl_ref[0:1, :]
        hi = share.astype(BF16).astype(F32)
        mid = (share - hi).astype(BF16).astype(F32)
        low = share - hi - mid
        lane = lax.broadcasted_iota(jnp.int32, (1, 128), 1)
        extra = jnp.where(lane == 0, hi, jnp.where(lane == 1, mid, jnp.where(lane == 2, low, 0.0)))
        extra = jnp.broadcast_to(extra, (256, 128))
        row = lax.broadcasted_iota(jnp.int32, (256, LIVE), 0)
        eighth = lax.broadcasted_iota(jnp.int32, (256, 128), 0) % 8 == 7
        total = own_ref[...]
        for k in range(3):
            copies[k].wait()
            total += buf[k]
        total = total.astype(BF16)
        for j in range(4):
            pick = jnp.where(row + 256 * j == slot_ref[...], 1.0, 0.0).astype(BF16)
            back = lax.dot_general(pick, total, NT, preferred_element_type=F32)
            back = jnp.where(eighth, extra, back)
            out_ref[32 * j : 32 * (j + 1)] = back.reshape(32, 8, 128).astype(BF16)

    return pl.pallas_call(
        kernel,
        in_specs=[VMEM, VMEM, ANY, ANY, ANY, VMEM],
        out_specs=VMEM,
        out_shape=jax.ShapeDtypeStruct((128, 8, 128), BF16),
        scratch_shapes=[pltpu.VMEM((3, 128, LIVE), F32), pltpu.SemaphoreType.DMA((3,))],
        compiler_params=params(16),
        cost_estimate=cost(2 * 1024 * LIVE * 128, 2 << 20),
    )(slot, own, *came, kl)


def collect_call(back, kl):
    def kernel(b_ref, kl_ref, out_ref, mean_ref):
        shares = jnp.zeros((8, 128), F32)
        for y in range(4):
            for c in range(2):
                for x in range(4):
                    u = unit_of(y, c, x)
                    total = sum(b_ref[flat(y, c, x, z)].astype(F32) for z in range(4))
                    shares += total
                    out_ref[:, 128 * u : 128 * (u + 1)] = total.astype(BF16)[:OWN]
        row = lax.broadcasted_iota(jnp.int32, (8, 128), 0)
        lane = lax.broadcasted_iota(jnp.int32, (8, 128), 1)
        shares = jnp.where((row == 7) & (lane < 3), shares, 0.0)
        mean_ref[0, 0] = (jnp.sum(shares) + kl_ref[1, 0]) / LIVE

    return pl.pallas_call(
        kernel,
        in_specs=[VMEM, SMEM],
        out_specs=[VMEM, SMEM],
        out_shape=[jax.ShapeDtypeStruct((OWN, DS), BF16), jax.ShapeDtypeStruct((1, 1), F32)],
        compiler_params=params(8),
        cost_estimate=cost(0, 1 << 20),
    )(back, kl)


def local(student_hidden, teacher_hidden, student_head, teacher_head, token_weight, block_count):
    me = lax.axis_index("dp") * 16 + lax.axis_index("vocab")
    y, core, x, z = me // 32, (me // 16) % 2, (me // 4) % 4, me % 4
    turn = jnp.arange(4, dtype=jnp.int32)
    major_at = jnp.where(core == 0, y, x)
    minor_at = jnp.where(core == 0, x, y)

    arrived = lax.all_to_all(
        spread_call(teacher_hidden, student_hidden, token_weight), AXES, split_axis=0, concat_axis=0, tiled=True
    )

    ends = jnp.cumsum(block_count)
    block = jnp.arange(LIVE, dtype=jnp.int32) // BLOCK
    shard = jnp.sum((block[:, None] >= ends[None, :]).astype(jnp.int32), axis=1)
    begin = jnp.sum(jnp.where(jnp.arange(8)[None, :] < shard[:, None], block_count[None, :], 0), axis=1)
    place = (block - begin) * BLOCK + jnp.arange(LIVE, dtype=jnp.int32) % BLOCK
    slot = (shard * 16 + place // OWN) * 8 + place % OWN
    slots = jnp.arange(1024, dtype=jnp.int32)
    pick = (slot[:, None] == slots[None, :]).astype(BF16)
    own = lax.dot_general(
        arrived.reshape(1024, LIVE), pick, (((0,), (1,)), ((), ())), preferred_element_type=F32
    ).astype(BF16)
    weight = lax.dot_general(arrived[:, 7, :8].reshape(1, 1024), pick, NT, preferred_element_type=F32)

    piece = permute(own, across())
    parts = [own] + [permute(own, minor(l)) for l in (1, 2, 3)]
    heads = (teacher_head, student_head)
    stack = assemble_call((minor_at - turn + 4) % 4, parts, (piece,))
    before, after = permute(stack, major(1)), permute(stack, major(3))
    sib_stack = permute(stack, SWAP)
    pieces = [piece] + [permute(piece, along_z(l)) for l in (1, 2, 3)]

    def groups(*steps):
        steps = jnp.array(steps, jnp.int32)
        mine = core * 4 + (major_at - steps + 4) % 4
        theirs = (1 - core) * 4 + (minor_at - steps + 4) % 4
        return mine, theirs

    mine, theirs = groups(0)
    *sums, begun = logits_call(jnp.concatenate([mine, theirs]), [stack, sib_stack], *heads, None, False)
    before, after, begun = lax.optimization_barrier((before, after, begun))
    opposite = assemble_call((minor_at + z - turn + 4) % 4, pieces, [begun])
    sib_before, sib_after, sib_opposite = (permute(s, SWAP) for s in (before, after, opposite))
    mine, theirs = groups(1, 3, 2)
    *sums, _ = logits_call(mine, [before, after, opposite], *heads, sums, False)
    logits_t, logits_s, stat, sent = logits_call(
        theirs, [sib_before, sib_after, sib_opposite], *heads, sums, True
    )
    all_stats = lax.all_to_all(sent, AXES, split_axis=0, concat_axis=0, tiled=True)

    half, grad, kl = logit_grad_call(
        (1 - core) * 4 + (minor_at + turn) % 4, logits_t, logits_s, stat, all_stats, weight, heads[1]
    )
    half = permute(half, SWAP)
    full = hidden_half_call(core * 4 + (major_at + turn) % 4, grad, heads[1])
    mine, theirs = groups(0, 1, 2, 3)
    head_grad, done = head_grad_call(
        jnp.concatenate([mine, theirs]),
        [stack, before, opposite, after, sib_stack, sib_before, sib_opposite, sib_after],
        grad,
    )

    *leave, kept = join_call(full, half)
    came = [permute(leave[k - 1], major(k)) for k in (1, 2, 3)]
    kept, *leave = sum_major_call((minor_at + turn) % 4, kept, came, done)
    came = [permute(leave[l - 1], minor(l)) for l in (1, 2, 3)]
    back = return_call(slot.reshape(1, LIVE), kept, came, kl)
    back = lax.all_to_all(back, AXES, split_axis=0, concat_axis=0, tiled=True)
    hidden_grad, kl_mean = collect_call(back, kl)
    return kl_mean.reshape(()), hidden_grad, head_grad


def solution(mesh):
    rows = P(AXES, None)
    return jax.shard_map(
        local,
        mesh=mesh,
        in_specs=(rows, rows, rows, rows, P(AXES), P()),
        out_specs=(P(), rows, rows),
        check_vma=False,
    )
```

time: 817 us -> 173 us (0.21)
  blocking collectives: 555 us -> 18.8 us
  Pallas kernels: 0 us -> 53.3 us
  matrix products: 53.2 us -> 1.12 us
  waiting for transfers between devices: 91.1 us -> 54.9 us
  local copies, waits for them, and re-layouts: 32.1 us -> 5.88 us
  starting transfers between devices: 57.8 us -> 35.7 us
  between operations: 16.1 us -> 1.08 us
    unnamed x2 -> x0, blocking collectives: 426 us -> none
    all_gather x2 -> x0, waiting for transfers between devices: 66 us -> none  [the longest x1 60.3 us: local(): lax.all_gather(teacher_hidden, ('dp', 'vocab'), axis=0, tiled=True)]
    pmax x1 -> x0, blocking collectives: 64.5 us -> none  [local(): whole_t, whole_s = lax.pmax((top_t, top_s), ('dp', 'vocab'))]
    psum x1 -> x0, blocking collectives: 64.4 us -> none  [local(): lax.psum((sum_t * factor_t, cross_sum * factor_t, sum_s * factor_s), ('dp...]
    unnamed x16 -> x0, starting transfers between devices: 57.7 us -> none
    pallas_call x0 -> x13, Pallas kernels: none -> 53.3 us  [the longest x3 25.6 us: logits_call(): pl.pallas_call(kernel, in_specs=[SMEM] + [ANY] * (len(args) - 1), out_spe...]
    dot_general x4 -> x2, matrix products: 53.2 us -> 1.12 us  [the longest x1 0.69 us: local(): lax.dot_general(arrived.reshape(1024, LIVE), pick, (((0,), (1,)), ((), ()...]
    ppermute x0 -> x20, waiting for transfers between devices: none -> 27.7 us  [permute(): return lax.ppermute(value, AXES, pairs)]
  transfers between devices with their start and end apart: 18 -> 22, of which waited for: 3 -> 14; matrix products, arithmetic and copies ran while one was open for 4% -> 2% of each run, Pallas kernels for 0% -> 17%
where the time goes in v2:
time: 173 us
  waiting for transfers between devices  54.9 us (32%)
  Pallas kernels  53.3 us (31%)
  starting transfers between devices  35.7 us (21%)
  blocking collectives  18.8 us (11%)
  local copies, waits for them, and re-layouts  5.88 us (3%)
  other arithmetic  1.74 us (1%)
    ppermute x20, waiting for transfers between devices, permute(): return lax.ppermute(value, AXES, pairs)  27.7 us
    pallas_call x3, Pallas kernels, logits_call(): pl.pallas_call(kernel, in_specs=[SMEM] + [ANY] * (len(args) - 1), out_spe...  25.6 us
    ppermute x20, starting transfers between devices, permute(): return lax.ppermute(value, AXES, pairs)  19.7 us
    all_to_all x1, blocking collectives, local(): back = lax.all_to_all(back, AXES, split_axis=0, concat_axis=0, tiled=True)  18.8 us
    all_to_all x1, waiting for transfers between devices, local(): lax.all_to_all(spread_call(teacher_hidden, student_hidden, token_weight),...  15.6 us
    all_to_all x1, waiting for transfers between devices, local(): lax.all_to_all(sent, AXES, split_axis=0, concat_axis=0, tiled=True)  11.7 us
    all_to_all x1, starting transfers between devices, local(): lax.all_to_all(spread_call(teacher_hidden, student_hidden, token_weight),...  11.5 us
    pallas_call x1, Pallas kernels, head_grad_call(): pl.pallas_call(kernel, in_specs=[SMEM, VMEM] + [ANY] * n, out_specs=[ANY,...  7.68 us
  transfers between devices with their start and end apart: 22, of which 14 were waited for; matrix products, arithmetic and copies ran while one was open for 2% of the time, Pallas kernels for 17%

profile of v2, /device:TPU:1, one launch (start us, length us, event | category | flops | bytes accessed | tf_op | source)
XLA Modules:
  0.0 172.5 jit_solution(7912544640116400547)
XLA Ops:
  0.6 1.9 %shard_map.112 = bf16[128,8,384]{2,1,0:T(8,128)(2,1)} custom-call(bf16[7,8192]{1,0:T(8,128)(2,1)} %t_ref.1, bf16[7,4096]{1,0:T(8,128)(2,1)} %s_ref.1, s32[1,7]{1,0:T(1,128)} %bitcast.12), custom_call_target="tpu_custom_call" | custom-call | bytes 1048576 | tf_op jit(solution)/shard_map/pallas_call | solution.py:99
  2.5 11.5 %all-to-all-start = ((bf16[128,8,384]{2,1,0:T(8,128)(2,1)}), bf16[128,8,384]{2,1,0:T(8,128)(2,1)S(1)}, u32[]{:S(2)}, u32[]{:S(2)}) async-start(bf16[128,8,384]{2,1,0:T(8,128)(2,1)} %shard_map.112), calls=%async_computation | async-start | bytes 1572864 | tf_op jit(solution)/shard_map/all_to_all | solution.py:519
  14.4 15.6 %all-to-all-done = bf16[128,8,384]{2,1,0:T(8,128)(2,1)S(1)} async-done(((bf16[128,8,384]{2,1,0:T(8,128)(2,1)}), bf16[128,8,384]{2,1,0:T(8,128)(2,1)S(1)}, u32[]{:S(2)}, u32[]{:S(2)}) %all-to-all-start) | async-done | bytes 786464 | tf_op jit(solution)/shard_map/all_to_all | solution.py:519
  30.9 1.7 collective-permute-start.3
  34.5 3.8 %collective-permute-done.3.refs_4_.refs_0_ = bf16[384,384]{1,0:T(8,128)(2,1)S(1)} collective-permute-done((bf16[384,384]{1,0:T(8,128)(2,1)S(1)}, bf16[384,384]{1,0:T(8,128)(2,1)S(1)}, u32[]{:S(2)}, u32[]{:S(2)}) %collective-permute-start.3) | collective-permute-done | bytes 294944 | tf_op jit(solution)/shard_map/ppermute | solution.py:61
  38.3 3.3 %collective-permute-done.2.refs_3_ = bf16[384,384]{1,0:T(8,128)(2,1)S(1)} collective-permute-done((bf16[384,384]{1,0:T(8,128)(2,1)S(1)}, bf16[384,384]{1,0:T(8,128)(2,1)S(1)}, u32[]{:S(2)}, u32[]{:S(2)}) %collective-permute-start.2) | collective-permute-done | bytes 294944 | tf_op jit(solution)/shard_map/ppermute | solution.py:61
  41.6 1.6 collective-permute-done.1.refs_2_
  43.1 3.1 %collective-permute-done.refs_1_ = bf16[384,384]{1,0:T(8,128)(2,1)S(1)} collective-permute-done((bf16[384,384]{1,0:T(8,128)(2,1)S(1)}, bf16[384,384]{1,0:T(8,128)(2,1)S(1)}, u32[]{:S(2)}, u32[]{:S(2)}) %collective-permute-start) | collective-permute-done | bytes 294944 | tf_op jit(solution)/shard_map/ppermute | solution.py:61
  47.2 1.3 collective-permute-start.4
  48.5 5.0 %collective-permute-start.11 = (bf16[384,384]{1,0:T(8,128)(2,1)S(1)}, bf16[384,384]{1,0:T(8,128)(2,1)S(1)}, u32[]{:S(2)}, u32[]{:S(2)}) collective-permute-start(bf16[384,384]{1,0:T(8,128)(2,1)S(1)} %collective-permute-done.3.refs_4_.refs_0_), channel_id=1, source_target_pairs={{0,3},{1,0},{2,1},{3,2},{4,7},{5,4},{6,5},{7,6},{8,11},{9,8},{10,9... | collective-permute-start | bytes 884744 | tf_op jit(solution)/shard_map/ppermute | solution.py:61
  55.0 7.1 %shard_map.114 = (f32[768,384]{1,0:T(8,128)}, f32[768,384]{1,0:T(8,128)}, f32[8,128]{1,0:T(8,128)}) custom-call(s32[2]{0:T(128)} %pad_add_fusion.at_ref, bf16[768,8192]{1,0:T(8,128)(2,1)} %ht_ref.5, bf16[768,4096]{1,0:T(8,128)(2,1)} %h_ref.3, bf16[1536,384]{1,0:T(8,128)(2,1)} %copy-done.1, bf16[1536,384]{1,0:T(8,128)(2,1)} %copy-done.6), custom_call_target="tpu_custom_call" | custom-call | flops 1811939328 | bytes 16777216 | tf_op jit(solution)/shard_map/pallas_call | solution.py:233
  62.5 1.3 collective-permute-done.4.refs_0_.refs_1_
  64.9 4.9 %collective-permute-done.9.refs_1_ = bf16[384,384]{1,0:T(8,128)(2,1)S(1)} collective-permute-done((bf16[384,384]{1,0:T(8,128)(2,1)S(1)}, bf16[384,384]{1,0:T(8,128)(2,1)S(1)}, u32[]{:S(2)}, u32[]{:S(2)}) %collective-permute-start.9) | collective-permute-done | bytes 294944 | tf_op jit(solution)/shard_map/ppermute | solution.py:61
  73.0 9.0 %shard_map.116 = (f32[768,384]{1,0:T(8,128)}, f32[768,384]{1,0:T(8,128)}, f32[8,128]{1,0:T(8,128)}) custom-call(s32[3]{0:T(128)} %get-tuple-element.59.at_ref, bf16[768,8192]{1,0:T(8,128)(2,1)} %ht_ref.5, bf16[768,4096]{1,0:T(8,128)(2,1)} %h_ref.3, bf16[1536,384]{1,0:T(8,128)(2,1)} %collective-permute-done.4.refs_0_.refs_1_, ...), custom_call_target="tpu_custom_call" | custom-call | flops 2717908992 | bytes 25165824 | tf_op jit(solution)/shard_map/pallas_call | solution.py:233
  83.9 9.4 %shard_map.117 = (f32[768,384]{1,0:T(8,128)}, f32[768,384]{1,0:T(8,128)}, f32[16,128]{1,0:T(8,128)}, f32[128,8,128]{2,1,0:T(8,128)}) custom-call(s32[3]{0:T(128)} %get-tuple-element.60.at_ref, bf16[768,8192]{1,0:T(8,128)(2,1)} %ht_ref.5, bf16[768,4096]{1,0:T(8,128)(2,1)} %h_ref.3, bf16[1536,384]{1,0:T(8,128)(2,1)} %copy-done.8, bf16[1536,384]{1,0:T(8,128)(2,1)} %copy-done.9, ...), custom_call_target="tpu_custom_call" | custom-call | flops 2717908992 | bytes 25165824 | tf_op jit(solution)/shard_map/pallas_call | solution.py:233
  93.4 4.5 %all-to-all-start.1 = ((f32[128,8,128]{2,1,0:T(8,128)}), f32[128,8,128]{2,1,0:T(8,128)S(1)}, u32[]{:S(2)}, u32[]{:S(2)}) async-start(f32[128,8,128]{2,1,0:T(8,128)} %get-tuple-element.41), calls=%async_computation.1 | async-start | bytes 1048576 | tf_op jit(solution)/shard_map/all_to_all | solution.py:560
  97.9 1.2 slice_reduce_fusion
  99.6 11.7 %all-to-all-done.1.all_ref = f32[128,8,128]{2,1,0:T(8,128)S(1)} async-done(((f32[128,8,128]{2,1,0:T(8,128)}), f32[128,8,128]{2,1,0:T(8,128)S(1)}, u32[]{:S(2)}, u32[]{:S(2)}) %all-to-all-start.1) | async-done | bytes 524320 | tf_op jit(solution)/shard_map/all_to_all | solution.py:560
  111.3 6.7 %shard_map.118 = (bf16[4,512,384]{2,1,0:T(8,128)(2,1)}, bf16[768,384]{1,0:T(8,128)(2,1)S(1)}, f32[8,128]{1,0:T(8,128)S(1)}) custom-call(s32[4]{0:T(128)S(1)} %broadcast_add_fusion.1.at_ref, f32[768,384]{1,0:T(8,128)} %get-tuple-element.38.t_ref, f32[768,384]{1,0:T(8,128)} %get-tuple-element.39.s_ref, f32[16,128]{1,0:T(8,128)S(1)} %copy-done.4, ...), custom_call_target="tpu_custom_call" | custom-call | flops 1207959552 | bytes 8388608 | tf_op jit(solution)/shard_map/pallas_call | solution.py:296
  118.0 1.6 collective-permute-start.13
  119.6 5.1 %shard_map.119.f_ref = f32[4,512,384]{2,1,0:T(8,128)} custom-call(s32[4]{0:T(128)S(1)} %fusion.21.at_ref, bf16[768,384]{1,0:T(8,128)(2,1)S(1)} %get-tuple-element.42.g_ref, bf16[768,4096]{1,0:T(8,128)(2,1)} %h_ref.3), custom_call_target="tpu_custom_call" | custom-call | flops 1207959552 | bytes 7340032 | tf_op jit(solution)/shard_map/pallas_call | solution.py:333
  124.7 1.9 %copy-done = f32[4,512,384]{2,1,0:T(8,128)S(1)} copy-done((f32[4,512,384]{2,1,0:T(8,128)S(1)}, f32[4,512,384]{2,1,0:T(8,128)}, u32[]{:S(2)}) %copy-start) | copy-done | bytes 3145752
  126.6 1.3 shard_map.120
  129.4 1.4 collective-permute-start.16
  130.8 7.7 %shard_map.121 = (bf16[768,4096]{1,0:T(8,128)(2,1)}, f32[8,128]{1,0:T(8,128)S(1)}) custom-call(s32[8]{0:T(128)S(1)} %pad_add_fusion.1.at_ref, bf16[768,384]{1,0:T(8,128)(2,1)S(1)} %get-tuple-element.42.g_ref, bf16[1536,384]{1,0:T(8,128)(2,1)S(1)} %copy-done.2, bf16[1536,384]{1,0:T(8,128)(2,1)} %collective-permute-done.4.refs_0_.refs_1_, ...), custom_call_target="tpu_custom_call" | custom-call | flops 2415919104 | bytes 10485760 | tf_op jit(solution)/shard_map/pallas_call | solution.py:381
  138.5 1.8 %collective-permute-done.14.c0 = bf16[512,384]{1,0:T(8,128)(2,1)S(1)} collective-permute-done((bf16[512,384]{1,0:T(8,128)(2,1)S(1)}, bf16[512,384]{1,0:T(8,128)(2,1)S(1)}, u32[]{:S(2)}, u32[]{:S(2)}) %collective-permute-start.14) | collective-permute-done | bytes 393248 | tf_op jit(solution)/shard_map/ppermute | solution.py:61
  140.9 1.3 shard_map.122
  142.7 1.7 collective-permute-start.18
  145.2 5.3 %collective-permute-done.17.c0 = f32[128,384]{1,0:T(8,128)S(1)} collective-permute-done((f32[128,384]{1,0:T(8,128)S(1)}, f32[128,384]{1,0:T(8,128)S(1)}, u32[]{:S(2)}, u32[]{:S(2)}) %collective-permute-start.17) | collective-permute-done | bytes 196640 | tf_op jit(solution)/shard_map/ppermute | solution.py:61
  151.1 1.2 shard_map.123
  152.3 18.8 %all_to_all.15.b_ref = bf16[128,8,128]{2,1,0:T(8,128)(2,1)S(1)} all-to-all(bf16[128,8,128]{2,1,0:T(8,128)(2,1)S(1)} %shard_map.123), channel_id=1, replica_groups=mesh['dp'=8,'vocab'=16] {'dp','vocab'}, dimensions={0} | all-to-all | bytes 524288 | tf_op jit(solution)/shard_map/all_to_all | solution.py:579
  171.1 1.3 shard_map.124
  (71 shorter events, 16.7 us)
Async XLA Ops:
  0.6 13.4 %copy-start.11 = (s32[8]{0:T(128)S(1)}, s32[8]{0:T(128)}, u32[]{:S(2)}) copy-start(s32[8]{0:T(128)} %param.14) | copy-start | bytes 100
  2.5 27.5 %all-to-all-start = ((bf16[128,8,384]{2,1,0:T(8,128)(2,1)}), bf16[128,8,384]{2,1,0:T(8,128)(2,1)S(1)}, u32[]{:S(2)}, u32[]{:S(2)}) async-start(bf16[128,8,384]{2,1,0:T(8,128)(2,1)} %shard_map.112), calls=%async_computation | async-start | bytes 1572864 | tf_op jit(solution)/shard_map/all_to_all | solution.py:519
  30.9 7.4 %collective-permute-start.3 = (bf16[384,384]{1,0:T(8,128)(2,1)S(1)}, bf16[384,384]{1,0:T(8,128)(2,1)S(1)}, u32[]{:S(2)}, u32[]{:S(2)}) collective-permute-start(bf16[384,384]{1,0:T(8,128)(2,1)S(1)} %fusion.2.refs_0_), channel_id=1, source_target_pairs={{0,64},{1,77},{2,74},{3,71},{4,68},{5,65},{6,78},{7,75},{8,72},{9,... | collective-permute-start | bytes 884744 | tf_op jit(solution)/shard_map/ppermute | solution.py:61
  32.6 8.9 %collective-permute-start.2 = (bf16[384,384]{1,0:T(8,128)(2,1)S(1)}, bf16[384,384]{1,0:T(8,128)(2,1)S(1)}, u32[]{:S(2)}, u32[]{:S(2)}) collective-permute-start(bf16[384,384]{1,0:T(8,128)(2,1)S(1)} %fusion.2.refs_0_), channel_id=1, source_target_pairs={{0,12},{1,13},{2,14},{3,15},{4,0},{5,1},{6,2},{7,3},{8,4},{9,5},{1... | collective-permute-start | bytes 884744 | tf_op jit(solution)/shard_map/ppermute | solution.py:61
  33.4 9.7 %collective-permute-start.1 = (bf16[384,384]{1,0:T(8,128)(2,1)S(1)}, bf16[384,384]{1,0:T(8,128)(2,1)S(1)}, u32[]{:S(2)}, u32[]{:S(2)}) collective-permute-start(bf16[384,384]{1,0:T(8,128)(2,1)S(1)} %fusion.2.refs_0_), channel_id=1, source_target_pairs={{0,8},{1,9},{2,10},{3,11},{4,12},{5,13},{6,14},{7,15},{8,0},{9,1},... | collective-permute-start | bytes 884744 | tf_op jit(solution)/shard_map/ppermute | solution.py:61
  34.4 11.8 %collective-permute-start = (bf16[384,384]{1,0:T(8,128)(2,1)S(1)}, bf16[384,384]{1,0:T(8,128)(2,1)S(1)}, u32[]{:S(2)}, u32[]{:S(2)}) collective-permute-start(bf16[384,384]{1,0:T(8,128)(2,1)S(1)} %fusion.2.refs_0_), channel_id=1, source_target_pairs={{0,4},{1,5},{2,6},{3,7},{4,8},{5,9},{6,10},{7,11},{8,12},{9,13},{1... | collective-permute-start | bytes 884744 | tf_op jit(solution)/shard_map/ppermute | solution.py:61
  46.9 8.2 %copy-start.1 = (bf16[1536,384]{1,0:T(8,128)(2,1)}, bf16[1536,384]{1,0:T(8,128)(2,1)S(1)}, u32[]{:S(2)}) copy-start(bf16[1536,384]{1,0:T(8,128)(2,1)S(1)} %shard_map.113.refs_0_) | copy-start | bytes 3538948
  46.9 6.7 %collective-permute-start.6 = (bf16[1536,384]{1,0:T(8,128)(2,1)S(1)}, bf16[1536,384]{1,0:T(8,128)(2,1)S(1)}, u32[]{:S(2)}, u32[]{:S(2)}) collective-permute-start(bf16[1536,384]{1,0:T(8,128)(2,1)S(1)} %shard_map.113.refs_0_), channel_id=1, source_target_pairs={{0,16},{1,17},{2,18},{3,19},{4,20},{5,21},{6,22},{7,23},{8,24},{9,... | collective-permute-start | bytes 3538952 | tf_op jit(solution)/shard_map/ppermute | solution.py:61
  47.0 15.5 %collective-permute-start.5 = (bf16[1536,384]{1,0:T(8,128)(2,1)S(1)}, bf16[1536,384]{1,0:T(8,128)(2,1)}, u32[]{:S(2)}, u32[]{:S(2)}) collective-permute-start(bf16[1536,384]{1,0:T(8,128)(2,1)S(1)} %shard_map.113.refs_0_), channel_id=1, source_target_pairs={{0,96},{1,97},{2,98},{3,99},{4,100},{5,101},{6,102},{7,103},{8,104... | collective-permute-start | bytes 3538952 | tf_op jit(solution)/shard_map/ppermute | solution.py:61
  47.2 16.7 %collective-permute-start.4 = (bf16[1536,384]{1,0:T(8,128)(2,1)S(1)}, bf16[1536,384]{1,0:T(8,128)(2,1)}, u32[]{:S(2)}, u32[]{:S(2)}) collective-permute-start(bf16[1536,384]{1,0:T(8,128)(2,1)S(1)} %shard_map.113.refs_0_), channel_id=1, source_target_pairs={{0,32},{1,33},{2,34},{3,35},{4,36},{5,37},{6,38},{7,39},{8,40},{9,... | collective-permute-start | bytes 3538952 | tf_op jit(solution)/shard_map/ppermute | solution.py:61
  48.5 16.4 %collective-permute-start.11 = (bf16[384,384]{1,0:T(8,128)(2,1)S(1)}, bf16[384,384]{1,0:T(8,128)(2,1)S(1)}, u32[]{:S(2)}, u32[]{:S(2)}) collective-permute-start(bf16[384,384]{1,0:T(8,128)(2,1)S(1)} %collective-permute-done.3.refs_4_.refs_0_), channel_id=1, source_target_pairs={{0,3},{1,0},{2,1},{3,2},{4,7},{5,4},{6,5},{7,6},{8,11},{9,8},{10,9... | collective-permute-start | bytes 884744 | tf_op jit(solution)/shard_map/ppermute | solution.py:61
  53.4 11.5 %collective-permute-start.10 = (bf16[384,384]{1,0:T(8,128)(2,1)S(1)}, bf16[384,384]{1,0:T(8,128)(2,1)S(1)}, u32[]{:S(2)}, u32[]{:S(2)}) collective-permute-start(bf16[384,384]{1,0:T(8,128)(2,1)S(1)} %collective-permute-done.3.refs_4_.refs_0_), channel_id=1, source_target_pairs={{0,2},{1,3},{2,0},{3,1},{4,6},{5,7},{6,4},{7,5},{8,10},{9,11},{10,... | collective-permute-start | bytes 884744 | tf_op jit(solution)/shard_map/ppermute | solution.py:61
  53.5 1.5 copy-start.6
  53.5 16.3 %collective-permute-start.9 = (bf16[384,384]{1,0:T(8,128)(2,1)S(1)}, bf16[384,384]{1,0:T(8,128)(2,1)S(1)}, u32[]{:S(2)}, u32[]{:S(2)}) collective-permute-start(bf16[384,384]{1,0:T(8,128)(2,1)S(1)} %collective-permute-done.3.refs_4_.refs_0_), channel_id=1, source_target_pairs={{0,1},{1,2},{2,3},{3,0},{4,5},{5,6},{6,7},{7,4},{8,9},{9,10},{10,1... | collective-permute-start | bytes 884744 | tf_op jit(solution)/shard_map/ppermute | solution.py:61
  63.8 8.6 %copy-start.12 = (s32[3]{0:T(128)S(1)}, s32[3]{0:T(128)}, u32[]{:S(2)}) copy-start(s32[3]{0:T(128)} %constant.204) | copy-start | bytes 40
  71.2 1.9 %copy-start.3 = (bf16[1536,384]{1,0:T(8,128)(2,1)}, bf16[1536,384]{1,0:T(8,128)(2,1)S(1)}, u32[]{:S(2)}) copy-start(bf16[1536,384]{1,0:T(8,128)(2,1)S(1)} %shard_map.115.refs_2_) | copy-start | bytes 3538948
  71.2 10.9 %collective-permute-start.12 = (bf16[1536,384]{1,0:T(8,128)(2,1)S(1)}, bf16[1536,384]{1,0:T(8,128)(2,1)S(1)}, u32[]{:S(2)}, u32[]{:S(2)}) collective-permute-start(bf16[1536,384]{1,0:T(8,128)(2,1)S(1)} %shard_map.115.refs_2_), channel_id=1, source_target_pairs={{0,16},{1,17},{2,18},{3,19},{4,20},{5,21},{6,22},{7,23},{8,24},{9,... | collective-permute-start | bytes 3538952 | tf_op jit(solution)/shard_map/ppermute | solution.py:61
  71.9 10.2 %collective-permute-start.7 = (bf16[1536,384]{1,0:T(8,128)(2,1)}, bf16[1536,384]{1,0:T(8,128)(2,1)S(1)}, u32[]{:S(2)}, u32[]{:S(2)}) collective-permute-start(bf16[1536,384]{1,0:T(8,128)(2,1)} %collective-permute-done.4.refs_0_.refs_1_), channel_id=1, source_target_pairs={{0,16},{1,17},{2,18},{3,19},{4,20},{5,21},{6,22},{7,23},{8,24},{9,... | collective-permute-start | bytes 3538952 | tf_op jit(solution)/shard_map/ppermute | solution.py:61
  72.0 10.1 %collective-permute-start.8 = (bf16[1536,384]{1,0:T(8,128)(2,1)}, bf16[1536,384]{1,0:T(8,128)(2,1)S(1)}, u32[]{:S(2)}, u32[]{:S(2)}) collective-permute-start(bf16[1536,384]{1,0:T(8,128)(2,1)} %collective-permute-done.5.refs_1_.refs_3_), channel_id=1, source_target_pairs={{0,16},{1,17},{2,18},{3,19},{4,20},{5,21},{6,22},{7,23},{8,24},{9,... | collective-permute-start | bytes 3538952 | tf_op jit(solution)/shard_map/ppermute | solution.py:61
  82.1 1.4 copy-start.8
  82.1 1.8 %copy-start.9 = (bf16[1536,384]{1,0:T(8,128)(2,1)}, bf16[1536,384]{1,0:T(8,128)(2,1)S(1)}, u32[]{:S(2)}) copy-start(bf16[1536,384]{1,0:T(8,128)(2,1)S(1)} %collective-permute-done.8.refs_1_.refs_7_) | copy-start | bytes 3538948
  93.3 17.9 %copy-start.4 = (f32[16,128]{1,0:T(8,128)S(1)}, f32[16,128]{1,0:T(8,128)}, u32[]{:S(2)}) copy-start(f32[16,128]{1,0:T(8,128)} %get-tuple-element.40.stat_ref) | copy-start | bytes 24580
  93.4 17.9 %all-to-all-start.1 = ((f32[128,8,128]{2,1,0:T(8,128)}), f32[128,8,128]{2,1,0:T(8,128)S(1)}, u32[]{:S(2)}, u32[]{:S(2)}) async-start(f32[128,8,128]{2,1,0:T(8,128)} %get-tuple-element.41), calls=%async_computation.1 | async-start | bytes 1048576 | tf_op jit(solution)/shard_map/all_to_all | solution.py:560
  118.0 6.7 %collective-permute-start.13 = (bf16[4,512,384]{2,1,0:T(8,128)(2,1)}, bf16[4,512,384]{2,1,0:T(8,128)(2,1)S(1)}, u32[]{:S(2)}, u32[]{:S(2)}) collective-permute-start(bf16[4,512,384]{2,1,0:T(8,128)(2,1)} %get-tuple-element.43), channel_id=1, source_target_pairs={{0,16},{1,17},{2,18},{3,19},{4,20},{5,21},{6,22},{7,23},{8,24},{9,... | collective-permute-start | bytes 4718600 | tf_op jit(solution)/shard_map/ppermute | solution.py:61
  124.7 1.9 %copy-start = (f32[4,512,384]{2,1,0:T(8,128)S(1)}, f32[4,512,384]{2,1,0:T(8,128)}, u32[]{:S(2)}) copy-start(f32[4,512,384]{2,1,0:T(8,128)} %shard_map.119.f_ref) | copy-start | bytes 9437188
  126.6 4.3 %copy-start.2 = (bf16[1536,384]{1,0:T(8,128)(2,1)S(1)}, bf16[1536,384]{1,0:T(8,128)(2,1)}, u32[]{:S(2)}) copy-start(bf16[1536,384]{1,0:T(8,128)(2,1)} %copy-done.1) | copy-start | bytes 3538948
  127.9 12.4 %collective-permute-start.14 = (bf16[512,384]{1,0:T(8,128)(2,1)S(1)}, bf16[512,384]{1,0:T(8,128)(2,1)S(1)}, u32[]{:S(2)}, u32[]{:S(2)}) collective-permute-start(bf16[512,384]{1,0:T(8,128)(2,1)S(1)} %get-tuple-element.45), channel_id=1, source_target_pairs={{0,32},{1,33},{2,34},{3,35},{4,36},{5,37},{6,38},{7,39},{8,40},{9,... | collective-permute-start | bytes 1179656 | tf_op jit(solution)/shard_map/ppermute | solution.py:61
  128.3 12.0 %collective-permute-start.15 = (bf16[512,384]{1,0:T(8,128)(2,1)S(1)}, bf16[512,384]{1,0:T(8,128)(2,1)S(1)}, u32[]{:S(2)}, u32[]{:S(2)}) collective-permute-start(bf16[512,384]{1,0:T(8,128)(2,1)S(1)} %get-tuple-element.46), channel_id=1, source_target_pairs={{0,64},{1,65},{2,66},{3,67},{4,68},{5,69},{6,70},{7,71},{8,72},{9,... | collective-permute-start | bytes 1179656 | tf_op jit(solution)/shard_map/ppermute | solution.py:61
  129.4 11.6 %collective-permute-start.16 = (bf16[512,384]{1,0:T(8,128)(2,1)S(1)}, bf16[512,384]{1,0:T(8,128)(2,1)S(1)}, u32[]{:S(2)}, u32[]{:S(2)}) collective-permute-start(bf16[512,384]{1,0:T(8,128)(2,1)S(1)} %get-tuple-element.47), channel_id=1, source_target_pairs={{0,96},{1,97},{2,98},{3,99},{4,100},{5,101},{6,102},{7,103},{8,104... | collective-permute-start | bytes 1179656 | tf_op jit(solution)/shard_map/ppermute | solution.py:61
  142.2 8.2 %collective-permute-start.17 = (f32[128,384]{1,0:T(8,128)S(1)}, f32[128,384]{1,0:T(8,128)S(1)}, u32[]{:S(2)}, u32[]{:S(2)}) collective-permute-start(f32[128,384]{1,0:T(8,128)S(1)} %get-tuple-element.50), channel_id=1, source_target_pairs={{0,4},{1,5},{2,6},{3,7},{4,8},{5,9},{6,10},{7,11},{8,12},{9,13},{1... | collective-permute-start | bytes 589832 | tf_op jit(solution)/shard_map/ppermute | solution.py:61
  142.7 7.8 %collective-permute-start.18 = (f32[128,384]{1,0:T(8,128)S(1)}, f32[128,384]{1,0:T(8,128)S(1)}, u32[]{:S(2)}, u32[]{:S(2)}) collective-permute-start(f32[128,384]{1,0:T(8,128)S(1)} %get-tuple-element.51), channel_id=1, source_target_pairs={{0,8},{1,9},{2,10},{3,11},{4,12},{5,13},{6,14},{7,15},{8,0},{9,1},... | collective-permute-start | bytes 589832 | tf_op jit(solution)/shard_map/ppermute | solution.py:61
  144.3 6.8 %collective-permute-start.19 = (f32[128,384]{1,0:T(8,128)S(1)}, f32[128,384]{1,0:T(8,128)S(1)}, u32[]{:S(2)}, u32[]{:S(2)}) collective-permute-start(f32[128,384]{1,0:T(8,128)S(1)} %get-tuple-element.52), channel_id=1, source_target_pairs={{0,12},{1,13},{2,14},{3,15},{4,0},{5,1},{6,2},{7,3},{8,4},{9,5},{1... | collective-permute-start | bytes 589832 | tf_op jit(solution)/shard_map/ppermute | solution.py:61
  (3 other events, 2.6 us)

commit v3 on v2

--- a/solution.py
+++ b/solution.py
@@ -128,23 +128,32 @@
     )(places, *parts, *after)
 
 
+def hold_call(values, after):
+    n = len(values)
+
+    def kernel(*refs):
+        pass
+
+    return pl.pallas_call(
+        kernel,
+        in_specs=[ANY] * (n + len(after)),
+        out_specs=[ANY] * n,
+        out_shape=[jax.ShapeDtypeStruct(v.shape, v.dtype) for v in values],
+        input_output_aliases={k: k for k in range(n)},
+        compiler_params=params(50),
+        cost_estimate=cost(0, 0),
+    )(*values, *after)
+
+
 def logits_call(groups, stacks, teacher_head, student_head, prior, last):
     n = len(stacks)
 
     def kernel(at_ref, ht_ref, hs_ref, *refs):
-        refs, (ht_buf, hs_buf, x_buf, acc_t, acc_s, old_t, old_s, sem, sum_sem) = refs[:-9], refs[-9:]
+        refs, (ht_buf, hs_buf, x_buf, sem) = refs[:-4], refs[-4:]
         x_refs, refs = refs[:n], refs[n:]
-        old = []
         if prior is not None:
-            old = [
-                pltpu.make_async_copy(refs[0], old_t, sum_sem.at[0]),
-                pltpu.make_async_copy(refs[1], old_s, sum_sem.at[1]),
-            ]
-            refs = refs[2:]
-        new = [
-            pltpu.make_async_copy(acc_t, refs[0], sum_sem.at[2]),
-            pltpu.make_async_copy(acc_s, refs[1], sum_sem.at[3]),
-        ]
+            old_t, old_s, *refs = refs
+        acc_t, acc_s = refs[:2]
         fetch_t, fetch_s = [], []
         for k in range(n):
             g = at_ref[k]
@@ -170,33 +179,25 @@
             )
             for c in fetch_t[k] + fetch_s[k]:
                 c.start()
-        for c in old:
-            c.start()
         for k in range(n):
-            end = k == n - 1
             for c in fetch_t[k]:
                 c.wait()
             add_t = jnp.dot(ht_buf[k], x_buf[k, :1024, :], preferred_element_type=F32)
-            if end and old:
-                old[0].wait()
-                add_t += old_t[...]
             if k > 0:
                 acc_t[...] += add_t
+            elif prior is None:
+                acc_t[...] = add_t
             else:
-                acc_t[...] = add_t
-            if end:
-                new[0].start()
+                acc_t[...] = old_t[...] + add_t
             for c in fetch_s[k]:
                 c.wait()
             add_s = jnp.dot(hs_buf[k], x_buf[k, 1024:, :], preferred_element_type=F32)
-            if end and old:
-                old[1].wait()
-                add_s += old_s[...]
             if k > 0:
                 acc_s[...] += add_s
+            elif prior is None:
+                acc_s[...] = add_s
             else:
-                acc_s[...] = add_s
-        new[1].start()
+                acc_s[...] = old_s[...] + add_s
         if not last:
             refs[2][...] = jnp.zeros((8, 128), F32)
         if last:
@@ -218,8 +219,6 @@
                 stat_ref[3 + j : 4 + j, :] = lse_s[:, cols]
                 stat_ref[8 + j : 9 + j, :] = mean[:, cols]
             sent_ref[...] = jnp.broadcast_to(stat_ref[:8, :][None], (128, 8, 128))
-        for c in new:
-            c.wait()
 
     args = [groups, teacher_head, student_head, *stacks]
     if prior is not None:
@@ -232,43 +231,23 @@
         out_shape.append(jax.ShapeDtypeStruct((8, 128), F32))
     return pl.pallas_call(
         kernel,
-        in_specs=[SMEM] + [ANY] * (len(args) - 1),
-        out_specs=[ANY, ANY] + [VMEM] * (len(out_shape) - 2),
+        in_specs=[SMEM] + [ANY] * (n + 2) + [VMEM] * (len(args) - 3 - n),
+        out_specs=[VMEM] * len(out_shape),
         out_shape=out_shape,
+        input_output_aliases={} if prior is None else {3 + n: 0, 4 + n: 1},
         scratch_shapes=[
             pltpu.VMEM((n, VOC, 1024), BF16),
             pltpu.VMEM((n, VOC, 512), BF16),
             pltpu.VMEM((n, 1536, LIVE), BF16),
-            pltpu.VMEM((VOC, LIVE), F32),
-            pltpu.VMEM((VOC, LIVE), F32),
-            pltpu.VMEM((VOC, LIVE), F32),
-            pltpu.VMEM((VOC, LIVE), F32),
             pltpu.SemaphoreType.DMA((n, 5)),
-            pltpu.SemaphoreType.DMA((4,)),
         ],
-        compiler_params=params(BIG),
+        compiler_params=params(50),
         cost_estimate=cost(n * 2 * 1536 * LIVE * VOC, n * 8 << 20),
     )(*args)
 
 
-def head_copies(at_ref, h_ref, h_buf, sem):
-    return [
-        pltpu.make_async_copy(
-            h_ref.at[:, pl.ds(pl.multiple_of(512 * at_ref[k], 512), 512)], h_buf.at[k], sem.at[k]
-        )
-        for k in range(4)
-    ]
-
-
 def logit_grad_call(groups, logits_t, logits_s, stat, all_stats, weight, student_head):
-    def kernel(at_ref, t_ref, s_ref, stat_ref, all_ref, w_ref, h_ref, out_ref, g_ref, kl_ref, t_buf, s_buf, h_buf, o_buf, sem, sum_sem, out_sem):
-        sums = [
-            pltpu.make_async_copy(s_ref, s_buf, sum_sem.at[0]),
-            pltpu.make_async_copy(t_ref, t_buf, sum_sem.at[1]),
-        ]
-        copies = head_copies(at_ref, h_ref, h_buf, sem)
-        for c in sums + copies:
-            c.start()
+    def kernel(at_ref, t_ref, s_ref, stat_ref, all_ref, w_ref, h_ref, out_ref, g_ref, kl_ref):
         every = all_ref[...]
         top = jnp.max(every, axis=0)
         total = top + jnp.log(jnp.sum(jnp.exp(every - top[None]), axis=0))
@@ -277,71 +256,41 @@
         own_t = jnp.concatenate([stat_ref[j : j + 1, :] for j in range(3)], axis=1)
         mean = jnp.concatenate([stat_ref[8 + j : 9 + j, :] for j in range(3)], axis=1)
         w = w_ref[...]
-        for c in sums:
-            c.wait()
-        g_ref[...] = (w * (jnp.exp(s_buf[...] - log_zs) - jnp.exp(t_buf[...] - log_zt))).astype(BF16)
+        g_ref[...] = (w * (jnp.exp(s_ref[...] - log_zs) - jnp.exp(t_ref[...] - log_zt))).astype(BF16)
         share = jnp.sum(w * mean * jnp.exp(own_t - log_zt), axis=1, keepdims=True)
         common = jnp.sum(w * (log_zs - log_zt), axis=1, keepdims=True)
         kl_ref[0:1, :] = jnp.broadcast_to(share, (1, 128))
         kl_ref[1:2, :] = jnp.broadcast_to(common, (1, 128))
-        leave = []
         for k in range(4):
-            copies[k].wait()
-            o_buf[k] = lax.dot_general(h_buf[k], g_ref[...], TN, preferred_element_type=F32).astype(BF16)
-            leave.append(pltpu.make_async_copy(o_buf.at[k], out_ref.at[k], out_sem.at[k]))
-            leave[k].start()
-        for c in leave:
-            c.wait()
-
-    return pl.pallas_call(
-        kernel,
-        in_specs=[SMEM, ANY, ANY, VMEM, VMEM, VMEM, ANY],
-        out_specs=[ANY, VMEM, VMEM],
-        scratch_shapes=[
-            pltpu.VMEM((VOC, LIVE), F32),
-            pltpu.VMEM((VOC, LIVE), F32),
-            pltpu.VMEM((4, VOC, 512), BF16),
-            pltpu.VMEM((4, 512, LIVE), BF16),
-            pltpu.SemaphoreType.DMA((4,)),
-            pltpu.SemaphoreType.DMA((2,)),
-            pltpu.SemaphoreType.DMA((4,)),
-        ],
+            head = h_ref[:, pl.ds(pl.multiple_of(512 * at_ref[k], 512), 512)]
+            out_ref[k] = lax.dot_general(head, g_ref[...], TN, preferred_element_type=F32).astype(BF16)
+
+    return pl.pallas_call(
+        kernel,
+        in_specs=[SMEM] + [VMEM] * 6,
+        out_specs=[VMEM] * 3,
         out_shape=[
             jax.ShapeDtypeStruct((4, 512, LIVE), BF16),
             jax.ShapeDtypeStruct((VOC, LIVE), BF16),
             jax.ShapeDtypeStruct((8, 128), F32),
         ],
-        compiler_params=params(BIG - 4),
+        compiler_params=params(16),
         cost_estimate=cost(2 * LIVE * VOC * 2048, 8 << 20, VOC * LIVE * 2),
     )(groups, logits_t, logits_s, stat, all_stats, weight, student_head)
 
 
 def hidden_half_call(groups, grad, student_head):
-    def kernel(at_ref, g_ref, h_ref, out_ref, h_buf, o_buf, sem, out_sem):
-        copies = head_copies(at_ref, h_ref, h_buf, sem)
-        for c in copies:
-            c.start()
-        leave = []
+    def kernel(at_ref, g_ref, h_ref, out_ref):
         for k in range(4):
-            copies[k].wait()
-            o_buf[k] = lax.dot_general(h_buf[k], g_ref[...], TN, preferred_element_type=F32)
-            leave.append(pltpu.make_async_copy(o_buf.at[k], out_ref.at[k], out_sem.at[k]))
-            leave[k].start()
-        for c in leave:
-            c.wait()
-
-    return pl.pallas_call(
-        kernel,
-        in_specs=[SMEM, VMEM, ANY],
-        out_specs=ANY,
-        scratch_shapes=[
-            pltpu.VMEM((4, VOC, 512), BF16),
-            pltpu.VMEM((4, 512, LIVE), F32),
-            pltpu.SemaphoreType.DMA((4,)),
-            pltpu.SemaphoreType.DMA((4,)),
-        ],
+            head = h_ref[:, pl.ds(pl.multiple_of(512 * at_ref[k], 512), 512)]
+            out_ref[k] = lax.dot_general(head, g_ref[...], TN, preferred_element_type=F32)
+
+    return pl.pallas_call(
+        kernel,
+        in_specs=[SMEM, VMEM, VMEM],
+        out_specs=VMEM,
         out_shape=jax.ShapeDtypeStruct((4, 512, LIVE), F32),
-        compiler_params=params(BIG - 4),
+        compiler_params=params(16),
         cost_estimate=cost(2 * LIVE * VOC * 2048, 7 << 20),
     )(groups, grad, student_head)
 
@@ -435,13 +384,13 @@
             total = own_ref[rows, :]
             for k in range(3):
                 total += buf[k, rows, :].astype(F32)
-            outs[l][...] = total
+            outs[l][...] = total.astype(outs[l].dtype)
 
     return pl.pallas_call(
         kernel,
         in_specs=[SMEM, VMEM, ANY, ANY, ANY, ANY],
         out_specs=[VMEM] * 4,
-        out_shape=[jax.ShapeDtypeStruct((128, LIVE), F32)] * 4,
+        out_shape=[jax.ShapeDtypeStruct((128, LIVE), F32)] + [jax.ShapeDtypeStruct((128, LIVE), BF16)] * 3,
         scratch_shapes=[pltpu.VMEM((3, 512, LIVE), BF16), pltpu.SemaphoreType.DMA((3,))],
         compiler_params=params(16),
         cost_estimate=cost(0, 4 << 20),
@@ -465,7 +414,7 @@
         total = own_ref[...]
         for k in range(3):
             copies[k].wait()
-            total += buf[k]
+            total += buf[k].astype(F32)
         total = total.astype(BF16)
         for j in range(4):
             pick = jnp.where(row + 256 * j == slot_ref[...], 1.0, 0.0).astype(BF16)
@@ -478,7 +427,7 @@
         in_specs=[VMEM, VMEM, ANY, ANY, ANY, VMEM],
         out_specs=VMEM,
         out_shape=jax.ShapeDtypeStruct((128, 8, 128), BF16),
-        scratch_shapes=[pltpu.VMEM((3, 128, LIVE), F32), pltpu.SemaphoreType.DMA((3,))],
+        scratch_shapes=[pltpu.VMEM((3, 128, LIVE), BF16), pltpu.SemaphoreType.DMA((3,))],
         compiler_params=params(16),
         cost_estimate=cost(2 * 1024 * LIVE * 128, 2 << 20),
     )(slot, own, *came, kl)
@@ -548,14 +497,14 @@
         return mine, theirs
 
     mine, theirs = groups(0)
-    *sums, begun = logits_call(jnp.concatenate([mine, theirs]), [stack, sib_stack], *heads, None, False)
-    before, after, begun = lax.optimization_barrier((before, after, begun))
-    opposite = assemble_call((minor_at + z - turn + 4) % 4, pieces, [begun])
+    *sums, token = logits_call(jnp.concatenate([mine, theirs]), [stack, sib_stack], *heads, None, False)
+    opposite = assemble_call((minor_at + z - turn + 4) % 4, pieces, [token])
+    before, after = hold_call([before, after], [token])
     sib_before, sib_after, sib_opposite = (permute(s, SWAP) for s in (before, after, opposite))
-    mine, theirs = groups(1, 3, 2)
-    *sums, _ = logits_call(mine, [before, after, opposite], *heads, sums, False)
+    mine, theirs = groups(1, 3)
+    *sums, _ = logits_call(mine, [before, after], *heads, sums, False)
     logits_t, logits_s, stat, sent = logits_call(
-        theirs, [sib_before, sib_after, sib_opposite], *heads, sums, True
+        jnp.concatenate([theirs, *groups(2)]), [sib_before, sib_after, opposite, sib_opposite], *heads, sums, True
     )
     all_stats = lax.all_to_all(sent, AXES, split_axis=0, concat_axis=0, tiled=True)
 

time: 173 us -> 162 us (0.936)
  Pallas kernels: 53.3 us -> 43.1 us
  waiting for transfers between devices: 54.9 us -> 50.3 us
  starting transfers between devices: 35.7 us -> 37.8 us
    pallas_call x5 -> x6, Pallas kernels: 37.4 us -> 25.8 us  [the longest x3 20.1 us: logits_call(): pl.pallas_call(kernel, in_specs=[SMEM] + [ANY] * (n + 2) + [VMEM] * (len(...]
    all_to_all x1, waiting for transfers between devices: 11.7 us -> 8.67 us  [local(): lax.all_to_all(sent, AXES, split_axis=0, concat_axis=0, tiled=True)]
    unnamed x26 -> x20, local copies, waits for them, and re-layouts: 4.6 us -> 3.77 us
  transfers between devices with their start and end apart: 22 -> 22, of which waited for: 14 -> 14; matrix products, arithmetic and copies ran while one was open for 2% -> 3% of each run, Pallas kernels for 17% -> 15%
where the time goes in v3:
time: 162 us; the launch traced here: 161 us
  waiting for transfers between devices  50.3 us (31%)
  Pallas kernels  43.1 us (27%)
  starting transfers between devices  37.8 us (23%)
  blocking collectives  19.1 us (12%)
  local copies, waits for them, and re-layouts  7.01 us (4%)
  matrix products  1.81 us (1%)
    ppermute x20, waiting for transfers between devices, permute(): return lax.ppermute(value, AXES, pairs)  26.6 us
    ppermute x20, starting transfers between devices, permute(): return lax.ppermute(value, AXES, pairs)  21.4 us
    pallas_call x3, Pallas kernels, logits_call(): pl.pallas_call(kernel, in_specs=[SMEM] + [ANY] * (n + 2) + [VMEM] * (len(...  20.1 us
    all_to_all x1, blocking collectives, local(): back = lax.all_to_all(back, AXES, split_axis=0, concat_axis=0, tiled=True)  19.1 us
    all_to_all x1, waiting for transfers between devices, local(): lax.all_to_all(spread_call(teacher_hidden, student_hidden, token_weight),...  15 us
    all_to_all x1, starting transfers between devices, local(): lax.all_to_all(spread_call(teacher_hidden, student_hidden, token_weight),...  11.5 us
    all_to_all x1, waiting for transfers between devices, local(): lax.all_to_all(sent, AXES, split_axis=0, concat_axis=0, tiled=True)  8.67 us
    pallas_call x1, Pallas kernels, head_grad_call(): pl.pallas_call(kernel, in_specs=[SMEM, VMEM] + [ANY] * n, out_specs=[ANY,...  7.69 us
  transfers between devices with their start and end apart: 22, of which 14 were waited for; matrix products, arithmetic and copies ran while one was open for 3% of the time, Pallas kernels for 15%

profile of v3, /device:TPU:1, one launch (start us, length us, event | category | flops | bytes accessed | tf_op | source)
XLA Modules:
  0.0 161.5 jit_solution(3959051409325226477)
XLA Ops:
  0.6 1.9 %shard_map.121 = bf16[128,8,384]{2,1,0:T(8,128)(2,1)} custom-call(bf16[7,8192]{1,0:T(8,128)(2,1)} %t_ref.1, bf16[7,4096]{1,0:T(8,128)(2,1)} %s_ref.1, s32[1,7]{1,0:T(1,128)} %bitcast.14), custom_call_target="tpu_custom_call" | custom-call | bytes 1048576 | tf_op jit(solution)/shard_map/pallas_call | solution.py:99
  2.5 11.5 %all-to-all-start = ((bf16[128,8,384]{2,1,0:T(8,128)(2,1)}), bf16[128,8,384]{2,1,0:T(8,128)(2,1)S(1)}, u32[]{:S(2)}, u32[]{:S(2)}) async-start(bf16[128,8,384]{2,1,0:T(8,128)(2,1)} %shard_map.121), calls=%async_computation | async-start | bytes 1572864 | tf_op jit(solution)/shard_map/all_to_all | solution.py:468
  15.0 15.0 %all-to-all-done = bf16[128,8,384]{2,1,0:T(8,128)(2,1)S(1)} async-done(((bf16[128,8,384]{2,1,0:T(8,128)(2,1)}), bf16[128,8,384]{2,1,0:T(8,128)(2,1)S(1)}, u32[]{:S(2)}, u32[]{:S(2)}) %all-to-all-start) | async-done | bytes 786464 | tf_op jit(solution)/shard_map/all_to_all | solution.py:468
  30.7 1.8 %collective-permute-start.3 = (bf16[384,384]{1,0:T(8,128)(2,1)S(1)}, bf16[384,384]{1,0:T(8,128)(2,1)}, u32[]{:S(2)}, u32[]{:S(2)}) collective-permute-start(bf16[384,384]{1,0:T(8,128)(2,1)S(1)} %fusion.2.refs_0_), channel_id=1, source_target_pairs={{0,64},{1,77},{2,74},{3,71},{4,68},{5,65},{6,78},{7,75},{8,72},{9,... | collective-permute-start | bytes 884744 | tf_op jit(solution)/shard_map/ppermute | solution.py:61
  34.4 3.9 %collective-permute-done.3.refs_4_.refs_0_ = bf16[384,384]{1,0:T(8,128)(2,1)} collective-permute-done((bf16[384,384]{1,0:T(8,128)(2,1)S(1)}, bf16[384,384]{1,0:T(8,128)(2,1)}, u32[]{:S(2)}, u32[]{:S(2)}) %collective-permute-start.3) | collective-permute-done | bytes 294944 | tf_op jit(solution)/shard_map/ppermute | solution.py:61
  38.3 3.3 %collective-permute-done.2.refs_3_ = bf16[384,384]{1,0:T(8,128)(2,1)S(1)} collective-permute-done((bf16[384,384]{1,0:T(8,128)(2,1)S(1)}, bf16[384,384]{1,0:T(8,128)(2,1)S(1)}, u32[]{:S(2)}, u32[]{:S(2)}) %collective-permute-start.2) | collective-permute-done | bytes 294944 | tf_op jit(solution)/shard_map/ppermute | solution.py:61
  41.6 1.5 collective-permute-done.1.refs_2_
  43.0 3.0 %collective-permute-done.refs_1_ = bf16[384,384]{1,0:T(8,128)(2,1)S(1)} collective-permute-done((bf16[384,384]{1,0:T(8,128)(2,1)S(1)}, bf16[384,384]{1,0:T(8,128)(2,1)S(1)}, u32[]{:S(2)}, u32[]{:S(2)}) %collective-permute-start) | collective-permute-done | bytes 294944 | tf_op jit(solution)/shard_map/ppermute | solution.py:61
  47.0 1.3 collective-permute-start.4
  48.4 4.9 %collective-permute-start.11 = (bf16[384,384]{1,0:T(8,128)(2,1)}, bf16[384,384]{1,0:T(8,128)(2,1)}, u32[]{:S(2)}, u32[]{:S(2)}) collective-permute-start(bf16[384,384]{1,0:T(8,128)(2,1)} %collective-permute-done.3.refs_4_.refs_0_), channel_id=1, source_target_pairs={{0,3},{1,0},{2,1},{3,2},{4,7},{5,4},{6,5},{7,6},{8,11},{9,8},{10,9... | collective-permute-start | bytes 884744 | tf_op jit(solution)/shard_map/ppermute | solution.py:61
  54.5 5.2 %shard_map.123 = (f32[768,384]{1,0:T(8,128)S(1)}, f32[768,384]{1,0:T(8,128)S(1)}, f32[8,128]{1,0:T(8,128)S(1)}) custom-call(s32[2]{0:T(128)S(1)} %pad_add_fusion.1.at_ref, bf16[768,8192]{1,0:T(8,128)(2,1)} %ht_ref.5, bf16[768,4096]{1,0:T(8,128)(2,1)} %h_ref.3, bf16[1536,384]{1,0:T(8,128)(2,1)S(1)} %shard_map.122.refs_0_, bf16[1536,384]{1,0:T(8,128)(2,1)} %copy-done.2), custom_call_target="tpu_custom_call" | custom-call | flops 1811939328 | bytes 16777216 | tf_op jit(solution)/shard_map/pallas_call | solution.py:232
  59.7 2.7 %collective-permute-done.5.refs_1_ = bf16[1536,384]{1,0:T(8,128)(2,1)} collective-permute-done((bf16[1536,384]{1,0:T(8,128)(2,1)S(1)}, bf16[1536,384]{1,0:T(8,128)(2,1)}, u32[]{:S(2)}, u32[]{:S(2)}) %collective-permute-start.5) | collective-permute-done | bytes 1179680 | tf_op jit(solution)/shard_map/ppermute | solution.py:61
  62.3 1.3 collective-permute-done.4.refs_0_
  63.7 2.2 %collective-permute-start.7 = (bf16[1536,384]{1,0:T(8,128)(2,1)}, bf16[1536,384]{1,0:T(8,128)(2,1)}, u32[]{:S(2)}, u32[]{:S(2)}) collective-permute-start(bf16[1536,384]{1,0:T(8,128)(2,1)} %get-tuple-element.30.refs_0_.refs_1_), channel_id=1, source_target_pairs={{0,16},{1,17},{2,18},{3,19},{4,20},{5,21},{6,22},{7,23},{8,24},{9,... | collective-permute-start | bytes 3538952 | tf_op jit(solution)/shard_map/ppermute | solution.py:61
  65.9 4.1 %collective-permute-done.9.refs_1_ = bf16[384,384]{1,0:T(8,128)(2,1)} collective-permute-done((bf16[384,384]{1,0:T(8,128)(2,1)}, bf16[384,384]{1,0:T(8,128)(2,1)}, u32[]{:S(2)}, u32[]{:S(2)}) %collective-permute-start.9) | collective-permute-done | bytes 294944 | tf_op jit(solution)/shard_map/ppermute | solution.py:61
  70.0 2.4 %shard_map.125.refs_2_ = bf16[1536,384]{1,0:T(8,128)(2,1)} custom-call(s32[4]{0:T(128)S(1)} %and_select_fusion.6.at_ref, bf16[384,384]{1,0:T(8,128)(2,1)} %collective-permute-done.3.refs_4_.refs_0_, bf16[384,384]{1,0:T(8,128)(2,1)} %collective-permute-done.9.refs_1_, bf16[384,384]{1,0:T(8,128)(2,1)} %collective-permute-done.10.refs_2_, ...), custom_call_target="tpu_custom_call" | custom-call | bytes 2097152 | tf_op jit(solution)/shard_map/pallas_call | solution.py:121
  73.1 5.9 %shard_map.126 = (f32[768,384]{1,0:T(8,128)S(1)}, f32[768,384]{1,0:T(8,128)S(1)}, f32[8,128]{1,0:T(8,128)}) custom-call(s32[2]{0:T(128)S(1)} %get-tuple-element.57.at_ref, bf16[768,8192]{1,0:T(8,128)(2,1)} %ht_ref.5, bf16[768,4096]{1,0:T(8,128)(2,1)} %h_ref.3, ...), custom_call_target="tpu_custom_call", output_to_operand_aliasing={{0}: (5, {}), {1}: (6, {})} | custom-call | flops 1811939328 | bytes 16777216 | tf_op jit(solution)/shard_map/pallas_call | solution.py:232
  79.1 9.0 %shard_map.127 = (f32[768,384]{1,0:T(8,128)S(1)}, f32[768,384]{1,0:T(8,128)S(1)}, f32[16,128]{1,0:T(8,128)S(1)}, f32[128,8,128]{2,1,0:T(8,128)S(1)}) custom-call(s32[4]{0:T(128)S(1)} %pad_add_fusion.at_ref, bf16[768,8192]{1,0:T(8,128)(2,1)} %ht_ref.5, bf16[768,4096]{1,0:T(8,128)(2,1)} %h_ref.3, ...), custom_call_target="tpu_custom_call", output_to_operand_aliasing={{0}: (7, {}), {1}: (8, {})} | custom-call | flops 3623878656 | bytes 33554432 | tf_op jit(solution)/shard_map/pallas_call | solution.py:232
  88.9 5.0 %all-to-all-start.1 = ((f32[128,8,128]{2,1,0:T(8,128)}), f32[128,8,128]{2,1,0:T(8,128)}, u32[]{:S(2)}, u32[]{:S(2)}) async-start(f32[128,8,128]{2,1,0:T(8,128)} %copy-done.1), calls=%async_computation.1 | async-start | bytes 1048576 | tf_op jit(solution)/shard_map/all_to_all | solution.py:509
  93.9 1.8 %slice_reduce_fusion = bf16[128,8]{1,0:T(8,128)(2,1)} fusion(bf16[128,8,384]{2,1,0:T(8,128)(2,1)} %copy-done.3), kind=kLoop, calls=%fused_computation.7 | loop fusion | bytes 4096 | tf_op jit(solution)/shard_map/slice | solution.py:483
  95.7 1.4 reshape.237
  98.3 8.7 %all-to-all-done.1.all_ref = f32[128,8,128]{2,1,0:T(8,128)} async-done(((f32[128,8,128]{2,1,0:T(8,128)}), f32[128,8,128]{2,1,0:T(8,128)}, u32[]{:S(2)}, u32[]{:S(2)}) %all-to-all-start.1) | async-done | bytes 524320 | tf_op jit(solution)/shard_map/all_to_all | solution.py:509
  107.0 2.8 %copy-done = bf16[768,4096]{1,0:T(8,128)(2,1)S(1)} copy-done((bf16[768,4096]{1,0:T(8,128)(2,1)S(1)}, bf16[768,4096]{1,0:T(8,128)(2,1)}, u32[]{:S(2)}) %copy-start) | copy-done | bytes 6291480
  109.7 3.3 %shard_map.128 = (bf16[4,512,384]{2,1,0:T(8,128)(2,1)S(1)}, bf16[768,384]{1,0:T(8,128)(2,1)S(1)}, f32[8,128]{1,0:T(8,128)S(1)}) custom-call(s32[4]{0:T(128)S(1)} %broadcast_add_fusion.1.at_ref, f32[768,384]{1,0:T(8,128)S(1)} %get-tuple-element.36.t_ref, f32[768,384]{1,0:T(8,128)S(1)} %get-tuple-element.37.s_ref, f32[16,128]{1,0:T(8,128)S(1)} %get-tuple-element.38.stat_ref, ...), custom_call_target="tpu_custom_call" | custom-call | flops 1207959552 | bytes 8388608 | tf_op jit(solution)/shard_map/pallas_call | solution.py:268
  113.1 1.3 collective-permute-start.13
  114.4 2.4 %shard_map.129.f_ref = f32[4,512,384]{2,1,0:T(8,128)S(1)} custom-call(s32[4]{0:T(128)S(1)} %fusion.21.at_ref, bf16[768,384]{1,0:T(8,128)(2,1)S(1)} %get-tuple-element.40.g_ref, bf16[768,4096]{1,0:T(8,128)(2,1)S(1)} %copy-done), custom_call_target="tpu_custom_call" | custom-call | flops 1207959552 | bytes 7340032 | tf_op jit(solution)/shard_map/pallas_call | solution.py:288
  121.9 7.7 %shard_map.131 = (bf16[768,4096]{1,0:T(8,128)(2,1)}, f32[8,128]{1,0:T(8,128)S(1)}) custom-call(s32[8]{0:T(128)S(1)} %pad_add_fusion.2.at_ref, bf16[768,384]{1,0:T(8,128)(2,1)S(1)} %get-tuple-element.40.g_ref, bf16[1536,384]{1,0:T(8,128)(2,1)S(1)} %shard_map.122.refs_0_, bf16[1536,384]{1,0:T(8,128)(2,1)} %get-tuple-element.30.refs_0_.refs_1_, ...), custom_call_target="tpu_custom_call" | custom-call | flops 2415919104 | bytes 10485760 | tf_op jit(solution)/shard_map/pallas_call | solution.py:330
  129.7 1.7 %collective-permute-done.14.c0 = bf16[512,384]{1,0:T(8,128)(2,1)S(1)} collective-permute-done((bf16[512,384]{1,0:T(8,128)(2,1)S(1)}, bf16[512,384]{1,0:T(8,128)(2,1)S(1)}, u32[]{:S(2)}, u32[]{:S(2)}) %collective-permute-start.14) | collective-permute-done | bytes 393248 | tf_op jit(solution)/shard_map/ppermute | solution.py:61
  132.0 1.3 shard_map.132
  133.8 1.7 %collective-permute-start.18 = (bf16[128,384]{1,0:T(8,128)(2,1)S(1)}, bf16[128,384]{1,0:T(8,128)(2,1)S(1)}, u32[]{:S(2)}, u32[]{:S(2)}) collective-permute-start(bf16[128,384]{1,0:T(8,128)(2,1)S(1)} %get-tuple-element.49), channel_id=1, source_target_pairs={{0,8},{1,9},{2,10},{3,11},{4,12},{5,13},{6,14},{7,15},{8,0},{9,1},... | collective-permute-start | bytes 294920 | tf_op jit(solution)/shard_map/ppermute | solution.py:61
  136.3 3.2 %collective-permute-done.17.c0 = bf16[128,384]{1,0:T(8,128)(2,1)S(1)} collective-permute-done((bf16[128,384]{1,0:T(8,128)(2,1)S(1)}, bf16[128,384]{1,0:T(8,128)(2,1)S(1)}, u32[]{:S(2)}, u32[]{:S(2)}) %collective-permute-start.17) | collective-permute-done | bytes 98336 | tf_op jit(solution)/shard_map/ppermute | solution.py:61
  140.9 19.1 %all_to_all.15.b_ref = bf16[128,8,128]{2,1,0:T(8,128)(2,1)S(1)} all-to-all(bf16[128,8,128]{2,1,0:T(8,128)(2,1)S(1)} %shard_map.133), channel_id=1, replica_groups=mesh['dp'=8,'vocab'=16] {'dp','vocab'}, dimensions={0} | all-to-all | bytes 524288 | tf_op jit(solution)/shard_map/all_to_all | solution.py:528
  (67 shorter events, 18.1 us)
Async XLA Ops:
  0.6 13.4 %copy-start.8 = (s32[8]{0:T(128)S(1)}, s32[8]{0:T(128)}, u32[]{:S(2)}) copy-start(s32[8]{0:T(128)} %param.15) | copy-start | bytes 100
  2.5 27.5 %all-to-all-start = ((bf16[128,8,384]{2,1,0:T(8,128)(2,1)}), bf16[128,8,384]{2,1,0:T(8,128)(2,1)S(1)}, u32[]{:S(2)}, u32[]{:S(2)}) async-start(bf16[128,8,384]{2,1,0:T(8,128)(2,1)} %shard_map.121), calls=%async_computation | async-start | bytes 1572864 | tf_op jit(solution)/shard_map/all_to_all | solution.py:468
  14.4 28.6 %copy-start.4 = (s32[384]{0:T(512)}, s32[384]{0:T(512)S(1)}, u32[]{:S(2)}) copy-start(s32[384]{0:T(512)S(1)} %select_reduce_fusion) | copy-start | bytes 4612
  15.0 28.0 %copy-start.7 = (s32[384]{0:T(512)}, s32[384]{0:T(512)S(1)}, u32[]{:S(2)}) copy-start(s32[384]{0:T(512)S(1)} %get-tuple-element.55) | copy-start | bytes 4612
  30.0 13.0 %copy-start.3 = (bf16[128,8,384]{2,1,0:T(8,128)(2,1)}, bf16[128,8,384]{2,1,0:T(8,128)(2,1)S(1)}, u32[]{:S(2)}) copy-start(bf16[128,8,384]{2,1,0:T(8,128)(2,1)S(1)} %all-to-all-done) | copy-start | bytes 2359300
  30.7 7.6 %collective-permute-start.3 = (bf16[384,384]{1,0:T(8,128)(2,1)S(1)}, bf16[384,384]{1,0:T(8,128)(2,1)}, u32[]{:S(2)}, u32[]{:S(2)}) collective-permute-start(bf16[384,384]{1,0:T(8,128)(2,1)S(1)} %fusion.2.refs_0_), channel_id=1, source_target_pairs={{0,64},{1,77},{2,74},{3,71},{4,68},{5,65},{6,78},{7,75},{8,72},{9,... | collective-permute-start | bytes 884744 | tf_op jit(solution)/shard_map/ppermute | solution.py:61
  32.5 9.0 %collective-permute-start.2 = (bf16[384,384]{1,0:T(8,128)(2,1)S(1)}, bf16[384,384]{1,0:T(8,128)(2,1)S(1)}, u32[]{:S(2)}, u32[]{:S(2)}) collective-permute-start(bf16[384,384]{1,0:T(8,128)(2,1)S(1)} %fusion.2.refs_0_), channel_id=1, source_target_pairs={{0,12},{1,13},{2,14},{3,15},{4,0},{5,1},{6,2},{7,3},{8,4},{9,5},{1... | collective-permute-start | bytes 884744 | tf_op jit(solution)/shard_map/ppermute | solution.py:61
  33.3 9.8 %collective-permute-start.1 = (bf16[384,384]{1,0:T(8,128)(2,1)S(1)}, bf16[384,384]{1,0:T(8,128)(2,1)S(1)}, u32[]{:S(2)}, u32[]{:S(2)}) collective-permute-start(bf16[384,384]{1,0:T(8,128)(2,1)S(1)} %fusion.2.refs_0_), channel_id=1, source_target_pairs={{0,8},{1,9},{2,10},{3,11},{4,12},{5,13},{6,14},{7,15},{8,0},{9,1},... | collective-permute-start | bytes 884744 | tf_op jit(solution)/shard_map/ppermute | solution.py:61
  34.3 11.8 %collective-permute-start = (bf16[384,384]{1,0:T(8,128)(2,1)S(1)}, bf16[384,384]{1,0:T(8,128)(2,1)S(1)}, u32[]{:S(2)}, u32[]{:S(2)}) collective-permute-start(bf16[384,384]{1,0:T(8,128)(2,1)S(1)} %fusion.2.refs_0_), channel_id=1, source_target_pairs={{0,4},{1,5},{2,6},{3,7},{4,8},{5,9},{6,10},{7,11},{8,12},{9,13},{1... | collective-permute-start | bytes 884744 | tf_op jit(solution)/shard_map/ppermute | solution.py:61
  46.7 6.7 %collective-permute-start.6 = (bf16[1536,384]{1,0:T(8,128)(2,1)S(1)}, bf16[1536,384]{1,0:T(8,128)(2,1)S(1)}, u32[]{:S(2)}, u32[]{:S(2)}) collective-permute-start(bf16[1536,384]{1,0:T(8,128)(2,1)S(1)} %shard_map.122.refs_0_), channel_id=1, source_target_pairs={{0,16},{1,17},{2,18},{3,19},{4,20},{5,21},{6,22},{7,23},{8,24},{9,... | collective-permute-start | bytes 3538952 | tf_op jit(solution)/shard_map/ppermute | solution.py:61
  46.8 15.5 %collective-permute-start.5 = (bf16[1536,384]{1,0:T(8,128)(2,1)S(1)}, bf16[1536,384]{1,0:T(8,128)(2,1)}, u32[]{:S(2)}, u32[]{:S(2)}) collective-permute-start(bf16[1536,384]{1,0:T(8,128)(2,1)S(1)} %shard_map.122.refs_0_), channel_id=1, source_target_pairs={{0,96},{1,97},{2,98},{3,99},{4,100},{5,101},{6,102},{7,103},{8,104... | collective-permute-start | bytes 3538952 | tf_op jit(solution)/shard_map/ppermute | solution.py:61
  47.0 16.7 %collective-permute-start.4 = (bf16[1536,384]{1,0:T(8,128)(2,1)S(1)}, bf16[1536,384]{1,0:T(8,128)(2,1)}, u32[]{:S(2)}, u32[]{:S(2)}) collective-permute-start(bf16[1536,384]{1,0:T(8,128)(2,1)S(1)} %shard_map.122.refs_0_), channel_id=1, source_target_pairs={{0,32},{1,33},{2,34},{3,35},{4,36},{5,37},{6,38},{7,39},{8,40},{9,... | collective-permute-start | bytes 3538952 | tf_op jit(solution)/shard_map/ppermute | solution.py:61
  48.4 17.5 %collective-permute-start.11 = (bf16[384,384]{1,0:T(8,128)(2,1)}, bf16[384,384]{1,0:T(8,128)(2,1)}, u32[]{:S(2)}, u32[]{:S(2)}) collective-permute-start(bf16[384,384]{1,0:T(8,128)(2,1)} %collective-permute-done.3.refs_4_.refs_0_), channel_id=1, source_target_pairs={{0,3},{1,0},{2,1},{3,2},{4,7},{5,4},{6,5},{7,6},{8,11},{9,8},{10,9... | collective-permute-start | bytes 884744 | tf_op jit(solution)/shard_map/ppermute | solution.py:61
  53.3 12.6 %collective-permute-start.10 = (bf16[384,384]{1,0:T(8,128)(2,1)}, bf16[384,384]{1,0:T(8,128)(2,1)}, u32[]{:S(2)}, u32[]{:S(2)}) collective-permute-start(bf16[384,384]{1,0:T(8,128)(2,1)} %collective-permute-done.3.refs_4_.refs_0_), channel_id=1, source_target_pairs={{0,2},{1,3},{2,0},{3,1},{4,6},{5,7},{6,4},{7,5},{8,10},{9,11},{10,... | collective-permute-start | bytes 884744 | tf_op jit(solution)/shard_map/ppermute | solution.py:61
  53.4 1.0 copy-start.2
  53.4 16.6 %collective-permute-start.9 = (bf16[384,384]{1,0:T(8,128)(2,1)}, bf16[384,384]{1,0:T(8,128)(2,1)}, u32[]{:S(2)}, u32[]{:S(2)}) collective-permute-start(bf16[384,384]{1,0:T(8,128)(2,1)} %collective-permute-done.3.refs_4_.refs_0_), channel_id=1, source_target_pairs={{0,1},{1,2},{2,3},{3,0},{4,5},{5,6},{6,7},{7,4},{8,9},{9,10},{10,1... | collective-permute-start | bytes 884744 | tf_op jit(solution)/shard_map/ppermute | solution.py:61
  63.7 15.4 %collective-permute-start.7 = (bf16[1536,384]{1,0:T(8,128)(2,1)}, bf16[1536,384]{1,0:T(8,128)(2,1)}, u32[]{:S(2)}, u32[]{:S(2)}) collective-permute-start(bf16[1536,384]{1,0:T(8,128)(2,1)} %get-tuple-element.30.refs_0_.refs_1_), channel_id=1, source_target_pairs={{0,16},{1,17},{2,18},{3,19},{4,20},{5,21},{6,22},{7,23},{8,24},{9,... | collective-permute-start | bytes 3538952 | tf_op jit(solution)/shard_map/ppermute | solution.py:61
  65.9 7.2 %copy-start.9 = (s32[2]{0:T(128)S(1)}, s32[2]{0:T(128)}, u32[]{:S(2)}) copy-start(s32[2]{0:T(128)} %constant.221) | copy-start | bytes 28
  65.9 13.2 %collective-permute-start.8 = (bf16[1536,384]{1,0:T(8,128)(2,1)}, bf16[1536,384]{1,0:T(8,128)(2,1)}, u32[]{:S(2)}, u32[]{:S(2)}) collective-permute-start(bf16[1536,384]{1,0:T(8,128)(2,1)} %get-tuple-element.31.refs_1_.refs_3_), channel_id=1, source_target_pairs={{0,16},{1,17},{2,18},{3,19},{4,20},{5,21},{6,22},{7,23},{8,24},{9,... | collective-permute-start | bytes 3538952 | tf_op jit(solution)/shard_map/ppermute | solution.py:61
  72.4 6.7 %collective-permute-start.12 = (bf16[1536,384]{1,0:T(8,128)(2,1)}, bf16[1536,384]{1,0:T(8,128)(2,1)}, u32[]{:S(2)}, u32[]{:S(2)}) collective-permute-start(bf16[1536,384]{1,0:T(8,128)(2,1)} %shard_map.125.refs_2_), channel_id=1, source_target_pairs={{0,16},{1,17},{2,18},{3,19},{4,20},{5,21},{6,22},{7,23},{8,24},{9,... | collective-permute-start | bytes 3538952 | tf_op jit(solution)/shard_map/ppermute | solution.py:61
  88.1 0.8 copy-start.1
  88.9 18.0 %all-to-all-start.1 = ((f32[128,8,128]{2,1,0:T(8,128)}), f32[128,8,128]{2,1,0:T(8,128)}, u32[]{:S(2)}, u32[]{:S(2)}) async-start(f32[128,8,128]{2,1,0:T(8,128)} %copy-done.1), calls=%async_computation.1 | async-start | bytes 1048576 | tf_op jit(solution)/shard_map/all_to_all | solution.py:509
  106.9 2.8 %copy-start = (bf16[768,4096]{1,0:T(8,128)(2,1)S(1)}, bf16[768,4096]{1,0:T(8,128)(2,1)}, u32[]{:S(2)}) copy-start(bf16[768,4096]{1,0:T(8,128)(2,1)} %h_ref.3) | copy-start | bytes 18874372
  113.1 4.4 %collective-permute-start.13 = (bf16[4,512,384]{2,1,0:T(8,128)(2,1)S(1)}, bf16[4,512,384]{2,1,0:T(8,128)(2,1)S(1)}, u32[]{:S(2)}, u32[]{:S(2)}) collective-permute-start(bf16[4,512,384]{2,1,0:T(8,128)(2,1)S(1)} %get-tuple-element.41), channel_id=1, source_target_pairs={{0,16},{1,17},{2,18},{3,19},{4,20},{5,21},{6,22},{7,23},{8,24},{9,... | collective-permute-start | bytes 4718600 | tf_op jit(solution)/shard_map/ppermute | solution.py:61
  118.8 12.6 %collective-permute-start.14 = (bf16[512,384]{1,0:T(8,128)(2,1)S(1)}, bf16[512,384]{1,0:T(8,128)(2,1)S(1)}, u32[]{:S(2)}, u32[]{:S(2)}) collective-permute-start(bf16[512,384]{1,0:T(8,128)(2,1)S(1)} %get-tuple-element.43), channel_id=1, source_target_pairs={{0,32},{1,33},{2,34},{3,35},{4,36},{5,37},{6,38},{7,39},{8,40},{9,... | collective-permute-start | bytes 1179656 | tf_op jit(solution)/shard_map/ppermute | solution.py:61
  119.4 12.0 %collective-permute-start.15 = (bf16[512,384]{1,0:T(8,128)(2,1)S(1)}, bf16[512,384]{1,0:T(8,128)(2,1)S(1)}, u32[]{:S(2)}, u32[]{:S(2)}) collective-permute-start(bf16[512,384]{1,0:T(8,128)(2,1)S(1)} %get-tuple-element.44), channel_id=1, source_target_pairs={{0,64},{1,65},{2,66},{3,67},{4,68},{5,69},{6,70},{7,71},{8,72},{9,... | collective-permute-start | bytes 1179656 | tf_op jit(solution)/shard_map/ppermute | solution.py:61
  120.6 11.5 %collective-permute-start.16 = (bf16[512,384]{1,0:T(8,128)(2,1)S(1)}, bf16[512,384]{1,0:T(8,128)(2,1)S(1)}, u32[]{:S(2)}, u32[]{:S(2)}) collective-permute-start(bf16[512,384]{1,0:T(8,128)(2,1)S(1)} %get-tuple-element.45), channel_id=1, source_target_pairs={{0,96},{1,97},{2,98},{3,99},{4,100},{5,101},{6,102},{7,103},{8,104... | collective-permute-start | bytes 1179656 | tf_op jit(solution)/shard_map/ppermute | solution.py:61
  129.6 6.6 %copy-start.5 = (s32[384]{0:T(512)S(1)}, s32[384]{0:T(512)}, u32[]{:S(2)}) copy-start(s32[384]{0:T(512)} %copy-done.4) | copy-start | bytes 4612
  129.6 6.6 %copy-start.6 = (s32[384]{0:T(512)S(1)}, s32[384]{0:T(512)}, u32[]{:S(2)}) copy-start(s32[384]{0:T(512)} %get-tuple-element.56) | copy-start | bytes 4612
  133.4 6.1 %collective-permute-start.17 = (bf16[128,384]{1,0:T(8,128)(2,1)S(1)}, bf16[128,384]{1,0:T(8,128)(2,1)S(1)}, u32[]{:S(2)}, u32[]{:S(2)}) collective-permute-start(bf16[128,384]{1,0:T(8,128)(2,1)S(1)} %get-tuple-element.48), channel_id=1, source_target_pairs={{0,4},{1,5},{2,6},{3,7},{4,8},{5,9},{6,10},{7,11},{8,12},{9,13},{1... | collective-permute-start | bytes 294920 | tf_op jit(solution)/shard_map/ppermute | solution.py:61
  133.8 5.7 %collective-permute-start.18 = (bf16[128,384]{1,0:T(8,128)(2,1)S(1)}, bf16[128,384]{1,0:T(8,128)(2,1)S(1)}, u32[]{:S(2)}, u32[]{:S(2)}) collective-permute-start(bf16[128,384]{1,0:T(8,128)(2,1)S(1)} %get-tuple-element.49), channel_id=1, source_target_pairs={{0,8},{1,9},{2,10},{3,11},{4,12},{5,13},{6,14},{7,15},{8,0},{9,1},... | collective-permute-start | bytes 294920 | tf_op jit(solution)/shard_map/ppermute | solution.py:61
  135.4 4.6 %collective-permute-start.19 = (bf16[128,384]{1,0:T(8,128)(2,1)S(1)}, bf16[128,384]{1,0:T(8,128)(2,1)S(1)}, u32[]{:S(2)}, u32[]{:S(2)}) collective-permute-start(bf16[128,384]{1,0:T(8,128)(2,1)S(1)} %get-tuple-element.50), channel_id=1, source_target_pairs={{0,12},{1,13},{2,14},{3,15},{4,0},{5,1},{6,2},{7,3},{8,4},{9,5},{1... | collective-permute-start | bytes 294920 | tf_op jit(solution)/shard_map/ppermute | solution.py:61

commit v4 on v3

--- a/solution.py
+++ b/solution.py
@@ -157,18 +157,15 @@
         fetch_t, fetch_s = [], []
         for k in range(n):
             g = at_ref[k]
-            cols_t = pl.ds(pl.multiple_of(1024 * g, 1024), 1024)
+            cols_t = [pl.ds(pl.multiple_of(1024 * g + 512 * j, 512), 512) for j in range(2)]
             cols_s = pl.ds(pl.multiple_of(512 * g, 512), 512)
             x = x_refs[k]
             fetch_t.append(
                 [
-                    pltpu.make_async_copy(x.at[pl.ds(0, 1024), :], x_buf.at[k, pl.ds(0, 1024), :], sem.at[k, 0]),
-                    pltpu.make_async_copy(
-                        ht_ref.at[pl.ds(0, 384), cols_t], ht_buf.at[k, pl.ds(0, 384), :], sem.at[k, 1]
-                    ),
-                    pltpu.make_async_copy(
-                        ht_ref.at[pl.ds(384, 384), cols_t], ht_buf.at[k, pl.ds(384, 384), :], sem.at[k, 2]
-                    ),
+                    pltpu.make_async_copy(x.at[pl.ds(0, 512), :], x_buf.at[k, pl.ds(0, 512), :], sem.at[k, 0]),
+                    pltpu.make_async_copy(ht_ref.at[:, cols_t[0]], ht_buf.at[k, :, pl.ds(0, 512)], sem.at[k, 1]),
+                    pltpu.make_async_copy(x.at[pl.ds(512, 512), :], x_buf.at[k, pl.ds(512, 512), :], sem.at[k, 2]),
+                    pltpu.make_async_copy(ht_ref.at[:, cols_t[1]], ht_buf.at[k, :, pl.ds(512, 512)], sem.at[k, 5]),
                 ]
             )
             fetch_s.append(
@@ -180,15 +177,19 @@
             for c in fetch_t[k] + fetch_s[k]:
                 c.start()
         for k in range(n):
-            for c in fetch_t[k]:
+            for c in fetch_t[k][:2]:
                 c.wait()
-            add_t = jnp.dot(ht_buf[k], x_buf[k, :1024, :], preferred_element_type=F32)
+            if k == 0:
+                add_t = jnp.dot(ht_buf[0, :, :512], x_buf[0, :512, :], preferred_element_type=F32)
+                acc_t[...] = add_t if prior is None else old_t[...] + add_t
+            for c in fetch_t[k][2:]:
+                c.wait()
+            if k == 0:
+                acc_t[...] += jnp.dot(ht_buf[0, :, 512:], x_buf[0, 512:1024, :], preferred_element_type=F32)
+            else:
+                add_t = jnp.dot(ht_buf[k], x_buf[k, :1024, :], preferred_element_type=F32)
             if k > 0:
                 acc_t[...] += add_t
-            elif prior is None:
-                acc_t[...] = add_t
-            else:
-                acc_t[...] = old_t[...] + add_t
             for c in fetch_s[k]:
                 c.wait()
             add_s = jnp.dot(hs_buf[k], x_buf[k, 1024:, :], preferred_element_type=F32)
@@ -218,7 +219,7 @@
                 stat_ref[j : j + 1, :] = lse_t[:, cols]
                 stat_ref[3 + j : 4 + j, :] = lse_s[:, cols]
                 stat_ref[8 + j : 9 + j, :] = mean[:, cols]
-            sent_ref[...] = jnp.broadcast_to(stat_ref[:8, :][None], (128, 8, 128))
+            sent_ref[...] = jnp.broadcast_to(stat_ref[:6, :][None], (128, 6, 128))
 
     args = [groups, teacher_head, student_head, *stacks]
     if prior is not None:
@@ -226,7 +227,7 @@
     out_shape = [jax.ShapeDtypeStruct((VOC, LIVE), F32)] * 2
     if last:
         out_shape.append(jax.ShapeDtypeStruct((16, 128), F32))
-        out_shape.append(jax.ShapeDtypeStruct((128, 8, 128), F32))
+        out_shape.append(jax.ShapeDtypeStruct((128, 6, 128), F32))
     else:
         out_shape.append(jax.ShapeDtypeStruct((8, 128), F32))
     return pl.pallas_call(
@@ -239,7 +240,7 @@
             pltpu.VMEM((n, VOC, 1024), BF16),
             pltpu.VMEM((n, VOC, 512), BF16),
             pltpu.VMEM((n, 1536, LIVE), BF16),
-            pltpu.SemaphoreType.DMA((n, 5)),
+            pltpu.SemaphoreType.DMA((n, 6)),
         ],
         compiler_params=params(50),
         cost_estimate=cost(n * 2 * 1536 * LIVE * VOC, n * 8 << 20),

time: 162 us -> 162 us (level)
  transfers between devices with their start and end apart: 22 -> 22, of which waited for: 14 -> 14; matrix products, arithmetic and copies ran while one was open for 3% -> 4% of each run, Pallas kernels for 15% -> 14%
where the time goes in v4:
time: 162 us; the launch traced here: 161 us
  waiting for transfers between devices  50.3 us (31%)
  Pallas kernels  42.7 us (26%)
  starting transfers between devices  37.8 us (23%)
  blocking collectives  19.1 us (12%)
  local copies, waits for them, and re-layouts  7.01 us (4%)
  matrix products  1.81 us (1%)
    ppermute x20, waiting for transfers between devices, permute(): return lax.ppermute(value, AXES, pairs)  26.6 us
    ppermute x20, starting transfers between devices, permute(): return lax.ppermute(value, AXES, pairs)  21.4 us
    pallas_call x3, Pallas kernels, logits_call(): pl.pallas_call(kernel, in_specs=[SMEM] + [ANY] * (n + 2) + [VMEM] * (len(...  19.7 us
    all_to_all x1, blocking collectives, local(): back = lax.all_to_all(back, AXES, split_axis=0, concat_axis=0, tiled=True)  19.1 us
    all_to_all x1, waiting for transfers between devices, local(): lax.all_to_all(spread_call(teacher_hidden, student_hidden, token_weight),...  15 us
    all_to_all x1, starting transfers between devices, local(): lax.all_to_all(spread_call(teacher_hidden, student_hidden, token_weight),...  11.5 us
    all_to_all x1, waiting for transfers between devices, local(): lax.all_to_all(sent, AXES, split_axis=0, concat_axis=0, tiled=True)  8.67 us
    pallas_call x1, Pallas kernels, head_grad_call(): pl.pallas_call(kernel, in_specs=[SMEM, VMEM] + [ANY] * n, out_specs=[ANY,...  7.68 us
  transfers between devices with their start and end apart: 22, of which 14 were waited for; matrix products, arithmetic and copies ran while one was open for 4% of the time, Pallas kernels for 14%

profile of v4, /device:TPU:1, one launch (start us, length us, event | category | flops | bytes accessed | tf_op | source)
XLA Modules:
  0.0 161.1 jit_solution(12464121359525716315)
XLA Ops:
  0.6 1.9 %shard_map.121 = bf16[128,8,384]{2,1,0:T(8,128)(2,1)} custom-call(bf16[7,8192]{1,0:T(8,128)(2,1)} %t_ref.1, bf16[7,4096]{1,0:T(8,128)(2,1)} %s_ref.1, s32[1,7]{1,0:T(1,128)} %bitcast.14), custom_call_target="tpu_custom_call" | custom-call | bytes 1048576 | tf_op jit(solution)/shard_map/pallas_call | solution.py:99
  2.5 11.5 %all-to-all-start = ((bf16[128,8,384]{2,1,0:T(8,128)(2,1)}), bf16[128,8,384]{2,1,0:T(8,128)(2,1)S(1)}, u32[]{:S(2)}, u32[]{:S(2)}) async-start(bf16[128,8,384]{2,1,0:T(8,128)(2,1)} %shard_map.121), calls=%async_computation | async-start | bytes 1572864 | tf_op jit(solution)/shard_map/all_to_all | solution.py:469
  15.0 15.0 %all-to-all-done = bf16[128,8,384]{2,1,0:T(8,128)(2,1)S(1)} async-done(((bf16[128,8,384]{2,1,0:T(8,128)(2,1)}), bf16[128,8,384]{2,1,0:T(8,128)(2,1)S(1)}, u32[]{:S(2)}, u32[]{:S(2)}) %all-to-all-start) | async-done | bytes 786464 | tf_op jit(solution)/shard_map/all_to_all | solution.py:469
  30.7 1.8 %collective-permute-start.3 = (bf16[384,384]{1,0:T(8,128)(2,1)S(1)}, bf16[384,384]{1,0:T(8,128)(2,1)}, u32[]{:S(2)}, u32[]{:S(2)}) collective-permute-start(bf16[384,384]{1,0:T(8,128)(2,1)S(1)} %fusion.2.refs_0_), channel_id=1, source_target_pairs={{0,64},{1,77},{2,74},{3,71},{4,68},{5,65},{6,78},{7,75},{8,72},{9,... | collective-permute-start | bytes 884744 | tf_op jit(solution)/shard_map/ppermute | solution.py:61
  34.4 3.9 %collective-permute-done.3.refs_4_.refs_0_ = bf16[384,384]{1,0:T(8,128)(2,1)} collective-permute-done((bf16[384,384]{1,0:T(8,128)(2,1)S(1)}, bf16[384,384]{1,0:T(8,128)(2,1)}, u32[]{:S(2)}, u32[]{:S(2)}) %collective-permute-start.3) | collective-permute-done | bytes 294944 | tf_op jit(solution)/shard_map/ppermute | solution.py:61
  38.3 3.3 %collective-permute-done.2.refs_3_ = bf16[384,384]{1,0:T(8,128)(2,1)S(1)} collective-permute-done((bf16[384,384]{1,0:T(8,128)(2,1)S(1)}, bf16[384,384]{1,0:T(8,128)(2,1)S(1)}, u32[]{:S(2)}, u32[]{:S(2)}) %collective-permute-start.2) | collective-permute-done | bytes 294944 | tf_op jit(solution)/shard_map/ppermute | solution.py:61
  41.6 1.5 collective-permute-done.1.refs_2_
  43.0 3.0 %collective-permute-done.refs_1_ = bf16[384,384]{1,0:T(8,128)(2,1)S(1)} collective-permute-done((bf16[384,384]{1,0:T(8,128)(2,1)S(1)}, bf16[384,384]{1,0:T(8,128)(2,1)S(1)}, u32[]{:S(2)}, u32[]{:S(2)}) %collective-permute-start) | collective-permute-done | bytes 294944 | tf_op jit(solution)/shard_map/ppermute | solution.py:61
  47.0 1.3 collective-permute-start.4
  48.4 4.9 %collective-permute-start.11 = (bf16[384,384]{1,0:T(8,128)(2,1)}, bf16[384,384]{1,0:T(8,128)(2,1)}, u32[]{:S(2)}, u32[]{:S(2)}) collective-permute-start(bf16[384,384]{1,0:T(8,128)(2,1)} %collective-permute-done.3.refs_4_.refs_0_), channel_id=1, source_target_pairs={{0,3},{1,0},{2,1},{3,2},{4,7},{5,4},{6,5},{7,6},{8,11},{9,8},{10,9... | collective-permute-start | bytes 884744 | tf_op jit(solution)/shard_map/ppermute | solution.py:61
  54.5 5.1 %shard_map.123 = (f32[768,384]{1,0:T(8,128)S(1)}, f32[768,384]{1,0:T(8,128)S(1)}, f32[8,128]{1,0:T(8,128)S(1)}) custom-call(s32[2]{0:T(128)S(1)} %pad_add_fusion.1.at_ref, bf16[768,8192]{1,0:T(8,128)(2,1)} %ht_ref.5, bf16[768,4096]{1,0:T(8,128)(2,1)} %h_ref.3, bf16[1536,384]{1,0:T(8,128)(2,1)S(1)} %shard_map.122.refs_0_, bf16[1536,384]{1,0:T(8,128)(2,1)} %copy-done.2), custom_call_target="tpu_custom_call" | custom-call | flops 1811939328 | bytes 16777216 | tf_op jit(solution)/shard_map/pallas_call | solution.py:233
  59.7 2.7 %collective-permute-done.5.refs_1_ = bf16[1536,384]{1,0:T(8,128)(2,1)} collective-permute-done((bf16[1536,384]{1,0:T(8,128)(2,1)S(1)}, bf16[1536,384]{1,0:T(8,128)(2,1)}, u32[]{:S(2)}, u32[]{:S(2)}) %collective-permute-start.5) | collective-permute-done | bytes 1179680 | tf_op jit(solution)/shard_map/ppermute | solution.py:61
  62.3 1.3 collective-permute-done.4.refs_0_
  63.7 2.2 %collective-permute-start.7 = (bf16[1536,384]{1,0:T(8,128)(2,1)}, bf16[1536,384]{1,0:T(8,128)(2,1)}, u32[]{:S(2)}, u32[]{:S(2)}) collective-permute-start(bf16[1536,384]{1,0:T(8,128)(2,1)} %get-tuple-element.30.refs_0_.refs_1_), channel_id=1, source_target_pairs={{0,16},{1,17},{2,18},{3,19},{4,20},{5,21},{6,22},{7,23},{8,24},{9,... | collective-permute-start | bytes 3538952 | tf_op jit(solution)/shard_map/ppermute | solution.py:61
  65.9 4.1 %collective-permute-done.9.refs_1_ = bf16[384,384]{1,0:T(8,128)(2,1)} collective-permute-done((bf16[384,384]{1,0:T(8,128)(2,1)}, bf16[384,384]{1,0:T(8,128)(2,1)}, u32[]{:S(2)}, u32[]{:S(2)}) %collective-permute-start.9) | collective-permute-done | bytes 294944 | tf_op jit(solution)/shard_map/ppermute | solution.py:61
  70.0 2.4 %shard_map.125.refs_2_ = bf16[1536,384]{1,0:T(8,128)(2,1)} custom-call(s32[4]{0:T(128)S(1)} %and_select_fusion.6.at_ref, bf16[384,384]{1,0:T(8,128)(2,1)} %collective-permute-done.3.refs_4_.refs_0_, bf16[384,384]{1,0:T(8,128)(2,1)} %collective-permute-done.9.refs_1_, bf16[384,384]{1,0:T(8,128)(2,1)} %collective-permute-done.10.refs_2_, ...), custom_call_target="tpu_custom_call" | custom-call | bytes 2097152 | tf_op jit(solution)/shard_map/pallas_call | solution.py:121
  73.1 5.8 %shard_map.126 = (f32[768,384]{1,0:T(8,128)S(1)}, f32[768,384]{1,0:T(8,128)S(1)}, f32[8,128]{1,0:T(8,128)}) custom-call(s32[2]{0:T(128)S(1)} %get-tuple-element.57.at_ref, bf16[768,8192]{1,0:T(8,128)(2,1)} %ht_ref.5, bf16[768,4096]{1,0:T(8,128)(2,1)} %h_ref.3, ...), custom_call_target="tpu_custom_call", output_to_operand_aliasing={{0}: (5, {}), {1}: (6, {})} | custom-call | flops 1811939328 | bytes 16777216 | tf_op jit(solution)/shard_map/pallas_call | solution.py:233
  78.9 8.9 %shard_map.127 = (f32[768,384]{1,0:T(8,128)S(1)}, f32[768,384]{1,0:T(8,128)S(1)}, f32[16,128]{1,0:T(8,128)S(1)}, f32[128,6,128]{2,1,0:T(8,128)S(1)}) custom-call(s32[4]{0:T(128)S(1)} %pad_add_fusion.at_ref, bf16[768,8192]{1,0:T(8,128)(2,1)} %ht_ref.5, bf16[768,4096]{1,0:T(8,128)(2,1)} %h_ref.3, ...), custom_call_target="tpu_custom_call", output_to_operand_aliasing={{0}: (7, {}), {1}: (8, {})} | custom-call | flops 3623878656 | bytes 33554432 | tf_op jit(solution)/shard_map/pallas_call | solution.py:233
  88.6 4.9 %all-to-all-start.1 = ((f32[128,6,128]{2,1,0:T(8,128)}), f32[128,6,128]{2,1,0:T(8,128)}, u32[]{:S(2)}, u32[]{:S(2)}) async-start(f32[128,6,128]{2,1,0:T(8,128)} %copy-done.1), calls=%async_computation.1 | async-start | bytes 1048576 | tf_op jit(solution)/shard_map/all_to_all | solution.py:510
  93.6 1.8 %slice_reduce_fusion = bf16[128,8]{1,0:T(8,128)(2,1)} fusion(bf16[128,8,384]{2,1,0:T(8,128)(2,1)} %copy-done.3), kind=kLoop, calls=%fused_computation.7 | loop fusion | bytes 4096 | tf_op jit(solution)/shard_map/slice | solution.py:484
  95.4 1.4 reshape.237
  97.9 8.7 %all-to-all-done.1.all_ref = f32[128,6,128]{2,1,0:T(8,128)} async-done(((f32[128,6,128]{2,1,0:T(8,128)}), f32[128,6,128]{2,1,0:T(8,128)}, u32[]{:S(2)}, u32[]{:S(2)}) %all-to-all-start.1) | async-done | bytes 393248 | tf_op jit(solution)/shard_map/all_to_all | solution.py:510
  106.6 2.8 %copy-done = bf16[768,4096]{1,0:T(8,128)(2,1)S(1)} copy-done((bf16[768,4096]{1,0:T(8,128)(2,1)S(1)}, bf16[768,4096]{1,0:T(8,128)(2,1)}, u32[]{:S(2)}) %copy-start) | copy-done | bytes 6291480
  109.4 3.2 %shard_map.128 = (bf16[4,512,384]{2,1,0:T(8,128)(2,1)S(1)}, bf16[768,384]{1,0:T(8,128)(2,1)S(1)}, f32[8,128]{1,0:T(8,128)S(1)}) custom-call(s32[4]{0:T(128)S(1)} %broadcast_add_fusion.1.at_ref, f32[768,384]{1,0:T(8,128)S(1)} %get-tuple-element.36.t_ref, f32[768,384]{1,0:T(8,128)S(1)} %get-tuple-element.37.s_ref, f32[16,128]{1,0:T(8,128)S(1)} %get-tuple-element.38.stat_ref, ...), custom_call_target="tpu_custom_call" | custom-call | flops 1207959552 | bytes 8388608 | tf_op jit(solution)/shard_map/pallas_call | solution.py:269
  112.6 1.6 collective-permute-start.13
  114.2 2.4 %shard_map.129.f_ref = f32[4,512,384]{2,1,0:T(8,128)S(1)} custom-call(s32[4]{0:T(128)S(1)} %fusion.21.at_ref, bf16[768,384]{1,0:T(8,128)(2,1)S(1)} %get-tuple-element.40.g_ref, bf16[768,4096]{1,0:T(8,128)(2,1)S(1)} %copy-done), custom_call_target="tpu_custom_call" | custom-call | flops 1207959552 | bytes 7340032 | tf_op jit(solution)/shard_map/pallas_call | solution.py:289
  121.5 7.7 %shard_map.131 = (bf16[768,4096]{1,0:T(8,128)(2,1)}, f32[8,128]{1,0:T(8,128)S(1)}) custom-call(s32[8]{0:T(128)S(1)} %pad_add_fusion.2.at_ref, bf16[768,384]{1,0:T(8,128)(2,1)S(1)} %get-tuple-element.40.g_ref, bf16[1536,384]{1,0:T(8,128)(2,1)S(1)} %shard_map.122.refs_0_, bf16[1536,384]{1,0:T(8,128)(2,1)} %get-tuple-element.30.refs_0_.refs_1_, ...), custom_call_target="tpu_custom_call" | custom-call | flops 2415919104 | bytes 10485760 | tf_op jit(solution)/shard_map/pallas_call | solution.py:331
  129.2 1.8 %collective-permute-done.14.c0 = bf16[512,384]{1,0:T(8,128)(2,1)S(1)} collective-permute-done((bf16[512,384]{1,0:T(8,128)(2,1)S(1)}, bf16[512,384]{1,0:T(8,128)(2,1)S(1)}, u32[]{:S(2)}, u32[]{:S(2)}) %collective-permute-start.14) | collective-permute-done | bytes 393248 | tf_op jit(solution)/shard_map/ppermute | solution.py:61
  131.6 1.3 shard_map.132
  133.3 1.7 %collective-permute-start.18 = (bf16[128,384]{1,0:T(8,128)(2,1)S(1)}, bf16[128,384]{1,0:T(8,128)(2,1)S(1)}, u32[]{:S(2)}, u32[]{:S(2)}) collective-permute-start(bf16[128,384]{1,0:T(8,128)(2,1)S(1)} %get-tuple-element.49), channel_id=1, source_target_pairs={{0,8},{1,9},{2,10},{3,11},{4,12},{5,13},{6,14},{7,15},{8,0},{9,1},... | collective-permute-start | bytes 294920 | tf_op jit(solution)/shard_map/ppermute | solution.py:61
  135.9 3.2 %collective-permute-done.17.c0 = bf16[128,384]{1,0:T(8,128)(2,1)S(1)} collective-permute-done((bf16[128,384]{1,0:T(8,128)(2,1)S(1)}, bf16[128,384]{1,0:T(8,128)(2,1)S(1)}, u32[]{:S(2)}, u32[]{:S(2)}) %collective-permute-start.17) | collective-permute-done | bytes 98336 | tf_op jit(solution)/shard_map/ppermute | solution.py:61
  140.5 19.1 %all_to_all.15.b_ref = bf16[128,8,128]{2,1,0:T(8,128)(2,1)S(1)} all-to-all(bf16[128,8,128]{2,1,0:T(8,128)(2,1)S(1)} %shard_map.133), channel_id=1, replica_groups=mesh['dp'=8,'vocab'=16] {'dp','vocab'}, dimensions={0} | all-to-all | bytes 524288 | tf_op jit(solution)/shard_map/all_to_all | solution.py:529
  (67 shorter events, 17.9 us)
Async XLA Ops:
  0.6 13.4 %copy-start.8 = (s32[8]{0:T(128)S(1)}, s32[8]{0:T(128)}, u32[]{:S(2)}) copy-start(s32[8]{0:T(128)} %param.15) | copy-start | bytes 100
  2.5 27.5 %all-to-all-start = ((bf16[128,8,384]{2,1,0:T(8,128)(2,1)}), bf16[128,8,384]{2,1,0:T(8,128)(2,1)S(1)}, u32[]{:S(2)}, u32[]{:S(2)}) async-start(bf16[128,8,384]{2,1,0:T(8,128)(2,1)} %shard_map.121), calls=%async_computation | async-start | bytes 1572864 | tf_op jit(solution)/shard_map/all_to_all | solution.py:469
  14.4 28.6 %copy-start.4 = (s32[384]{0:T(512)}, s32[384]{0:T(512)S(1)}, u32[]{:S(2)}) copy-start(s32[384]{0:T(512)S(1)} %select_reduce_fusion) | copy-start | bytes 4612
  15.0 28.0 %copy-start.7 = (s32[384]{0:T(512)}, s32[384]{0:T(512)S(1)}, u32[]{:S(2)}) copy-start(s32[384]{0:T(512)S(1)} %get-tuple-element.55) | copy-start | bytes 4612
  30.0 13.0 %copy-start.3 = (bf16[128,8,384]{2,1,0:T(8,128)(2,1)}, bf16[128,8,384]{2,1,0:T(8,128)(2,1)S(1)}, u32[]{:S(2)}) copy-start(bf16[128,8,384]{2,1,0:T(8,128)(2,1)S(1)} %all-to-all-done) | copy-start | bytes 2359300
  30.7 7.6 %collective-permute-start.3 = (bf16[384,384]{1,0:T(8,128)(2,1)S(1)}, bf16[384,384]{1,0:T(8,128)(2,1)}, u32[]{:S(2)}, u32[]{:S(2)}) collective-permute-start(bf16[384,384]{1,0:T(8,128)(2,1)S(1)} %fusion.2.refs_0_), channel_id=1, source_target_pairs={{0,64},{1,77},{2,74},{3,71},{4,68},{5,65},{6,78},{7,75},{8,72},{9,... | collective-permute-start | bytes 884744 | tf_op jit(solution)/shard_map/ppermute | solution.py:61
  32.5 9.0 %collective-permute-start.2 = (bf16[384,384]{1,0:T(8,128)(2,1)S(1)}, bf16[384,384]{1,0:T(8,128)(2,1)S(1)}, u32[]{:S(2)}, u32[]{:S(2)}) collective-permute-start(bf16[384,384]{1,0:T(8,128)(2,1)S(1)} %fusion.2.refs_0_), channel_id=1, source_target_pairs={{0,12},{1,13},{2,14},{3,15},{4,0},{5,1},{6,2},{7,3},{8,4},{9,5},{1... | collective-permute-start | bytes 884744 | tf_op jit(solution)/shard_map/ppermute | solution.py:61
  33.3 9.8 %collective-permute-start.1 = (bf16[384,384]{1,0:T(8,128)(2,1)S(1)}, bf16[384,384]{1,0:T(8,128)(2,1)S(1)}, u32[]{:S(2)}, u32[]{:S(2)}) collective-permute-start(bf16[384,384]{1,0:T(8,128)(2,1)S(1)} %fusion.2.refs_0_), channel_id=1, source_target_pairs={{0,8},{1,9},{2,10},{3,11},{4,12},{5,13},{6,14},{7,15},{8,0},{9,1},... | collective-permute-start | bytes 884744 | tf_op jit(solution)/shard_map/ppermute | solution.py:61
  34.3 11.8 %collective-permute-start = (bf16[384,384]{1,0:T(8,128)(2,1)S(1)}, bf16[384,384]{1,0:T(8,128)(2,1)S(1)}, u32[]{:S(2)}, u32[]{:S(2)}) collective-permute-start(bf16[384,384]{1,0:T(8,128)(2,1)S(1)} %fusion.2.refs_0_), channel_id=1, source_target_pairs={{0,4},{1,5},{2,6},{3,7},{4,8},{5,9},{6,10},{7,11},{8,12},{9,13},{1... | collective-permute-start | bytes 884744 | tf_op jit(solution)/shard_map/ppermute | solution.py:61
  46.7 6.7 %collective-permute-start.6 = (bf16[1536,384]{1,0:T(8,128)(2,1)S(1)}, bf16[1536,384]{1,0:T(8,128)(2,1)S(1)}, u32[]{:S(2)}, u32[]{:S(2)}) collective-permute-start(bf16[1536,384]{1,0:T(8,128)(2,1)S(1)} %shard_map.122.refs_0_), channel_id=1, source_target_pairs={{0,16},{1,17},{2,18},{3,19},{4,20},{5,21},{6,22},{7,23},{8,24},{9,... | collective-permute-start | bytes 3538952 | tf_op jit(solution)/shard_map/ppermute | solution.py:61
  46.8 15.5 %collective-permute-start.5 = (bf16[1536,384]{1,0:T(8,128)(2,1)S(1)}, bf16[1536,384]{1,0:T(8,128)(2,1)}, u32[]{:S(2)}, u32[]{:S(2)}) collective-permute-start(bf16[1536,384]{1,0:T(8,128)(2,1)S(1)} %shard_map.122.refs_0_), channel_id=1, source_target_pairs={{0,96},{1,97},{2,98},{3,99},{4,100},{5,101},{6,102},{7,103},{8,104... | collective-permute-start | bytes 3538952 | tf_op jit(solution)/shard_map/ppermute | solution.py:61
  47.0 16.7 %collective-permute-start.4 = (bf16[1536,384]{1,0:T(8,128)(2,1)S(1)}, bf16[1536,384]{1,0:T(8,128)(2,1)}, u32[]{:S(2)}, u32[]{:S(2)}) collective-permute-start(bf16[1536,384]{1,0:T(8,128)(2,1)S(1)} %shard_map.122.refs_0_), channel_id=1, source_target_pairs={{0,32},{1,33},{2,34},{3,35},{4,36},{5,37},{6,38},{7,39},{8,40},{9,... | collective-permute-start | bytes 3538952 | tf_op jit(solution)/shard_map/ppermute | solution.py:61
  48.4 17.5 %collective-permute-start.11 = (bf16[384,384]{1,0:T(8,128)(2,1)}, bf16[384,384]{1,0:T(8,128)(2,1)}, u32[]{:S(2)}, u32[]{:S(2)}) collective-permute-start(bf16[384,384]{1,0:T(8,128)(2,1)} %collective-permute-done.3.refs_4_.refs_0_), channel_id=1, source_target_pairs={{0,3},{1,0},{2,1},{3,2},{4,7},{5,4},{6,5},{7,6},{8,11},{9,8},{10,9... | collective-permute-start | bytes 884744 | tf_op jit(solution)/shard_map/ppermute | solution.py:61
  53.3 12.6 %collective-permute-start.10 = (bf16[384,384]{1,0:T(8,128)(2,1)}, bf16[384,384]{1,0:T(8,128)(2,1)}, u32[]{:S(2)}, u32[]{:S(2)}) collective-permute-start(bf16[384,384]{1,0:T(8,128)(2,1)} %collective-permute-done.3.refs_4_.refs_0_), channel_id=1, source_target_pairs={{0,2},{1,3},{2,0},{3,1},{4,6},{5,7},{6,4},{7,5},{8,10},{9,11},{10,... | collective-permute-start | bytes 884744 | tf_op jit(solution)/shard_map/ppermute | solution.py:61
  53.4 1.0 copy-start.2
  53.4 16.6 %collective-permute-start.9 = (bf16[384,384]{1,0:T(8,128)(2,1)}, bf16[384,384]{1,0:T(8,128)(2,1)}, u32[]{:S(2)}, u32[]{:S(2)}) collective-permute-start(bf16[384,384]{1,0:T(8,128)(2,1)} %collective-permute-done.3.refs_4_.refs_0_), channel_id=1, source_target_pairs={{0,1},{1,2},{2,3},{3,0},{4,5},{5,6},{6,7},{7,4},{8,9},{9,10},{10,1... | collective-permute-start | bytes 884744 | tf_op jit(solution)/shard_map/ppermute | solution.py:61
  63.7 15.2 %collective-permute-start.7 = (bf16[1536,384]{1,0:T(8,128)(2,1)}, bf16[1536,384]{1,0:T(8,128)(2,1)}, u32[]{:S(2)}, u32[]{:S(2)}) collective-permute-start(bf16[1536,384]{1,0:T(8,128)(2,1)} %get-tuple-element.30.refs_0_.refs_1_), channel_id=1, source_target_pairs={{0,16},{1,17},{2,18},{3,19},{4,20},{5,21},{6,22},{7,23},{8,24},{9,... | collective-permute-start | bytes 3538952 | tf_op jit(solution)/shard_map/ppermute | solution.py:61
  65.9 7.2 %copy-start.9 = (s32[2]{0:T(128)S(1)}, s32[2]{0:T(128)}, u32[]{:S(2)}) copy-start(s32[2]{0:T(128)} %constant.221) | copy-start | bytes 28
  65.9 13.0 %collective-permute-start.8 = (bf16[1536,384]{1,0:T(8,128)(2,1)}, bf16[1536,384]{1,0:T(8,128)(2,1)}, u32[]{:S(2)}, u32[]{:S(2)}) collective-permute-start(bf16[1536,384]{1,0:T(8,128)(2,1)} %get-tuple-element.31.refs_1_.refs_3_), channel_id=1, source_target_pairs={{0,16},{1,17},{2,18},{3,19},{4,20},{5,21},{6,22},{7,23},{8,24},{9,... | collective-permute-start | bytes 3538952 | tf_op jit(solution)/shard_map/ppermute | solution.py:61
  72.4 6.6 %collective-permute-start.12 = (bf16[1536,384]{1,0:T(8,128)(2,1)}, bf16[1536,384]{1,0:T(8,128)(2,1)}, u32[]{:S(2)}, u32[]{:S(2)}) collective-permute-start(bf16[1536,384]{1,0:T(8,128)(2,1)} %shard_map.125.refs_2_), channel_id=1, source_target_pairs={{0,16},{1,17},{2,18},{3,19},{4,20},{5,21},{6,22},{7,23},{8,24},{9,... | collective-permute-start | bytes 3538952 | tf_op jit(solution)/shard_map/ppermute | solution.py:61
  87.8 0.8 copy-start.1
  88.6 18.0 %all-to-all-start.1 = ((f32[128,6,128]{2,1,0:T(8,128)}), f32[128,6,128]{2,1,0:T(8,128)}, u32[]{:S(2)}, u32[]{:S(2)}) async-start(f32[128,6,128]{2,1,0:T(8,128)} %copy-done.1), calls=%async_computation.1 | async-start | bytes 1048576 | tf_op jit(solution)/shard_map/all_to_all | solution.py:510
  106.6 2.8 %copy-start = (bf16[768,4096]{1,0:T(8,128)(2,1)S(1)}, bf16[768,4096]{1,0:T(8,128)(2,1)}, u32[]{:S(2)}) copy-start(bf16[768,4096]{1,0:T(8,128)(2,1)} %h_ref.3) | copy-start | bytes 18874372
  112.6 4.6 %collective-permute-start.13 = (bf16[4,512,384]{2,1,0:T(8,128)(2,1)S(1)}, bf16[4,512,384]{2,1,0:T(8,128)(2,1)S(1)}, u32[]{:S(2)}, u32[]{:S(2)}) collective-permute-start(bf16[4,512,384]{2,1,0:T(8,128)(2,1)S(1)} %get-tuple-element.41), channel_id=1, source_target_pairs={{0,16},{1,17},{2,18},{3,19},{4,20},{5,21},{6,22},{7,23},{8,24},{9,... | collective-permute-start | bytes 4718600 | tf_op jit(solution)/shard_map/ppermute | solution.py:61
  118.6 12.4 %collective-permute-start.14 = (bf16[512,384]{1,0:T(8,128)(2,1)S(1)}, bf16[512,384]{1,0:T(8,128)(2,1)S(1)}, u32[]{:S(2)}, u32[]{:S(2)}) collective-permute-start(bf16[512,384]{1,0:T(8,128)(2,1)S(1)} %get-tuple-element.43), channel_id=1, source_target_pairs={{0,32},{1,33},{2,34},{3,35},{4,36},{5,37},{6,38},{7,39},{8,40},{9,... | collective-permute-start | bytes 1179656 | tf_op jit(solution)/shard_map/ppermute | solution.py:61
  118.9 12.0 %collective-permute-start.15 = (bf16[512,384]{1,0:T(8,128)(2,1)S(1)}, bf16[512,384]{1,0:T(8,128)(2,1)S(1)}, u32[]{:S(2)}, u32[]{:S(2)}) collective-permute-start(bf16[512,384]{1,0:T(8,128)(2,1)S(1)} %get-tuple-element.44), channel_id=1, source_target_pairs={{0,64},{1,65},{2,66},{3,67},{4,68},{5,69},{6,70},{7,71},{8,72},{9,... | collective-permute-start | bytes 1179656 | tf_op jit(solution)/shard_map/ppermute | solution.py:61
  120.1 11.5 %collective-permute-start.16 = (bf16[512,384]{1,0:T(8,128)(2,1)S(1)}, bf16[512,384]{1,0:T(8,128)(2,1)S(1)}, u32[]{:S(2)}, u32[]{:S(2)}) collective-permute-start(bf16[512,384]{1,0:T(8,128)(2,1)S(1)} %get-tuple-element.45), channel_id=1, source_target_pairs={{0,96},{1,97},{2,98},{3,99},{4,100},{5,101},{6,102},{7,103},{8,104... | collective-permute-start | bytes 1179656 | tf_op jit(solution)/shard_map/ppermute | solution.py:61
  129.2 6.6 %copy-start.5 = (s32[384]{0:T(512)S(1)}, s32[384]{0:T(512)}, u32[]{:S(2)}) copy-start(s32[384]{0:T(512)} %copy-done.4) | copy-start | bytes 4612
  129.2 6.6 %copy-start.6 = (s32[384]{0:T(512)S(1)}, s32[384]{0:T(512)}, u32[]{:S(2)}) copy-start(s32[384]{0:T(512)} %get-tuple-element.56) | copy-start | bytes 4612
  132.9 6.1 %collective-permute-start.17 = (bf16[128,384]{1,0:T(8,128)(2,1)S(1)}, bf16[128,384]{1,0:T(8,128)(2,1)S(1)}, u32[]{:S(2)}, u32[]{:S(2)}) collective-permute-start(bf16[128,384]{1,0:T(8,128)(2,1)S(1)} %get-tuple-element.48), channel_id=1, source_target_pairs={{0,4},{1,5},{2,6},{3,7},{4,8},{5,9},{6,10},{7,11},{8,12},{9,13},{1... | collective-permute-start | bytes 294920 | tf_op jit(solution)/shard_map/ppermute | solution.py:61
  133.3 5.7 %collective-permute-start.18 = (bf16[128,384]{1,0:T(8,128)(2,1)S(1)}, bf16[128,384]{1,0:T(8,128)(2,1)S(1)}, u32[]{:S(2)}, u32[]{:S(2)}) collective-permute-start(bf16[128,384]{1,0:T(8,128)(2,1)S(1)} %get-tuple-element.49), channel_id=1, source_target_pairs={{0,8},{1,9},{2,10},{3,11},{4,12},{5,13},{6,14},{7,15},{8,0},{9,1},... | collective-permute-start | bytes 294920 | tf_op jit(solution)/shard_map/ppermute | solution.py:61
  135.0 4.6 %collective-permute-start.19 = (bf16[128,384]{1,0:T(8,128)(2,1)S(1)}, bf16[128,384]{1,0:T(8,128)(2,1)S(1)}, u32[]{:S(2)}, u32[]{:S(2)}) collective-permute-start(bf16[128,384]{1,0:T(8,128)(2,1)S(1)} %get-tuple-element.50), channel_id=1, source_target_pairs={{0,12},{1,13},{2,14},{3,15},{4,0},{5,1},{6,2},{7,3},{8,4},{9,5},{1... | collective-permute-start | bytes 294920 | tf_op jit(solution)/shard_map/ppermute | solution.py:61
